TPU v7x, 32 devices: a whole 2x2x4 slice. The times are simulated.
32 devices in a mesh: aa: 8 (over y, x, core), ba: 4 (over z).
Axes of the slice: x: 2, y: 2, z: 4, core: 2. Of those that a mesh axis runs over, the one named last changes fastest.
Arguments:
- amplitudes: bfloat16 [512, 512], P('aa', 'ba'), may hold values from -6 to 6
- code: int32 [32, 512], replicated, may hold values from -512 to 512, as said below
- counts: int32 [32], replicated, may hold values from 1 to 16, as said below
- pair_irrep: int32 [32], replicated, may hold values from 0 to 7
- integrals: bfloat16 [32, 32], replicated, may hold values from -3 to 3
- one_body: bfloat16 [32], replicated, may hold values from -1.5 to 1.5
Outputs:
- sigma: bfloat16 [512, 512], P('aa', 'ba')
Inputs may be any that keep to these rules, and one draw needn't show every extreme that they name: |code| - 1 names the target string of a replacement and the sign of code its sign; some entries reach both ends. `counts`: the live strings of fine block j fill its first slots, from slot j * 16 on; in every draw some block is full and some holds one string.
All inputs are finite; a program needn't handle non-finite values.
Results may differ from a plain program's by a relative error of at most 0.0045.
Values may be sent and summed in bfloat16 or wider, within the bound.
No kernel may reach another device: no remote copies, remote signals or barrier semaphores. Data moves between devices by JAX's collectives and lax.ppermute only.
A program may use at most 128 MiB of HBM per device.

v0:
```python
import jax
import jax.numpy as jnp
from jax import lax
from jax.sharding import PartitionSpec as P


def one_hot(tables, signs, first, width):
    ids = first + jnp.arange(width, dtype=jnp.int32)
    return jnp.where(
        tables[:, :, None] == ids[None, None, :], signs[:, :, None], jnp.zeros((), jnp.bfloat16)
    )


def alpha_term(tables, signs, values, start_a, rows_a, rows_b, count):
    groups = tables.shape[0] // 8
    rows_t = tables.reshape(groups, 8, count)
    rows_s = signs.reshape(groups, 8, count)

    def one_group(carry, items):
        tab, sgn, val = items
        hot = one_hot(tab, sgn, start_a, rows_a)
        return (
            carry + jnp.einsum("prk,pkb->rb", hot, val, preferred_element_type=jnp.float32),
            None,
        )

    total, _ = lax.scan(
        one_group,
        jnp.zeros((count, rows_b), jnp.float32),
        (rows_t, rows_s, values.reshape(groups, 8, rows_a, rows_b)),
    )
    return total


def per_device(amplitudes, code, counts, pair_irrep, integrals, one_body):
    rows_a, rows_b = amplitudes.shape
    pairs, strings = code.shape
    groups = pairs // 8
    capacity = strings // counts.shape[0]
    slots = jnp.arange(strings, dtype=jnp.int32)
    live_all = (slots % capacity < jnp.repeat(counts, capacity)).astype(jnp.bfloat16)
    start_a = lax.axis_index("aa") * rows_a
    start_b = lax.axis_index("ba") * rows_b
    live_a = lax.dynamic_slice_in_dim(live_all, start_a, rows_a)
    live_b = lax.dynamic_slice_in_dim(live_all, start_b, rows_b)
    masked = amplitudes * (live_a[:, None] * live_b[None, :])
    target = jnp.abs(code) - 1
    signs = jnp.sign(code).astype(jnp.bfloat16)
    target_a = lax.dynamic_slice_in_dim(target, start_a, rows_a, 1).reshape(groups, 8, rows_a)
    signs_a = lax.dynamic_slice_in_dim(signs, start_a, rows_a, 1).reshape(groups, 8, rows_a)
    target_b = lax.dynamic_slice_in_dim(target, start_b, rows_b, 1).reshape(groups, 8, rows_b)
    signs_b = lax.dynamic_slice_in_dim(signs, start_b, rows_b, 1).reshape(groups, 8, rows_b)
    piece = lax.all_gather(masked, "ba", axis=1, tiled=True)
    start = jnp.int32(0)

    def one_group(items):
        tab, sgn = items
        hot = one_hot(tab, sgn, start, piece.shape[1])
        return jnp.einsum("pkc,ic->pik", hot, piece, preferred_element_type=jnp.float32)

    beta_sum = lax.map(one_group, (target_b, signs_b)).reshape(pairs, rows_a, rows_b)
    dbeta = (beta_sum * live_b[None, None, :]).astype(jnp.bfloat16)
    alpha_piece = lax.all_gather(masked, "aa", axis=0, tiled=True)
    alpha_start = jnp.int32(0)

    def one_group(items):
        tab, sgn = items
        hot = one_hot(tab, sgn, alpha_start, alpha_piece.shape[0])
        return jnp.einsum("pkj,jb->pkb", hot, alpha_piece, preferred_element_type=jnp.float32)

    alpha_sum = lax.map(one_group, (target_a, signs_a)).reshape(pairs, rows_a, rows_b)
    dalpha = (alpha_sum * live_a[None, :, None]).astype(jnp.bfloat16)
    weights = jnp.where(
        pair_irrep[:, None] == pair_irrep[None, :], integrals, jnp.zeros((), jnp.bfloat16)
    )
    gbeta_full = jnp.einsum("pq,qik->pik", weights, dbeta, preferred_element_type=jnp.float32)
    galpha_full = jnp.einsum("pq,qik->pik", weights, dalpha, preferred_element_type=jnp.float32)
    gbeta = gbeta_full.astype(jnp.bfloat16)
    combined = (gbeta_full + 0.5 * galpha_full).astype(jnp.bfloat16)
    local = jnp.einsum("p,pik->ik", one_body, dbeta, preferred_element_type=jnp.float32)
    local = local + jnp.einsum("p,pik->ik", one_body, dalpha, preferred_element_type=jnp.float32)
    half_beta = gbeta * 0.5
    gathered_piece = lax.all_gather(half_beta, "ba", axis=2, tiled=True)
    gathered_start = jnp.int32(0)
    width = gathered_piece.shape[2]

    def one_group(acc, items):
        tab, sgn, val = items
        hot = one_hot(tab, sgn, gathered_start, width)
        return (acc + jnp.einsum("pbk,pak->ab", hot, val, preferred_element_type=jnp.float32), None)

    total, _ = lax.scan(
        one_group,
        jnp.zeros((rows_a, rows_b), jnp.float32),
        (target_b, signs_b, gathered_piece.reshape(groups, 8, rows_a, width)),
    )
    beta_part = total
    alpha_rows = lax.psum_scatter(
        alpha_term(target, signs, combined, start_a, rows_a, rows_b, lax.axis_size("aa") * rows_a),
        "aa",
        scatter_dimension=0,
        tiled=True,
    )
    total = local + beta_part + alpha_rows
    return (total * (live_a[:, None] * live_b[None, :])).astype(jnp.bfloat16)


def solution(mesh):
    placed = (P("aa", "ba"), P(), P(), P(), P(), P())
    return jax.shard_map(
        per_device, mesh=mesh, in_specs=placed, out_specs=P("aa", "ba"), check_vma=False
    )
```

profile of v0, /device:TPU:0, one launch (start us, length us, event | category | flops | bytes accessed | tf_op | source)
XLA Modules:
  0.0 93.7 jit_solution(91153610101638624)
XLA Ops:
  7.4 0.7 broadcast_in_dim.92
  8.3 0.7 fusion.54
  8.9 0.8 multiply_multiply_fusion
  9.7 13.7 %all_gather.9 = bf16[64,512]{1,0:T(8,128)(2,1)S(1)} all-gather(bf16[64,128]{1,0:T(8,128)(2,1)S(1)} %multiply_multiply_fusion), channel_id=1, replica_groups=mesh['aa'=8,'ba'=4] {'ba'}, dimensions={1}, use_global_device_ids=true | all-gather | bytes 81920 | tf_op jit(solution)/shard_map/all_gather | solution.py:53
  23.4 0.9 abs_add_fusion
  24.4 3.7 %while.42 = (s32[]{:T(128)}, f32[4,8,64,128]{3,2,1,0:T(8,128)S(1)}, s32[4,8,128]{2,1,0:T(8,128)S(1)}, bf16[4,8,128]{2,1,0:T(8,128)(2,1)S(1)}, bf16[64,512]{1,0:T(8,128)(2,1)S(1)}, /*index=5*/s32[]{:T(128)}) while((s32[]{:T(128)}, f32[4,8,64,128]{3,2,1,0:T(8,128)S(1)}, s32[4,8,128]{2,1,0:T(8,128)S(1)}, bf16[4,8,128]{2,1,0:T(8,128)(2,1)S(1)}, ...), condition=%wide.region_1.2_spmd, body=%wide.region_0.1_spmd.sunk | while | flops 68157440 | bytes 346201 | solution.py:61
  24.5 0.9 fusion.67
  25.4 0.9 fusion.67
  26.3 0.9 fusion.67
  27.3 0.9 fusion.67
  28.2 1.6 %convert_multiply_fusion = (bf16[32,64,128]{2,0,1:T(8,128)(2,1)}, f32[32,64,128]{2,0,1:T(8,128)S(1)}) fusion(f32[32,64,128]{2,1,0:T(8,128)S(1)} %bitcast.112, f32[128]{0:T(128)S(1)} %get-tuple-element.227, bf16[32,32]{1,0:T(8,128)(2,1)S(1)} %copy-done.2, s32[32]{0:T(128)S(1)} %copy-done.3), kind=kOutput, calls=%fused_computation.55 | convolution fusion | flops 17827840 | bytes 2624128 | tf_op jit(solution)/shard_map/pq,qik->pik/dot_general | solution.py:76
  29.9 9.2 %all_gather.10 = bf16[512,128]{1,0:T(8,128)(2,1)S(1)} all-gather(bf16[64,128]{1,0:T(8,128)(2,1)S(1)} %multiply_multiply_fusion), channel_id=1, replica_groups=mesh['aa'=8,'ba'=4] {'aa'}, dimensions={0}, use_global_device_ids=true | all-gather | bytes 147456 | tf_op jit(solution)/shard_map/all_gather | solution.py:63
  39.4 1.6 %while.43 = (s32[]{:T(128)}, f32[4,8,64,128]{3,2,1,0:T(8,128)S(1)}, s32[4,8,64]{2,1,0:T(8,128)S(1)}, bf16[4,8,64]{2,1,0:T(8,128)(2,1)S(1)}, bf16[512,128]{1,0:T(8,128)(2,1)S(1)}, /*index=5*/s32[]{:T(128)}) while((s32[]{:T(128)}, f32[4,8,64,128]{3,2,1,0:T(8,128)S(1)}, s32[4,8,64]{2,1,0:T(8,128)S(1)}, bf16[4,8,64]{2,1,0:T(8,128)(2,1)S(1)}, ...), condition=%wide.region_3.4_spmd, body=%wide.region_2.3_spmd.sunk | while | flops 67633152 | bytes 405593 | solution.py:71
  41.0 2.2 %fusion.31 = bf16[4,8,64,128]{3,1,0,2:T(8,128)(2,1)} fusion(f32[32,64,128]{2,0,1:T(8,128)S(1)} %get-tuple-element.233, bf16[32,32]{1,0:T(8,128)(2,1)S(1)} %copy-done.2, s32[32]{0:T(128)S(1)} %copy-done.3, f32[32,64,128]{2,1,0:T(8,128)S(1)} %bitcast.110, f32[64]{0:T(128)} %get-tuple-element.225), kind=kOutput, calls=%fused_computation.50 | convolution fusion | flops 18089984 | bytes 2623872 | tf_op jit(solution)/shard_map/pq,qik->pik/dot_general | solution.py:77
  43.2 6.0 %while.45 = (s32[]{:T(128)}, f32[512,128]{1,0:T(8,128)S(1)}, s32[4,8,512]{2,1,0:T(8,128)S(1)}, s32[]{:T(128)}, bf16[4,8,512]{2,1,0:T(8,128)(2,1)S(1)}, /*index=5...) while((s32[]{:T(128)}, f32[512,128]{1,0:T(8,128)S(1)}, s32[4,8,512]{2,1,0:T(8,128)S(1)}, ...), condition=%wide.region_7.8_spmd.clone, body=%wide.region_6.7_spmd.clone.sunk | while | flops 67764288 | bytes 991863 | solution.py:27
  43.3 0.9 constant_dynamic-slice_fusion.5
  44.8 0.9 constant_dynamic-slice_fusion.5
  46.3 0.9 constant_dynamic-slice_fusion.5
  47.8 0.9 constant_dynamic-slice_fusion.5
  49.2 0.7 copy-done.1
  50.0 0.7 fusion.36
  50.6 0.7 fusion.46
  51.3 26.6 %all-gather.2.cloned.1.call-done = bf16[32,64,512]{2,0,1:T(8,128)(2,1)} async-done(((bf16[32,64,128]{2,0,1:T(8,128)(2,1)}), bf16[32,64,512]{2,0,1:T(8,128)(2,1)}) %all-gather.2.cloned.1.call-update) | async-done | bytes 2097168 | tf_op jit(solution)/shard_map/all_gather | solution.py:83
  77.9 6.8 %while.44 = (s32[]{:T(128)}, f32[64,128]{1,0:T(8,128)S(1)}, bf16[4,8,64,512]{3,1,0,2:T(8,128)(2,1)}, s32[4,8,128]{2,1,0:T(8,128)S(1)}, bf16[4,8,128]{2,1,0:T(8,128)(2,1)S(1)}, /*index=5*/s32[]{:T(128)}, s32[]{:T(128)}) while((s32[]{:T(128)}, f32[64,128]{1,0:T(8,128)S(1)}, bf16[4,8,64,512]{3,1,0,2:T(8,128)(2,1)}, ...), condition=%wide.region_5.6_spmd.clone, body=%wide.region_4.5_spmd.clone.sunk | while | flops 68173824 | bytes 1656939 | solution.py:92
  77.9 1.1 %constant_dynamic-slice_fusion.4 = bf16[1,8,64,512]{3,1,0,2:T(8,128)(2,1)S(1)} fusion(bf16[4,8,64,512]{3,1,0,2:T(8,128)(2,1)} %get-tuple-element.440, s32[]{:T(128)S(6)} %copy.61), kind=kLoop, calls=%fused_computation.32.clone.1 | loop fusion | bytes 1048580 | tf_op jit(solution)/shard_map/while/body/jit(dynamic_index_in_dim)/dynamic_slice | solution.py:92
  79.0 0.6 fusion.72
  79.6 1.1 %constant_dynamic-slice_fusion.4 = bf16[1,8,64,512]{3,1,0,2:T(8,128)(2,1)S(1)} fusion(bf16[4,8,64,512]{3,1,0,2:T(8,128)(2,1)} %get-tuple-element.440, s32[]{:T(128)S(6)} %copy.61), kind=kLoop, calls=%fused_computation.32.clone.1 | loop fusion | bytes 1048580 | tf_op jit(solution)/shard_map/while/body/jit(dynamic_index_in_dim)/dynamic_slice | solution.py:92
  80.7 0.6 fusion.72
  81.3 1.1 %constant_dynamic-slice_fusion.4 = bf16[1,8,64,512]{3,1,0,2:T(8,128)(2,1)S(1)} fusion(bf16[4,8,64,512]{3,1,0,2:T(8,128)(2,1)} %get-tuple-element.440, s32[]{:T(128)S(6)} %copy.61), kind=kLoop, calls=%fused_computation.32.clone.1 | loop fusion | bytes 1048580 | tf_op jit(solution)/shard_map/while/body/jit(dynamic_index_in_dim)/dynamic_slice | solution.py:92
  83.1 1.1 %constant_dynamic-slice_fusion.4 = bf16[1,8,64,512]{3,1,0,2:T(8,128)(2,1)S(1)} fusion(bf16[4,8,64,512]{3,1,0,2:T(8,128)(2,1)} %get-tuple-element.440, s32[]{:T(128)S(6)} %copy.61), kind=kLoop, calls=%fused_computation.32.clone.1 | loop fusion | bytes 1048580 | tf_op jit(solution)/shard_map/while/body/jit(dynamic_index_in_dim)/dynamic_slice | solution.py:92
  84.1 0.6 fusion.72
  84.8 1.4 %multiply_convert_fusion = bf16[64,128]{1,0:T(8,128)(2,1)} fusion(f32[64,128]{1,0:T(8,128)} %reduce-scatter.2.cloned.1.call-done, f32[64,128]{1,0:T(8,128)S(1)} %get-tuple-element.120, f32[64,128]{1,0:T(8,128)S(1)} %bitcast.116, f32[64,128]{1,0:T(8,128)S(1)} %bitcast.117, bf16[128]{0:T(256)(128)(2,1)S(1)} %get-tuple-element.228, ...), kind=kLoop, calls=%fused_computation.60 | loop fusion | flops 57344 | bytes 147840 | tf_op jit(solution)/shard_map/convert_element_type | solution.py:105
  (74 shorter events, 4.9 us)
Async XLA Ops:
  7.4 42.6 %copy-start = (bf16[32]{0:T(256)(128)(2,1)S(1)}, bf16[32]{0:T(256)(128)(2,1)}, u32[]{:S(2)}) copy-start(bf16[32]{0:T(256)(128)(2,1)} %param.19) | copy-start | bytes 196
  7.4 70.5 %all-gather.2.cloned.1.call-start = ((), (), s32[]{:S(2)}) async-start(), calls=%async_computation.1 | async-start | bytes 2621440 | tf_op jit(solution)/shard_map/all_gather | solution.py:83
  8.3 19.9 %copy-start.4 = (f32[128]{0:T(128)}, f32[128]{0:T(128)S(1)}, u32[]{:S(2)}) copy-start(f32[128]{0:T(128)S(1)} %get-tuple-element.227) | copy-start | bytes 1540
  24.4 3.8 %copy-start.2 = (bf16[32,32]{1,0:T(8,128)(2,1)S(1)}, bf16[32,32]{1,0:T(8,128)(2,1)}, u32[]{:S(2)}) copy-start(bf16[32,32]{1,0:T(8,128)(2,1)} %param.18) | copy-start | bytes 6148
  24.4 3.8 %copy-start.3 = (s32[32]{0:T(128)S(1)}, s32[32]{0:T(128)}, u32[]{:S(2)}) copy-start(s32[32]{0:T(128)} %param.17) | copy-start | bytes 388
  29.8 54.9 %reduce-scatter.2.cloned.1.call-start = ((), (), s32[]{:S(2)}) async-start(), calls=%async_computation.2 | async-start | bytes 294912 | tf_op jit(solution)/shard_map/reduce_scatter | solution.py:98
  43.2 6.7 %copy-start.5 = (f32[128]{0:T(128)S(1)}, f32[128]{0:T(128)}, u32[]{:S(2)}) copy-start(f32[128]{0:T(128)} %copy-done.4) | copy-start | bytes 1540
  43.2 7.4 %copy-start.6 = (f32[64]{0:T(128)S(1)}, f32[64]{0:T(128)}, u32[]{:S(2)}) copy-start(f32[64]{0:T(128)} %get-tuple-element.225) | copy-start | bytes 772
  49.2 0.7 copy-start.1
Sparse Core Ops, SparseCore 0:
  30.0 47.8 all-gather.1
Sparse Core Ops, SparseCore 1:
  50.0 32.6 reduce-scatter.1
where the time goes:
time: 94.2 us; the launch traced here: 93.7 us
  waiting for transfers between devices  26.6 us (28%)
  blocking collectives  22.9 us (24%)
  between operations  15 us (16%)
  matrix products  14.4 us (15%)
  local copies, waits for them, and re-layouts  10.2 us (11%)
  other arithmetic  3.85 us (4%)
    all_gather x1, waiting for transfers between devices, per_device(): gathered_piece = lax.all_gather(half_beta, 'ba', axis=2, tiled=True)  26.6 us
    all_gather x1, blocking collectives, per_device(): piece = lax.all_gather(masked, 'ba', axis=1, tiled=True)  13.7 us
    all_gather x1, blocking collectives, per_device(): alpha_piece = lax.all_gather(masked, 'aa', axis=0, tiled=True)  9.23 us
    dynamic_slice x4, local copies, waits for them, and re-layouts, per_device(): lax.scan(one_group, jnp.zeros((rows_a, rows_b), jnp.float32), (target_b,...  4.33 us
    dynamic_slice x4, local copies, waits for them, and re-layouts, alpha_term(): lax.scan(one_group, jnp.zeros((count, rows_b), jnp.float32), (rows_t, row...  3.68 us
    dot_general x4, matrix products, one_group(): jnp.einsum('pkc,ic->pik', hot, piece, preferred_element_type=jnp.float32)  3.52 us
    dot_general x4, matrix products, one_group(): jnp.einsum('pbk,pak->ab', hot, val, preferred_element_type=jnp.float32)  2.29 us
    dot_general x1, matrix products, per_device(): jnp.einsum('pq,qik->pik', weights, dalpha, preferred_element_type=jnp.flo...  2.22 us
  transfers between devices with their start and end apart: 2, of which 1 were waited for; matrix products, arithmetic and copies ran while one was open for 19% of the time, Pallas kernels for 0%

commit v1 on v0

v1 whole, which is shorter than its diff:
```python
import functools

import jax
import jax.numpy as jnp
from jax import lax
from jax.experimental import pallas as pl
from jax.experimental.pallas import tpu as pltpu
from jax.sharding import PartitionSpec as P

BF16 = jnp.bfloat16
F32 = jnp.float32
I32 = jnp.int32
RESIDENT = 8 * 2**20
VMEM_LIMIT = 48 * 2**20


def iota(shape, dim):
    return lax.broadcasted_iota(I32, shape, dim)


def dot(x, y):
    return jnp.dot(x, y, preferred_element_type=F32)


def dot_nt(x, y):
    return lax.dot_general(x, y, (((1,), (1,)), ((), ())), preferred_element_type=F32)


def live_ids(counts_ref, first, shape, dim, cap):
    ids = iota(shape, dim)
    block = ids // cap
    count = jnp.zeros(shape, I32)
    for j in range(shape[dim] // cap):
        count = jnp.where(block == j, counts_ref[first // cap + j], count)
    return jnp.where(ids - block * cap < count, ids + first + 1, -1)


def sign_of(code):
    return jnp.where(code > 0, 1.0, -1.0).astype(F32)


def mix_kernel(steps, cap, start, counts_ref, irrep_ref, code_ref, integrals_ref, gains_ref, mixed_ref, one_ref):
    pairs, strings = code_ref.shape
    rows = one_ref.shape[0]
    step = 0 if steps == 1 else pl.program_id(0)
    wide = pairs * 8
    ids = live_ids(counts_ref, 0, (1, strings), 1, cap)
    irrep_p = jnp.zeros((pairs, pairs), I32)
    irrep_q = jnp.zeros((pairs, pairs), I32)
    for p in range(pairs):
        irrep_p = jnp.where(iota((pairs, pairs), 0) == p, irrep_ref[p], irrep_p)
        irrep_q = jnp.where(iota((pairs, pairs), 1) == p, irrep_ref[p], irrep_q)
    weights = jnp.where(irrep_p == irrep_q, integrals_ref[...].astype(F32), 0.0).astype(BF16)
    spread_q = jnp.where(iota((wide, pairs), 0) // 8 == iota((wide, pairs), 1), 1.0, 0.0).astype(BF16)
    spread_p = jnp.where(iota((pairs, wide), 1) % pairs == iota((pairs, wide), 0), 1.0, 0.0).astype(BF16)
    left = jnp.concatenate(
        [dot_nt(spread_q, weights), jnp.broadcast_to(gains_ref[...].astype(F32), (8, pairs))], 0
    ).astype(BF16)
    mixer = dot(left, spread_p)
    same = iota(mixer.shape, 0) % 8 == iota(mixer.shape, 1) // pairs
    mixer = jnp.where(same, mixer, 0.0).astype(BF16)
    first = pl.multiple_of(start(step), 128)
    code = code_ref[:, pl.ds(first, rows)]
    size = jnp.abs(code)
    sign = sign_of(code)
    for base in range(0, rows, 16):
        halves = []
        for low in (base, base + 8):
            hot = jnp.concatenate(
                [
                    jnp.where(size[:, a : a + 1] == ids, sign[:, a : a + 1], 0.0).astype(BF16)
                    for a in range(low, low + 8)
                ],
                0,
            )
            part = dot(mixer, hot)
            one_ref[pl.ds(low, 8), :] = part[wide:]
            halves.append(part[:wide].reshape(pairs, 8, strings))
        mixed_ref[:, pl.ds(base, 16), :] = jnp.concatenate(halves, 1).astype(BF16)


def same_spin_kernel(steps, cap, origin, counts_ref, code_ref, mixed_ref, one_ref, low_ref, high_ref, hot_ref, message_ref, total_ref):
    pairs, rows, strings = mixed_ref.shape
    columns = low_ref.shape[1]
    step = 0 if steps == 1 else pl.program_id(0)
    first_a, first_b = origin()
    ids = live_ids(counts_ref, first_b, (columns, 128), 0, cap)
    ids = jnp.concatenate([ids] * (strings // 128), 1)

    @pl.when(step == 0)
    def _():
        total_ref[...] = jnp.zeros_like(total_ref)

    total = total_ref[...]
    for q in range(pairs):
        code = code_ref[q : q + 1, :]
        hot = jnp.where(jnp.abs(code) == ids, sign_of(code), 0.0).astype(BF16)
        hot_ref[pl.ds(q * columns, columns), :] = hot
        total = total + dot_nt(mixed_ref[q], hot)
    total_ref[...] = total

    @pl.when(step == steps - 1)
    def _():
        half = low_ref.shape[0]
        message_ref[:half] = low_ref[...]
        message_ref[half : 2 * half] = high_ref[...]
        one = one_ref[:, pl.ds(pl.multiple_of(first_b, 128), columns)]
        message_ref[2 * half :] = (one + 0.5 * total_ref[...]).astype(BF16)


def mixed_kernel(steps, groups, peers, place, mixed_ref, hot_ref, *refs):
    arrived = refs[:groups]
    own_ref, amplitudes_ref = refs[groups : groups + 2]
    sent = refs[groups + 2 : groups + 1 + peers]
    all_f, line, total_ref = refs[groups + 1 + peers :]
    pairs, rows, strings = mixed_ref.shape[0], own_ref.shape[0], mixed_ref.shape[2]
    columns = own_ref.shape[1]
    chip = 2 * rows
    step = 0 if steps == 1 else pl.program_id(0)
    group, core, column = place()

    @pl.when(step == 0)
    def _():
        for k in range(groups):
            at = pl.multiple_of((group ^ k) * chip, chip)
            amplitudes_ref[pl.ds(at, chip), :] = arrived[k][:chip]
            all_f[pl.ds(at, chip), :] = arrived[k][chip:]
        at = pl.multiple_of(core * rows, rows)
        total_ref[...] = dot_nt(arrived[0][pl.ds(at, rows), :], all_f[...])

    amplitudes = amplitudes_ref[...]
    at = pl.multiple_of(core * rows, rows) if mixed_ref.shape[1] != rows else 0
    for q in range(pairs):
        part = dot(mixed_ref[q, pl.ds(at, rows), :], amplitudes)
        line[:, pl.ds(q * columns, columns)] = part.astype(BF16)
    total_ref[...] += dot(line[...], hot_ref[...])

    @pl.when(step == steps - 1)
    def _():
        own_f = arrived[0][pl.ds(pl.multiple_of(chip + core * rows, rows), rows), :]
        for k in range(peers):
            part = total_ref[:, pl.ds(pl.multiple_of((column ^ k) * columns, columns), columns)]
            if k == 0:
                own_ref[...] = part
            else:
                sent[k - 1][:rows] = part.astype(BF16)
                sent[k - 1][rows:] = own_f


def final_kernel(groups, peers, cap, place, counts_ref, own_ref, amplitudes_ref, message_ref, *refs):
    arrived, out_ref = refs[:-1], refs[-1]
    rows, columns = own_ref.shape
    chip = 2 * rows
    first_a, core, column = place()
    total = own_ref[...]
    own_f = message_ref[pl.ds(pl.multiple_of(chip + core * rows, rows), rows), :]
    for k in range(peers):
        block = amplitudes_ref[pl.ds(pl.multiple_of((column ^ k) * columns, columns), columns), :]
        if k == 0:
            total = total + dot(own_f, block)
        else:
            total = total + arrived[k - 1][:rows].astype(F32) + dot(arrived[k - 1][rows:], block)
    live_a = live_ids(counts_ref, first_a, (rows, columns), 0, cap)
    live_b = live_ids(counts_ref, column * columns, (1, columns), 1, cap)
    out_ref[...] = jnp.where((live_a > 0) & (live_b > 0), total, 0.0).astype(BF16)


def per_device(sizes, amplitudes, code, counts, pair_irrep, integrals, one_body):
    rows, columns = amplitudes.shape
    pairs, strings = code.shape
    cap = strings // counts.shape[0]
    groups, peers = sizes[0] // 2, sizes[1]
    chip = 2 * rows
    names = ("aa", "ba")
    resident = pairs * chip * strings * 2 <= RESIDENT
    row_tiles = 1 if resident else chip // 128
    pair_tiles = 1 if resident else pairs // 4
    smem = pl.BlockSpec(memory_space=pltpu.SMEM)

    def whole():
        return pl.BlockSpec(memory_space=pltpu.VMEM)

    def tiled(shape, dim):
        if resident:
            return whole()
        return pl.BlockSpec(shape, lambda i: tuple(i if d == dim else 0 for d in range(len(shape))))

    def shape_of(shape, dtype):
        return pltpu.VMEM(shape, dtype) if resident else jax.ShapeDtypeStruct(shape, dtype)

    def near(value):
        return pltpu.with_memory_space_constraint(value, pltpu.VMEM) if resident else value

    def call(body, name, tiles, *args, **keys):
        if tiles > 1:
            keys["grid"] = (tiles,)
        params = pltpu.CompilerParams(vmem_limit_bytes=VMEM_LIMIT)
        return pl.pallas_call(body, name=name, compiler_params=params, **keys)(*args)

    def group_at():
        return lax.axis_index("aa") // 2

    def send(value, axis, mask):
        size = lax.axis_size(axis)
        return lax.ppermute(value, axis, [(i, i ^ mask) for i in range(size)])

    def kernel(body, *static):
        return functools.partial(body, *static)

    sibling = send(amplitudes, "aa", 1)
    tile = chip // row_tiles
    mixed, one = call(
        kernel(mix_kernel, row_tiles, cap, lambda step: group_at() * chip + step * tile),
        "mix",
        row_tiles,
        counts,
        pair_irrep,
        code,
        integrals,
        one_body.reshape(1, pairs),
        in_specs=[smem, smem, whole(), whole(), whole()],
        out_shape=(shape_of((pairs, chip, strings), BF16), shape_of((chip, strings), F32)),
        out_specs=(tiled((pairs, tile, strings), 1), tiled((tile, strings), 0)),
    )
    first = lax.axis_index("aa") % 2 == 0
    low = jnp.where(first, amplitudes, sibling)
    high = jnp.where(first, sibling, amplitudes)
    part = pairs // pair_tiles
    hot, message = call(
        kernel(same_spin_kernel, pair_tiles, cap, lambda: (group_at() * chip, lax.axis_index("ba") * columns)),
        "same_spin",
        pair_tiles,
        counts,
        code if pair_tiles == 1 else code.reshape(pair_tiles, part, strings),
        near(mixed),
        near(one),
        low,
        high,
        in_specs=[
            smem,
            whole() if pair_tiles == 1 else pl.BlockSpec((None, part, strings), lambda i: (i, 0, 0)),
            tiled((part, chip, strings), 0),
            whole(),
            whole(),
            whole(),
        ],
        out_shape=(shape_of((pairs * columns, strings), BF16), shape_of((2 * chip, columns), BF16)),
        out_specs=(tiled((part * columns, strings), 0), whole()),
        scratch_shapes=[pltpu.VMEM((chip, columns), F32)],
    )
    messages = [message] + [send(message, "aa", 2 * k) for k in range(1, groups)]
    core_of = lambda: lax.axis_index("aa") % 2
    outs = call(
        kernel(mixed_kernel, pair_tiles, groups, peers, lambda: (group_at(), core_of(), lax.axis_index("ba"))),
        "mixed",
        pair_tiles,
        near(mixed),
        near(hot),
        *[near(m) for m in messages],
        in_specs=[tiled((part, chip, strings), 0), tiled((part * columns, strings), 0)] + [whole()] * groups,
        out_shape=(shape_of((rows, columns), F32), shape_of((strings, columns), BF16))
        + tuple(shape_of((2 * rows, columns), BF16) for _ in range(peers - 1)),
        out_specs=tuple(whole() for _ in range(peers + 1)),
        scratch_shapes=[
            pltpu.VMEM((strings, columns), BF16),
            pltpu.VMEM((rows, part * columns), BF16),
            pltpu.VMEM((rows, strings), F32),
        ],
    )
    own, gathered = outs[:2]
    arrived = [send(m, "ba", k + 1) for k, m in enumerate(outs[2:])]
    return call(
        kernel(final_kernel, groups, peers, cap, lambda: (lax.axis_index("aa") * rows, core_of(), lax.axis_index("ba"))),
        "final",
        1,
        counts,
        near(own),
        near(gathered),
        near(message),
        *[near(m) for m in arrived],
        in_specs=[smem] + [whole()] * (2 + peers),
        out_shape=jax.ShapeDtypeStruct((rows, columns), BF16),
        out_specs=whole(),
    )


def solution(mesh):
    placed = (P("aa", "ba"), P(), P(), P(), P(), P())
    sizes = (mesh.shape["aa"], mesh.shape["ba"])
    return jax.shard_map(
        functools.partial(per_device, sizes), mesh=mesh, in_specs=placed, out_specs=P("aa", "ba"), check_vma=False
    )
```

time: 94.2 us -> 31.2 us (0.33)
  blocking collectives: 22.9 us -> 0 us
  waiting for transfers between devices: 26.6 us -> 9.62 us
  between operations: 15 us -> 0.04 us
  matrix products: 14.4 us -> 0 us
  starting transfers between devices: 0.05 us -> 9.06 us
  Pallas kernels: 0 us -> 7.24 us
  local copies, waits for them, and re-layouts: 10.2 us -> 3.5 us
  other arithmetic: 3.85 us -> 1.33 us
    all_gather x1 -> x0, waiting for transfers between devices: 26.6 us -> none  [per_device(): gathered_piece = lax.all_gather(half_beta, 'ba', axis=2, tiled=True)]
    all_gather x2 -> x0, blocking collectives: 22.9 us -> none  [the longest x1 13.7 us: per_device(): piece = lax.all_gather(masked, 'ba', axis=1, tiled=True)]
    dot_general x20 -> x0, matrix products: 14.4 us -> none  [the longest x4 3.52 us: one_group(): jnp.einsum('pkc,ic->pik', hot, piece, preferred_element_type=jnp.float32)]
    ppermute x0 -> x7, waiting for transfers between devices: none -> 9.62 us  [send(): return lax.ppermute(value, axis, [(i, i ^ mask) for i in range(size)])]
    ppermute x0 -> x7, starting transfers between devices: none -> 9.06 us  [send(): return lax.ppermute(value, axis, [(i, i ^ mask) for i in range(size)])]
    dynamic_slice x8 -> x0, local copies, waits for them, and re-layouts: 8.02 us -> none  [the longest x4 4.33 us: per_device(): lax.scan(one_group, jnp.zeros((rows_a, rows_b), jnp.float32), (target_b,...]
    pallas_call x0 -> x4, Pallas kernels: none -> 7.24 us  [call(): pl.pallas_call(body, name=name, compiler_params=params, **keys)(*args)]
    unnamed x14 -> x12, local copies, waits for them, and re-layouts: 0.74 us -> 3.5 us
  transfers between devices with their start and end apart: 2 -> 7, of which waited for: 1 -> 5; matrix products, arithmetic and copies ran while one was open for 19% -> 0% of each run, Pallas kernels for 0% -> 7%
where the time goes in v1:
time: 31.2 us; the launch traced here: 30.8 us
  waiting for transfers between devices  9.62 us (31%)
  starting transfers between devices  9.06 us (29%)
  Pallas kernels  7.24 us (23%)
  local copies, waits for them, and re-layouts  3.5 us (11%)
  other arithmetic  1.33 us (4%)
    ppermute x7, waiting for transfers between devices, send(): return lax.ppermute(value, axis, [(i, i ^ mask) for i in range(size)])  9.62 us
    ppermute x7, starting transfers between devices, send(): return lax.ppermute(value, axis, [(i, i ^ mask) for i in range(size)])  9.06 us
    pallas_call x4, Pallas kernels, call(): pl.pallas_call(body, name=name, compiler_params=params, **keys)(*args)  7.24 us
    unnamed x12, local copies, waits for them, and re-layouts  3.5 us
    select_n x1, other arithmetic, per_device(): high = jnp.where(first, sibling, amplitudes)  1.33 us
  transfers between devices with their start and end apart: 7, of which 5 were waited for; matrix products, arithmetic and copies ran while one was open for 0% of the time, Pallas kernels for 7%

profile of v1, /device:TPU:0, one launch (start us, length us, event | category | flops | bytes accessed | tf_op | source)
XLA Modules:
  0.0 30.8 jit_solution(2900936930475177345)
XLA Ops:
  0.0 0.5 %collective-permute-start = (bf16[64,128]{1,0:T(8,128)(2,1)}, bf16[64,128]{1,0:T(8,128)(2,1)S(1)}, u32[]{:S(2)}, u32[]{:S(2)}) collective-permute-start(bf16[64,128]{1,0:T(8,128)(2,1)} %param.6), channel_id=1, source_target_pairs={{0,4},{4,0},{8,12},{12,8},{16,20},{20,16},{24,28},{28,24},{1,5},{5... | collective-permute-start | bytes 49160 | tf_op jit(solution)/shard_map/ppermute | solution.py:205
  0.5 0.0 copy-start
  0.5 0.8 %copy-done = s32[32,512]{1,0:T(8,128)S(1)} copy-done((s32[32,512]{1,0:T(8,128)S(1)}, s32[32,512]{1,0:T(8,128)}, u32[]{:S(2)}) %copy-start) | copy-done | bytes 65560
  1.3 0.0 copy-start.1
  1.3 0.7 %copy-done.1 = bf16[32,32]{1,0:T(8,128)(2,1)S(1)} copy-done((bf16[32,32]{1,0:T(8,128)(2,1)S(1)}, bf16[32,32]{1,0:T(8,128)(2,1)}, u32[]{:S(2)}) %copy-start.1) | copy-done | bytes 2072
  2.0 0.0 copy-start.2
  2.0 0.7 %copy-done.2 = s32[32]{0:T(128)S(1)} copy-done((s32[32]{0:T(128)S(1)}, s32[32]{0:T(128)}, u32[]{:S(2)}) %copy-start.2) | copy-done | bytes 152
  2.6 0.0 copy-start.4
  2.6 0.7 %copy-done.4 = s32[32]{0:T(128)S(1)} copy-done((s32[32]{0:T(128)S(1)}, s32[32]{0:T(128)}, u32[]{:S(2)}) %copy-start.4) | copy-done | bytes 152
  3.3 0.0 copy-start.5
  3.3 0.7 %copy-done.5 = bf16[32]{0:T(256)(128)(2,1)S(1)} copy-done((bf16[32]{0:T(256)(128)(2,1)S(1)}, bf16[32]{0:T(256)(128)(2,1)}, u32[]{:S(2)}) %copy-start.5) | copy-done | bytes 88
  4.0 2.1 %mix.1 = (bf16[32,128,512]{2,1,0:T(8,128)(2,1)S(1)}, f32[128,512]{1,0:T(8,128)S(1)}) custom-call(s32[32]{0:T(128)S(1)} %copy-done.2, s32[32]{0:T(128)S(1)} %copy-done.4, s32[32,512]{1,0:T(8,128)S(1)} %copy-done, bf16[32,32]{1,0:T(8,128)(2,1)S(1)} %copy-done.1, bf16[1,32]{1,0:T(2,128)(2,1)S(1)} %bitcast.1), custom_call_target="tpu_custom_call" | custom-call | tf_op jit(solution)/shard_map/mix/pallas_call | solution.py:198
  6.1 0.0 collective-permute-done
  6.1 1.3 %broadcast_select_fusion = (bf16[64,128]{1,0:T(8,128)(2,1)}, bf16[64,128]{1,0:T(8,128)(2,1)}) fusion(bf16[64,128]{1,0:T(8,128)(2,1)S(1)} %collective-permute-done, bf16[64,128]{1,0:T(8,128)(2,1)} %param.6, pred[]{:T(512)S(6)} %eq.5), kind=kLoop, calls=%fused_computation | loop fusion | flops 16384 | bytes 65537 | tf_op jit(solution)/shard_map/jit(_where)/select_n | solution.py:227
  7.4 2.3 %same_spin.1 = (bf16[4096,512]{1,0:T(8,128)(2,1)S(1)}, bf16[256,128]{1,0:T(8,128)(2,1)S(1)}) custom-call(s32[32]{0:T(128)} %counts_ref.5, s32[32,512]{1,0:T(8,128)} %code_ref.3, bf16[32,128,512]{2,1,0:T(8,128)(2,1)S(1)} %get-tuple-element.14.mixed_ref, f32[128,512]{1,0:T(8,128)S(1)} %get-tuple-element.15.one_ref, bf16[64,128]{1,0:T(8,128)(2,1)} %get-tuple-element.24.low_ref, ...), custom_call_target="tpu_custom_call" | custom-call | tf_op jit(solution)/shard_map/same_spin/pallas_call | solution.py:198
  9.7 3.5 %collective-permute-start.3 = (bf16[256,128]{1,0:T(8,128)(2,1)S(1)}, bf16[256,128]{1,0:T(8,128)(2,1)S(1)}, u32[]{:S(2)}, u32[]{:S(2)}) collective-permute-start(bf16[256,128]{1,0:T(8,128)(2,1)S(1)} %get-tuple-element.17.refs_0_.message_ref), channel_id=1, source_target_pairs={{0,24},{4,28},{8,16},{12,20},{16,8},{20,12},{24,0},{28,4},{1,25},{... | collective-permute-start | bytes 196616 | tf_op jit(solution)/shard_map/ppermute | solution.py:205
  13.2 0.5 %collective-permute-start.2 = (bf16[256,128]{1,0:T(8,128)(2,1)S(1)}, bf16[256,128]{1,0:T(8,128)(2,1)S(1)}, u32[]{:S(2)}, u32[]{:S(2)}) collective-permute-start(bf16[256,128]{1,0:T(8,128)(2,1)S(1)} %get-tuple-element.17.refs_0_.message_ref), channel_id=1, source_target_pairs={{0,16},{4,20},{8,24},{12,28},{16,0},{20,4},{24,8},{28,12},{1,17},{... | collective-permute-start | bytes 196616 | tf_op jit(solution)/shard_map/ppermute | solution.py:205
  13.7 0.1 collective-permute-start.1
  13.9 2.1 %collective-permute-done.3.refs_3_ = bf16[256,128]{1,0:T(8,128)(2,1)S(1)} collective-permute-done((bf16[256,128]{1,0:T(8,128)(2,1)S(1)}, bf16[256,128]{1,0:T(8,128)(2,1)S(1)}, u32[]{:S(2)}, u32[]{:S(2)}) %collective-permute-start.3) | collective-permute-done | bytes 65568 | tf_op jit(solution)/shard_map/ppermute | solution.py:205
  16.0 1.5 %collective-permute-done.2.refs_2_ = bf16[256,128]{1,0:T(8,128)(2,1)S(1)} collective-permute-done((bf16[256,128]{1,0:T(8,128)(2,1)S(1)}, bf16[256,128]{1,0:T(8,128)(2,1)S(1)}, u32[]{:S(2)}, u32[]{:S(2)}) %collective-permute-start.2) | collective-permute-done | bytes 65568 | tf_op jit(solution)/shard_map/ppermute | solution.py:205
  17.5 0.5 %collective-permute-done.1.refs_1_ = bf16[256,128]{1,0:T(8,128)(2,1)S(1)} collective-permute-done((bf16[256,128]{1,0:T(8,128)(2,1)S(1)}, bf16[256,128]{1,0:T(8,128)(2,1)S(1)}, u32[]{:S(2)}, u32[]{:S(2)}) %collective-permute-start.1) | collective-permute-done | bytes 65568 | tf_op jit(solution)/shard_map/ppermute | solution.py:205
  18.0 0.0 copy-start.3
  18.0 1.5 %mixed.1 = (f32[64,128]{1,0:T(8,128)S(1)}, bf16[512,128]{1,0:T(8,128)(2,1)S(1)}, bf16[128,128]{1,0:T(8,128)(2,1)S(1)}, bf16[128,128]{1,0:T(8,128)(2,1)S(1)}, bf16[128,128]{1,0:T(8,128)(2,1)S(1)}) custom-call(bf16[32,128,512]{2,1,0:T(8,128)(2,1)S(1)} %get-tuple-element.14.mixed_ref, bf16[4096,512]{1,0:T(8,128)(2,1)S(1)} %get-tuple-element.16.hot_ref, ...), custom_call_target="tpu_custom_call" | custom-call | tf_op jit(solution)/shard_map/mixed/pallas_call | solution.py:198
  19.5 1.6 %collective-permute-start.4 = (bf16[128,128]{1,0:T(8,128)(2,1)S(1)}, bf16[128,128]{1,0:T(8,128)(2,1)S(1)}, u32[]{:S(2)}, u32[]{:S(2)}) collective-permute-start(bf16[128,128]{1,0:T(8,128)(2,1)S(1)} %get-tuple-element.20), channel_id=1, source_target_pairs={{0,1},{1,0},{2,3},{3,2},{4,5},{5,4},{6,7},{7,6},{8,9},{9,8},{10,11... | collective-permute-start | bytes 98312 | tf_op jit(solution)/shard_map/ppermute | solution.py:205
  21.2 2.6 %collective-permute-start.5 = (bf16[128,128]{1,0:T(8,128)(2,1)S(1)}, bf16[128,128]{1,0:T(8,128)(2,1)S(1)}, u32[]{:S(2)}, u32[]{:S(2)}) collective-permute-start(bf16[128,128]{1,0:T(8,128)(2,1)S(1)} %get-tuple-element.21), channel_id=1, source_target_pairs={{0,2},{1,3},{2,0},{3,1},{4,6},{5,7},{6,4},{7,5},{8,10},{9,11},{10,... | collective-permute-start | bytes 98312 | tf_op jit(solution)/shard_map/ppermute | solution.py:205
  23.8 0.2 collective-permute-start.6
  24.0 0.0 collective-permute-done.4.refs_0_
  24.0 2.3 %collective-permute-done.5.refs_1_ = bf16[128,128]{1,0:T(8,128)(2,1)S(1)} collective-permute-done((bf16[128,128]{1,0:T(8,128)(2,1)S(1)}, bf16[128,128]{1,0:T(8,128)(2,1)S(1)}, u32[]{:S(2)}, u32[]{:S(2)}) %collective-permute-start.5) | collective-permute-done | bytes 32800 | tf_op jit(solution)/shard_map/ppermute | solution.py:205
  26.2 3.2 %collective-permute-done.6.refs_2_ = bf16[128,128]{1,0:T(8,128)(2,1)S(1)} collective-permute-done((bf16[128,128]{1,0:T(8,128)(2,1)S(1)}, bf16[128,128]{1,0:T(8,128)(2,1)S(1)}, u32[]{:S(2)}, u32[]{:S(2)}) %collective-permute-start.6) | collective-permute-done | bytes 32800 | tf_op jit(solution)/shard_map/ppermute | solution.py:205
  29.5 0.0 copy-done.3
  29.5 1.3 %final.1 = bf16[64,128]{1,0:T(8,128)(2,1)} custom-call(s32[32]{0:T(128)S(1)} %copy-done.3, f32[64,128]{1,0:T(8,128)S(1)} %get-tuple-element.18.own_ref, bf16[512,128]{1,0:T(8,128)(2,1)S(1)} %get-tuple-element.19.amplitudes_ref, bf16[256,128]{1,0:T(8,128)(2,1)S(1)} %get-tuple-element.17.refs_0_.message_ref, ...), custom_call_target="tpu_custom_call" | custom-call | tf_op jit(solution)/shard_map/final/pallas_call | solution.py:198
Async XLA Ops:
  0.0 6.1 %collective-permute-start = (bf16[64,128]{1,0:T(8,128)(2,1)}, bf16[64,128]{1,0:T(8,128)(2,1)S(1)}, u32[]{:S(2)}, u32[]{:S(2)}) collective-permute-start(bf16[64,128]{1,0:T(8,128)(2,1)} %param.6), channel_id=1, source_target_pairs={{0,4},{4,0},{8,12},{12,8},{16,20},{20,16},{24,28},{28,24},{1,5},{5... | collective-permute-start | bytes 49160 | tf_op jit(solution)/shard_map/ppermute | solution.py:205
  0.5 0.8 %copy-start = (s32[32,512]{1,0:T(8,128)S(1)}, s32[32,512]{1,0:T(8,128)}, u32[]{:S(2)}) copy-start(s32[32,512]{1,0:T(8,128)} %code_ref.3) | copy-start | bytes 196612
  1.3 0.7 %copy-start.1 = (bf16[32,32]{1,0:T(8,128)(2,1)S(1)}, bf16[32,32]{1,0:T(8,128)(2,1)}, u32[]{:S(2)}) copy-start(bf16[32,32]{1,0:T(8,128)(2,1)} %integrals_ref.1) | copy-start | bytes 6148
  2.0 0.7 %copy-start.2 = (s32[32]{0:T(128)S(1)}, s32[32]{0:T(128)}, u32[]{:S(2)}) copy-start(s32[32]{0:T(128)} %counts_ref.5) | copy-start | bytes 388
  2.6 0.7 %copy-start.4 = (s32[32]{0:T(128)S(1)}, s32[32]{0:T(128)}, u32[]{:S(2)}) copy-start(s32[32]{0:T(128)} %irrep_ref.1) | copy-start | bytes 388
  3.3 0.7 %copy-start.5 = (bf16[32]{0:T(256)(128)(2,1)S(1)}, bf16[32]{0:T(256)(128)(2,1)}, u32[]{:S(2)}) copy-start(bf16[32]{0:T(256)(128)(2,1)} %param.11) | copy-start | bytes 196
  9.7 6.3 %collective-permute-start.3 = (bf16[256,128]{1,0:T(8,128)(2,1)S(1)}, bf16[256,128]{1,0:T(8,128)(2,1)S(1)}, u32[]{:S(2)}, u32[]{:S(2)}) collective-permute-start(bf16[256,128]{1,0:T(8,128)(2,1)S(1)} %get-tuple-element.17.refs_0_.message_ref), channel_id=1, source_target_pairs={{0,24},{4,28},{8,16},{12,20},{16,8},{20,12},{24,0},{28,4},{1,25},{... | collective-permute-start | bytes 196616 | tf_op jit(solution)/shard_map/ppermute | solution.py:205
  13.2 4.3 %collective-permute-start.2 = (bf16[256,128]{1,0:T(8,128)(2,1)S(1)}, bf16[256,128]{1,0:T(8,128)(2,1)S(1)}, u32[]{:S(2)}, u32[]{:S(2)}) collective-permute-start(bf16[256,128]{1,0:T(8,128)(2,1)S(1)} %get-tuple-element.17.refs_0_.message_ref), channel_id=1, source_target_pairs={{0,16},{4,20},{8,24},{12,28},{16,0},{20,4},{24,8},{28,12},{1,17},{... | collective-permute-start | bytes 196616 | tf_op jit(solution)/shard_map/ppermute | solution.py:205
  13.7 4.3 %collective-permute-start.1 = (bf16[256,128]{1,0:T(8,128)(2,1)S(1)}, bf16[256,128]{1,0:T(8,128)(2,1)S(1)}, u32[]{:S(2)}, u32[]{:S(2)}) collective-permute-start(bf16[256,128]{1,0:T(8,128)(2,1)S(1)} %get-tuple-element.17.refs_0_.message_ref), channel_id=1, source_target_pairs={{0,8},{4,12},{8,0},{12,4},{16,24},{20,28},{24,16},{28,20},{1,9},{5... | collective-permute-start | bytes 196616 | tf_op jit(solution)/shard_map/ppermute | solution.py:205
  18.0 11.5 %copy-start.3 = (s32[32]{0:T(128)S(1)}, s32[32]{0:T(128)}, u32[]{:S(2)}) copy-start(s32[32]{0:T(128)} %counts_ref.5) | copy-start | bytes 388
  19.5 4.5 %collective-permute-start.4 = (bf16[128,128]{1,0:T(8,128)(2,1)S(1)}, bf16[128,128]{1,0:T(8,128)(2,1)S(1)}, u32[]{:S(2)}, u32[]{:S(2)}) collective-permute-start(bf16[128,128]{1,0:T(8,128)(2,1)S(1)} %get-tuple-element.20), channel_id=1, source_target_pairs={{0,1},{1,0},{2,3},{3,2},{4,5},{5,4},{6,7},{7,6},{8,9},{9,8},{10,11... | collective-permute-start | bytes 98312 | tf_op jit(solution)/shard_map/ppermute | solution.py:205
  21.2 5.1 %collective-permute-start.5 = (bf16[128,128]{1,0:T(8,128)(2,1)S(1)}, bf16[128,128]{1,0:T(8,128)(2,1)S(1)}, u32[]{:S(2)}, u32[]{:S(2)}) collective-permute-start(bf16[128,128]{1,0:T(8,128)(2,1)S(1)} %get-tuple-element.21), channel_id=1, source_target_pairs={{0,2},{1,3},{2,0},{3,1},{4,6},{5,7},{6,4},{7,5},{8,10},{9,11},{10,... | collective-permute-start | bytes 98312 | tf_op jit(solution)/shard_map/ppermute | solution.py:205
  23.8 5.7 %collective-permute-start.6 = (bf16[128,128]{1,0:T(8,128)(2,1)S(1)}, bf16[128,128]{1,0:T(8,128)(2,1)S(1)}, u32[]{:S(2)}, u32[]{:S(2)}) collective-permute-start(bf16[128,128]{1,0:T(8,128)(2,1)S(1)} %get-tuple-element.22), channel_id=1, source_target_pairs={{0,3},{1,2},{2,1},{3,0},{4,7},{5,6},{6,5},{7,4},{8,11},{9,10},{10,... | collective-permute-start | bytes 98312 | tf_op jit(solution)/shard_map/ppermute | solution.py:205

commit v2 on v1

v2 whole, which is shorter than its diff:
```python
import functools

import jax
import jax.numpy as jnp
from jax import lax
from jax.experimental import pallas as pl
from jax.experimental.pallas import tpu as pltpu
from jax.sharding import PartitionSpec as P

BF16 = jnp.bfloat16
F32 = jnp.float32
I32 = jnp.int32
RESIDENT = 8 * 2**20
VMEM_LIMIT = 48 * 2**20


def iota(shape, dim):
    return lax.broadcasted_iota(I32, shape, dim)


def dot(x, y):
    return jnp.dot(x, y, preferred_element_type=F32)


def dot_nt(x, y):
    return lax.dot_general(x, y, (((1,), (1,)), ((), ())), preferred_element_type=F32)


def live_ids(counts_ref, first, shape, dim, cap):
    ids = iota(shape, dim)
    block = ids // cap
    count = jnp.zeros(shape, I32)
    for j in range(shape[dim] // cap):
        count = jnp.where(block == j, counts_ref[first // cap + j], count)
    return jnp.where(ids - block * cap < count, ids + first + 1, -1)


def sign_of(code):
    return jnp.where(code > 0, 1.0, -1.0).astype(F32)


def mix_kernel(steps, cap, place, counts_hbm, irrep_hbm, code_hbm, integrals_hbm, gains_hbm, amplitudes_hbm, *refs):
    mixed_ref, one_ref, code_ref, ids_ref, alive_ref, amplitudes_ref = refs[:6]
    counts_ref, irrep_ref, integrals_ref, gains_ref, sems = refs[6:]
    pairs, strings = code_ref.shape
    tile = one_ref.shape[0]
    rows, columns = amplitudes_ref.shape
    step = 0 if steps == 1 else pl.program_id(0)
    group, first_a, first_b = place()
    copies = [
        pltpu.make_async_copy(source, target, sems.at[i])
        for i, (source, target) in enumerate(
            (
                (counts_hbm, counts_ref),
                (irrep_hbm, irrep_ref),
                (code_hbm, code_ref),
                (integrals_hbm, integrals_ref),
                (gains_hbm, gains_ref),
                (amplitudes_hbm, amplitudes_ref),
            )
        )
    ]
    for copy in copies:
        copy.start()
    wide = pairs * 8
    spread_q = jnp.where(iota((wide, pairs), 0) // 8 == iota((wide, pairs), 1), 1.0, 0.0).astype(BF16)
    spread_p = jnp.where(iota((pairs, wide), 1) % pairs == iota((pairs, wide), 0), 1.0, 0.0).astype(BF16)
    for copy in copies:
        copy.wait()
    ids = live_ids(counts_ref, 0, (1, strings), 1, cap)
    ids_ref[...] = live_ids(counts_ref, first_b, ids_ref.shape, 0, cap)
    live_a = live_ids(counts_ref, first_a, (rows, columns), 0, cap)
    live_b = live_ids(counts_ref, first_b, (1, columns), 1, cap)
    alive_ref[...] = jnp.where((live_a > 0) & (live_b > 0), 1.0, 0.0)
    irrep_p = jnp.zeros((pairs, pairs), I32)
    irrep_q = jnp.zeros((pairs, pairs), I32)
    for p in range(pairs):
        irrep_p = jnp.where(iota((pairs, pairs), 0) == p, irrep_ref[p], irrep_p)
        irrep_q = jnp.where(iota((pairs, pairs), 1) == p, irrep_ref[p], irrep_q)
    weights = jnp.where(irrep_p == irrep_q, integrals_ref[...].astype(F32), 0.0).astype(BF16)
    left = jnp.concatenate(
        [dot_nt(spread_q, weights), jnp.broadcast_to(gains_ref[...].astype(F32), (8, pairs))], 0
    ).astype(BF16)
    mixer = dot(left, spread_p)
    same = iota(mixer.shape, 0) % 8 == iota(mixer.shape, 1) // pairs
    mixer = jnp.where(same, mixer, 0.0).astype(BF16)
    code = code_ref[:, pl.ds(pl.multiple_of(group * 2 * rows + step * tile, 128), tile)]
    size = jnp.abs(code)
    sign = sign_of(code)
    for base in range(0, tile, 16):
        halves = []
        for low in (base, base + 8):
            hot = jnp.concatenate(
                [
                    jnp.where(size[:, a : a + 1] == ids, sign[:, a : a + 1], 0.0).astype(BF16)
                    for a in range(low, low + 8)
                ],
                0,
            )
            part = dot(mixer, hot)
            one_ref[pl.ds(low, 8), :] = part[wide:]
            halves.append(part[:wide].reshape(pairs, 8, strings))
        mixed_ref[:, pl.ds(base, 16), :] = jnp.concatenate(halves, 1).astype(BF16)


def same_spin_kernel(steps, place, ids_ref, code_ref, mixed_ref, one_ref, own_ref, sibling_ref, hot_ref, message_ref, total_ref):
    pairs, chip, strings = mixed_ref.shape
    rows, columns = own_ref.shape
    step = 0 if steps == 1 else pl.program_id(0)
    core, first_b = place()
    ids = jnp.concatenate([ids_ref[...]] * (strings // 128), 1)

    @pl.when(step == 0)
    def _():
        total_ref[...] = jnp.zeros_like(total_ref)

    total = total_ref[...]
    for q in range(pairs):
        code = code_ref[q : q + 1, :]
        hot = jnp.where(jnp.abs(code) == ids, sign_of(code), 0.0).astype(BF16)
        hot_ref[pl.ds(q * columns, columns), :] = hot
        total = total + dot_nt(mixed_ref[q], hot)
    total_ref[...] = total

    @pl.when(step == steps - 1)
    def _():
        message_ref[pl.ds(pl.multiple_of(core * rows, rows), rows), :] = own_ref[...]
        message_ref[pl.ds(pl.multiple_of((1 - core) * rows, rows), rows), :] = sibling_ref[...]
        one = one_ref[:, pl.ds(pl.multiple_of(first_b, 128), columns)]
        message_ref[chip:] = (one + 0.5 * total_ref[...]).astype(BF16)


def mixed_kernel(steps, groups, peers, place, mixed_ref, hot_ref, *refs):
    arrived = refs[:groups]
    own_ref, amplitudes_ref = refs[groups : groups + 2]
    sent = refs[groups + 2 : groups + 1 + peers]
    all_f, line, total_ref = refs[groups + 1 + peers :]
    pairs, rows, strings = mixed_ref.shape[0], own_ref.shape[0], mixed_ref.shape[2]
    columns = own_ref.shape[1]
    chip = 2 * rows
    step = 0 if steps == 1 else pl.program_id(0)
    group, core, column = place()

    @pl.when(step == 0)
    def _():
        for k in range(groups):
            at = pl.multiple_of((group ^ k) * chip, chip)
            amplitudes_ref[pl.ds(at, chip), :] = arrived[k][:chip]
            all_f[pl.ds(at, chip), :] = arrived[k][chip:]
        at = pl.multiple_of(core * rows, rows)
        total_ref[...] = dot_nt(arrived[0][pl.ds(at, rows), :], all_f[...])

    amplitudes = amplitudes_ref[...]
    at = pl.multiple_of(core * rows, rows) if mixed_ref.shape[1] != rows else 0
    for q in range(pairs):
        part = dot(mixed_ref[q, pl.ds(at, rows), :], amplitudes)
        line[:, pl.ds(q * columns, columns)] = part.astype(BF16)
    total_ref[...] += dot(line[...], hot_ref[...])

    @pl.when(step == steps - 1)
    def _():
        own_f = arrived[0][pl.ds(pl.multiple_of(chip + core * rows, rows), rows), :]
        for k in range(peers):
            part = total_ref[:, pl.ds(pl.multiple_of((column ^ k) * columns, columns), columns)]
            if k == 0:
                own_ref[...] = part
            else:
                sent[k - 1][:rows] = part.astype(BF16)
                sent[k - 1][rows:] = own_f


def final_kernel(peers, place, alive_ref, own_ref, amplitudes_ref, message_ref, *refs):
    arrived, out_ref = refs[:-1], refs[-1]
    rows, columns = own_ref.shape
    core, column = place()
    total = own_ref[...]
    own_f = message_ref[pl.ds(pl.multiple_of((2 + core) * rows, rows), rows), :]
    for k in range(peers):
        block = amplitudes_ref[pl.ds(pl.multiple_of((column ^ k) * columns, columns), columns), :]
        if k == 0:
            total = total + dot(own_f, block)
        else:
            total = total + arrived[k - 1][:rows].astype(F32) + dot(arrived[k - 1][rows:], block)
    out_ref[...] = (total * alive_ref[...]).astype(BF16)


def per_device(sizes, amplitudes, code, counts, pair_irrep, integrals, one_body):
    rows, columns = amplitudes.shape
    pairs, strings = code.shape
    cap = strings // counts.shape[0]
    groups, peers = sizes[0] // 2, sizes[1]
    chip = 2 * rows
    resident = pairs * chip * strings * 2 <= RESIDENT
    row_tiles = 1 if resident else chip // 128
    pair_tiles = 1 if resident else pairs // 4
    tile, part = chip // row_tiles, pairs // pair_tiles
    hbm = pl.BlockSpec(memory_space=pl.ANY)
    vmem = pl.BlockSpec(memory_space=pltpu.VMEM)

    def tiled(shape, dim):
        if resident:
            return vmem
        return pl.BlockSpec(shape, lambda i: tuple(i if d == dim else 0 for d in range(len(shape))))

    def shape_of(shape, dtype):
        return pltpu.VMEM(shape, dtype) if resident else jax.ShapeDtypeStruct(shape, dtype)

    def near(value):
        return pltpu.with_memory_space_constraint(value, pltpu.VMEM) if resident else value

    def far(value):
        return pltpu.with_memory_space_constraint(value, pltpu.HBM)

    def call(body, name, tiles, *args, **keys):
        if tiles > 1:
            keys["grid"] = (tiles,)
        params = pltpu.CompilerParams(vmem_limit_bytes=VMEM_LIMIT)
        return pl.pallas_call(body, name=name, compiler_params=params, **keys)(*args)

    def send(value, axis, mask):
        return lax.ppermute(value, axis, [(i, i ^ mask) for i in range(lax.axis_size(axis))])

    def alpha():
        return lax.axis_index("aa")

    def beta():
        return lax.axis_index("ba")

    sibling = send(amplitudes, "aa", 1)
    mixed, one, codes, ids, alive, own_c = call(
        functools.partial(mix_kernel, row_tiles, cap, lambda: (alpha() // 2, alpha() * rows, beta() * columns)),
        "mix",
        row_tiles,
        far(counts),
        far(pair_irrep),
        far(code),
        far(integrals),
        far(one_body.reshape(1, pairs)),
        far(amplitudes),
        in_specs=[hbm] * 6,
        out_shape=(
            shape_of((pairs, chip, strings), BF16),
            shape_of((chip, strings), F32),
            shape_of((pairs, strings), I32),
            shape_of((columns, 128), I32),
            shape_of((rows, columns), F32),
            shape_of((rows, columns), BF16),
        ),
        out_specs=(tiled((pairs, tile, strings), 1), tiled((tile, strings), 0), vmem, vmem, vmem, vmem),
        scratch_shapes=[
            pltpu.SMEM(counts.shape, I32),
            pltpu.SMEM(pair_irrep.shape, I32),
            pltpu.VMEM((pairs, pairs), BF16),
            pltpu.VMEM((1, pairs), BF16),
            pltpu.SemaphoreType.DMA((6,)),
        ],
    )
    hot, message = call(
        functools.partial(same_spin_kernel, pair_tiles, lambda: (alpha() % 2, beta() * columns)),
        "same_spin",
        pair_tiles,
        near(ids),
        near(codes) if resident else codes.reshape(pair_tiles, part, strings),
        near(mixed),
        near(one),
        near(own_c),
        near(sibling),
        in_specs=[
            vmem,
            vmem if resident else pl.BlockSpec((None, part, strings), lambda i: (i, 0, 0)),
            tiled((part, chip, strings), 0),
            vmem,
            vmem,
            vmem,
        ],
        out_shape=(shape_of((pairs * columns, strings), BF16), shape_of((2 * chip, columns), BF16)),
        out_specs=(tiled((part * columns, strings), 0), vmem),
        scratch_shapes=[pltpu.VMEM((chip, columns), F32)],
    )
    messages = [message] + [send(message, "aa", 2 * k) for k in range(1, groups)]
    outs = call(
        functools.partial(mixed_kernel, pair_tiles, groups, peers, lambda: (alpha() // 2, alpha() % 2, beta())),
        "mixed",
        pair_tiles,
        near(mixed),
        near(hot),
        *[near(m) for m in messages],
        in_specs=[tiled((part, chip, strings), 0), tiled((part * columns, strings), 0)] + [vmem] * groups,
        out_shape=(shape_of((rows, columns), F32), shape_of((strings, columns), BF16))
        + tuple(shape_of((2 * rows, columns), BF16) for _ in range(peers - 1)),
        out_specs=(vmem,) * (peers + 1),
        scratch_shapes=[
            pltpu.VMEM((strings, columns), BF16),
            pltpu.VMEM((rows, part * columns), BF16),
            pltpu.VMEM((rows, strings), F32),
        ],
    )
    own, gathered = outs[:2]
    arrived = [send(m, "ba", k + 1) for k, m in enumerate(outs[2:])]
    return call(
        functools.partial(final_kernel, peers, lambda: (alpha() % 2, beta())),
        "final",
        1,
        near(alive),
        near(own),
        near(gathered),
        near(message),
        *[near(m) for m in arrived],
        in_specs=[vmem] * (3 + peers),
        out_shape=jax.ShapeDtypeStruct((rows, columns), BF16),
        out_specs=vmem,
    )


def solution(mesh):
    placed = (P("aa", "ba"), P(), P(), P(), P(), P())
    sizes = (mesh.shape["aa"], mesh.shape["ba"])
    return jax.shard_map(
        functools.partial(per_device, sizes), mesh=mesh, in_specs=placed, out_specs=P("aa", "ba"), check_vma=False
    )
```

time: 31.2 us -> 25.1 us (0.80)
  local copies, waits for them, and re-layouts: 3.5 us -> 0 us
  other arithmetic: 1.33 us -> 0 us
  Pallas kernels: 7.24 us -> 6.22 us
    unnamed x12 -> x0, local copies, waits for them, and re-layouts: 3.5 us -> none
    select_n x1 -> x0, other arithmetic: 1.33 us -> none  [per_device(): high = jnp.where(first, sibling, amplitudes)]
    pallas_call x4, Pallas kernels: 7.24 us -> 6.22 us  [call(): pl.pallas_call(body, name=name, compiler_params=params, **keys)(*args)]
  transfers between devices with their start and end apart: 7 -> 7, of which waited for: 5 -> 5; matrix products, arithmetic and copies ran while one was open for 0% -> 0% of each run, Pallas kernels for 7% -> 10%
where the time goes in v2:
time: 25.1 us; the launch traced here: 24.9 us
  waiting for transfers between devices  9.63 us (38%)
  starting transfers between devices  9.06 us (36%)
  Pallas kernels  6.22 us (25%)
    ppermute x7, waiting for transfers between devices, send(): lax.ppermute(value, axis, [(i, i ^ mask) for i in range(lax.axis_size(axi...  9.63 us
    ppermute x7, starting transfers between devices, send(): lax.ppermute(value, axis, [(i, i ^ mask) for i in range(lax.axis_size(axi...  9.06 us
    pallas_call x4, Pallas kernels, call(): pl.pallas_call(body, name=name, compiler_params=params, **keys)(*args)  6.22 us
  transfers between devices with their start and end apart: 7, of which 5 were waited for; matrix products, arithmetic and copies ran while one was open for 0% of the time, Pallas kernels for 10%

profile of v2, /device:TPU:0, one launch (start us, length us, event | category | flops | bytes accessed | tf_op | source)
XLA Modules:
  0.0 24.9 jit_solution(15612537015872140310)
XLA Ops:
  0.0 0.5 %collective-permute-start = (bf16[64,128]{1,0:T(8,128)(2,1)}, bf16[64,128]{1,0:T(8,128)(2,1)S(1)}, u32[]{:S(2)}, u32[]{:S(2)}) collective-permute-start(bf16[64,128]{1,0:T(8,128)(2,1)} %amplitudes_hbm.1), channel_id=1, source_target_pairs={{0,4},{4,0},{8,12},{12,8},{16,20},{20,16},{24,28},{28,24},{1,5},{5... | collective-permute-start | bytes 49160 | tf_op jit(solution)/shard_map/ppermute | solution.py:221
  0.5 2.5 %mix.1 = (bf16[32,128,512]{2,1,0:T(8,128)(2,1)S(1)}, f32[128,512]{1,0:T(8,128)S(1)}, s32[32,512]{1,0:T(8,128)S(1)}, s32[128,128]{1,0:T(8,128)S(1)}, f32[64,128]{1,0:T(8,128)S(1)}, /*index=5*/bf16[64,128]{1,0:T(8,128)(2,1)S(1)}) custom-call(s32[32]{0:T(128)} %counts_hbm.1, s32[32]{0:T(128)} %irrep_hbm.1, s32[32,512]{1,0:T(8,128)} %code_hbm.1, ...), custom_call_target="tpu_custom_call" | custom-call | tf_op jit(solution)/shard_map/mix/pallas_call | solution.py:218
  3.0 0.0 collective-permute-done.sibling_ref
  3.0 1.4 %same_spin.1 = (bf16[4096,512]{1,0:T(8,128)(2,1)S(1)}, bf16[256,128]{1,0:T(8,128)(2,1)S(1)}) custom-call(s32[128,128]{1,0:T(8,128)S(1)} %get-tuple-element.20.ids_ref, s32[32,512]{1,0:T(8,128)S(1)} %get-tuple-element.21.code_ref, bf16[32,128,512]{2,1,0:T(8,128)(2,1)S(1)} %get-tuple-element.19.mixed_ref, f32[128,512]{1,0:T(8,128)S(1)} %get-tuple-element.22.one_ref, ...), custom_call_target="tpu_custom_call" | custom-call | tf_op jit(solution)/shard_map/same_spin/pallas_call | solution.py:218
  4.4 3.5 %collective-permute-start.3 = (bf16[256,128]{1,0:T(8,128)(2,1)S(1)}, bf16[256,128]{1,0:T(8,128)(2,1)S(1)}, u32[]{:S(2)}, u32[]{:S(2)}) collective-permute-start(bf16[256,128]{1,0:T(8,128)(2,1)S(1)} %get-tuple-element.25.refs_0_.message_ref), channel_id=1, source_target_pairs={{0,24},{4,28},{8,16},{12,20},{16,8},{20,12},{24,0},{28,4},{1,25},{... | collective-permute-start | bytes 196616 | tf_op jit(solution)/shard_map/ppermute | solution.py:221
  7.9 0.5 %collective-permute-start.2 = (bf16[256,128]{1,0:T(8,128)(2,1)S(1)}, bf16[256,128]{1,0:T(8,128)(2,1)S(1)}, u32[]{:S(2)}, u32[]{:S(2)}) collective-permute-start(bf16[256,128]{1,0:T(8,128)(2,1)S(1)} %get-tuple-element.25.refs_0_.message_ref), channel_id=1, source_target_pairs={{0,16},{4,20},{8,24},{12,28},{16,0},{20,4},{24,8},{28,12},{1,17},{... | collective-permute-start | bytes 196616 | tf_op jit(solution)/shard_map/ppermute | solution.py:221
  8.4 0.1 collective-permute-start.1
  8.5 2.1 %collective-permute-done.3.refs_3_ = bf16[256,128]{1,0:T(8,128)(2,1)S(1)} collective-permute-done((bf16[256,128]{1,0:T(8,128)(2,1)S(1)}, bf16[256,128]{1,0:T(8,128)(2,1)S(1)}, u32[]{:S(2)}, u32[]{:S(2)}) %collective-permute-start.3) | collective-permute-done | bytes 65568 | tf_op jit(solution)/shard_map/ppermute | solution.py:221
  10.7 1.5 %collective-permute-done.2.refs_2_ = bf16[256,128]{1,0:T(8,128)(2,1)S(1)} collective-permute-done((bf16[256,128]{1,0:T(8,128)(2,1)S(1)}, bf16[256,128]{1,0:T(8,128)(2,1)S(1)}, u32[]{:S(2)}, u32[]{:S(2)}) %collective-permute-start.2) | collective-permute-done | bytes 65568 | tf_op jit(solution)/shard_map/ppermute | solution.py:221
  12.2 0.5 %collective-permute-done.1.refs_1_ = bf16[256,128]{1,0:T(8,128)(2,1)S(1)} collective-permute-done((bf16[256,128]{1,0:T(8,128)(2,1)S(1)}, bf16[256,128]{1,0:T(8,128)(2,1)S(1)}, u32[]{:S(2)}, u32[]{:S(2)}) %collective-permute-start.1) | collective-permute-done | bytes 65568 | tf_op jit(solution)/shard_map/ppermute | solution.py:221
  12.7 1.5 %mixed.1 = (f32[64,128]{1,0:T(8,128)S(1)}, bf16[512,128]{1,0:T(8,128)(2,1)S(1)}, bf16[128,128]{1,0:T(8,128)(2,1)S(1)}, bf16[128,128]{1,0:T(8,128)(2,1)S(1)}, bf16[128,128]{1,0:T(8,128)(2,1)S(1)}) custom-call(bf16[32,128,512]{2,1,0:T(8,128)(2,1)S(1)} %get-tuple-element.19.mixed_ref, bf16[4096,512]{1,0:T(8,128)(2,1)S(1)} %get-tuple-element.24.hot_ref, ...), custom_call_target="tpu_custom_call" | custom-call | tf_op jit(solution)/shard_map/mixed/pallas_call | solution.py:218
  14.2 1.6 %collective-permute-start.4 = (bf16[128,128]{1,0:T(8,128)(2,1)S(1)}, bf16[128,128]{1,0:T(8,128)(2,1)S(1)}, u32[]{:S(2)}, u32[]{:S(2)}) collective-permute-start(bf16[128,128]{1,0:T(8,128)(2,1)S(1)} %get-tuple-element.28), channel_id=1, source_target_pairs={{0,1},{1,0},{2,3},{3,2},{4,5},{5,4},{6,7},{7,6},{8,9},{9,8},{10,11... | collective-permute-start | bytes 98312 | tf_op jit(solution)/shard_map/ppermute | solution.py:221
  15.9 2.6 %collective-permute-start.5 = (bf16[128,128]{1,0:T(8,128)(2,1)S(1)}, bf16[128,128]{1,0:T(8,128)(2,1)S(1)}, u32[]{:S(2)}, u32[]{:S(2)}) collective-permute-start(bf16[128,128]{1,0:T(8,128)(2,1)S(1)} %get-tuple-element.29), channel_id=1, source_target_pairs={{0,2},{1,3},{2,0},{3,1},{4,6},{5,7},{6,4},{7,5},{8,10},{9,11},{10,... | collective-permute-start | bytes 98312 | tf_op jit(solution)/shard_map/ppermute | solution.py:221
  18.5 0.2 collective-permute-start.6
  18.7 0.0 collective-permute-done.4.refs_0_
  18.7 2.3 %collective-permute-done.5.refs_1_ = bf16[128,128]{1,0:T(8,128)(2,1)S(1)} collective-permute-done((bf16[128,128]{1,0:T(8,128)(2,1)S(1)}, bf16[128,128]{1,0:T(8,128)(2,1)S(1)}, u32[]{:S(2)}, u32[]{:S(2)}) %collective-permute-start.5) | collective-permute-done | bytes 32800 | tf_op jit(solution)/shard_map/ppermute | solution.py:221
  20.9 3.2 %collective-permute-done.6.refs_2_ = bf16[128,128]{1,0:T(8,128)(2,1)S(1)} collective-permute-done((bf16[128,128]{1,0:T(8,128)(2,1)S(1)}, bf16[128,128]{1,0:T(8,128)(2,1)S(1)}, u32[]{:S(2)}, u32[]{:S(2)}) %collective-permute-start.6) | collective-permute-done | bytes 32800 | tf_op jit(solution)/shard_map/ppermute | solution.py:221
  24.2 0.8 %final.1 = bf16[64,128]{1,0:T(8,128)(2,1)} custom-call(f32[64,128]{1,0:T(8,128)S(1)} %get-tuple-element.18.alive_ref, f32[64,128]{1,0:T(8,128)S(1)} %get-tuple-element.26.own_ref, bf16[512,128]{1,0:T(8,128)(2,1)S(1)} %get-tuple-element.27.amplitudes_ref, bf16[256,128]{1,0:T(8,128)(2,1)S(1)} %get-tuple-element.25.refs_0_.message_ref, ...), custom_call_target="tpu_custom_call" | custom-call | tf_op jit(solution)/shard_map/final/pallas_call | solution.py:218
Async XLA Ops:
  0.0 3.0 %collective-permute-start = (bf16[64,128]{1,0:T(8,128)(2,1)}, bf16[64,128]{1,0:T(8,128)(2,1)S(1)}, u32[]{:S(2)}, u32[]{:S(2)}) collective-permute-start(bf16[64,128]{1,0:T(8,128)(2,1)} %amplitudes_hbm.1), channel_id=1, source_target_pairs={{0,4},{4,0},{8,12},{12,8},{16,20},{20,16},{24,28},{28,24},{1,5},{5... | collective-permute-start | bytes 49160 | tf_op jit(solution)/shard_map/ppermute | solution.py:221
  4.4 6.3 %collective-permute-start.3 = (bf16[256,128]{1,0:T(8,128)(2,1)S(1)}, bf16[256,128]{1,0:T(8,128)(2,1)S(1)}, u32[]{:S(2)}, u32[]{:S(2)}) collective-permute-start(bf16[256,128]{1,0:T(8,128)(2,1)S(1)} %get-tuple-element.25.refs_0_.message_ref), channel_id=1, source_target_pairs={{0,24},{4,28},{8,16},{12,20},{16,8},{20,12},{24,0},{28,4},{1,25},{... | collective-permute-start | bytes 196616 | tf_op jit(solution)/shard_map/ppermute | solution.py:221
  7.9 4.3 %collective-permute-start.2 = (bf16[256,128]{1,0:T(8,128)(2,1)S(1)}, bf16[256,128]{1,0:T(8,128)(2,1)S(1)}, u32[]{:S(2)}, u32[]{:S(2)}) collective-permute-start(bf16[256,128]{1,0:T(8,128)(2,1)S(1)} %get-tuple-element.25.refs_0_.message_ref), channel_id=1, source_target_pairs={{0,16},{4,20},{8,24},{12,28},{16,0},{20,4},{24,8},{28,12},{1,17},{... | collective-permute-start | bytes 196616 | tf_op jit(solution)/shard_map/ppermute | solution.py:221
  8.4 4.3 %collective-permute-start.1 = (bf16[256,128]{1,0:T(8,128)(2,1)S(1)}, bf16[256,128]{1,0:T(8,128)(2,1)S(1)}, u32[]{:S(2)}, u32[]{:S(2)}) collective-permute-start(bf16[256,128]{1,0:T(8,128)(2,1)S(1)} %get-tuple-element.25.refs_0_.message_ref), channel_id=1, source_target_pairs={{0,8},{4,12},{8,0},{12,4},{16,24},{20,28},{24,16},{28,20},{1,9},{5... | collective-permute-start | bytes 196616 | tf_op jit(solution)/shard_map/ppermute | solution.py:221
  14.2 4.5 %collective-permute-start.4 = (bf16[128,128]{1,0:T(8,128)(2,1)S(1)}, bf16[128,128]{1,0:T(8,128)(2,1)S(1)}, u32[]{:S(2)}, u32[]{:S(2)}) collective-permute-start(bf16[128,128]{1,0:T(8,128)(2,1)S(1)} %get-tuple-element.28), channel_id=1, source_target_pairs={{0,1},{1,0},{2,3},{3,2},{4,5},{5,4},{6,7},{7,6},{8,9},{9,8},{10,11... | collective-permute-start | bytes 98312 | tf_op jit(solution)/shard_map/ppermute | solution.py:221
  15.9 5.1 %collective-permute-start.5 = (bf16[128,128]{1,0:T(8,128)(2,1)S(1)}, bf16[128,128]{1,0:T(8,128)(2,1)S(1)}, u32[]{:S(2)}, u32[]{:S(2)}) collective-permute-start(bf16[128,128]{1,0:T(8,128)(2,1)S(1)} %get-tuple-element.29), channel_id=1, source_target_pairs={{0,2},{1,3},{2,0},{3,1},{4,6},{5,7},{6,4},{7,5},{8,10},{9,11},{10,... | collective-permute-start | bytes 98312 | tf_op jit(solution)/shard_map/ppermute | solution.py:221
  18.5 5.7 %collective-permute-start.6 = (bf16[128,128]{1,0:T(8,128)(2,1)S(1)}, bf16[128,128]{1,0:T(8,128)(2,1)S(1)}, u32[]{:S(2)}, u32[]{:S(2)}) collective-permute-start(bf16[128,128]{1,0:T(8,128)(2,1)S(1)} %get-tuple-element.30), channel_id=1, source_target_pairs={{0,3},{1,2},{2,1},{3,0},{4,7},{5,6},{6,5},{7,4},{8,11},{9,10},{10,... | collective-permute-start | bytes 98312 | tf_op jit(solution)/shard_map/ppermute | solution.py:221

commit v3 on v2

v3 whole, which is shorter than its diff:
```python
import functools

import jax
import jax.numpy as jnp
from jax import lax
from jax.experimental import pallas as pl
from jax.experimental.pallas import tpu as pltpu
from jax.sharding import PartitionSpec as P

BF16 = jnp.bfloat16
F32 = jnp.float32
I32 = jnp.int32
I16 = jnp.int16
RESIDENT = 8 * 2**20
VMEM_LIMIT = 48 * 2**20
NEAR_LIMIT = 16 * 2**20
SIDE_PIECES = 2


def iota(shape, dim):
    return lax.broadcasted_iota(I32, shape, dim)


def dot(x, y):
    return jnp.dot(x, y, preferred_element_type=F32)


def dot_nt(x, y):
    return lax.dot_general(x, y, (((1,), (1,)), ((), ())), preferred_element_type=F32)


def live_ids(counts_ref, first, shape, dim, cap):
    ids = iota(shape, dim)
    block = ids // cap
    count = jnp.zeros(shape, I32)
    for j in range(shape[dim] // cap):
        count = jnp.where(block == j, counts_ref[first // cap + j], count)
    return jnp.where(ids - block * cap < count, ids + first + 1, -1)


def sign_of(code):
    return jnp.where(code > 0, 1.0, -1.0).astype(F32)


def tables_kernel(cap, place, counts_hbm, irrep_hbm, code_hbm, integrals_hbm, gains_hbm, amplitudes_hbm, *refs):
    code_ref, live_ref, mixer_ref, alive_ref, amplitudes_ref = refs[:5]
    counts_ref, irrep_ref, integrals_ref, gains_ref, sems = refs[5:]
    pairs, strings = code_ref.shape
    rows, columns = amplitudes_ref.shape
    first_a, first_b = place()
    copies = [
        pltpu.make_async_copy(source, target, sems.at[i])
        for i, (source, target) in enumerate(
            (
                (irrep_hbm, irrep_ref),
                (integrals_hbm, integrals_ref),
                (gains_hbm, gains_ref),
                (counts_hbm, counts_ref),
                (code_hbm, code_ref),
                (amplitudes_hbm, amplitudes_ref),
            )
        )
    ]
    for copy in copies:
        copy.start()
    wide = pairs * 8
    spread_q = jnp.where(iota((wide, pairs), 0) // 8 == iota((wide, pairs), 1), 1.0, 0.0).astype(BF16)
    spread_p = jnp.where(iota((pairs, wide), 1) % pairs == iota((pairs, wide), 0), 1.0, 0.0).astype(BF16)
    for copy in copies:
        copy.wait()
    irrep_p = jnp.zeros((pairs, pairs), I32)
    irrep_q = jnp.zeros((pairs, pairs), I32)
    for p in range(pairs):
        irrep_p = jnp.where(iota((pairs, pairs), 0) == p, irrep_ref[p], irrep_p)
        irrep_q = jnp.where(iota((pairs, pairs), 1) == p, irrep_ref[p], irrep_q)
    weights = jnp.where(irrep_p == irrep_q, integrals_ref[...].astype(F32), 0.0).astype(BF16)
    left = jnp.concatenate(
        [dot_nt(spread_q, weights), jnp.broadcast_to(gains_ref[...].astype(F32), (8, pairs))], 0
    ).astype(BF16)
    mixer = dot(left, spread_p)
    same = iota(mixer.shape, 0) % 8 == iota(mixer.shape, 1) // pairs
    mixer_ref[...] = jnp.where(same, mixer, 0.0).astype(BF16)
    live_ref[...] = live_ids(counts_ref, 0, live_ref.shape, 0, cap)
    live_a = live_ids(counts_ref, first_a, (rows, columns), 0, cap)
    live_b = live_ids(counts_ref, first_b, (1, columns), 1, cap)
    alive_ref[...] = jnp.where((live_a > 0) & (live_b > 0), 1.0, 0.0)


def join_kernel(own_ref, sibling_ref, message_ref):
    rows = own_ref.shape[0]
    message_ref[:rows] = own_ref[...]
    message_ref[rows:] = sibling_ref[...]


def mix_kernel(columns_at, code_ref, live_ref, mixer_ref, after_ref, mixed_ref, one_ref):
    pairs, strings = code_ref.shape
    wide = pairs * 8
    ids = jnp.broadcast_to(jnp.transpose(live_ref[...])[:1], (pairs, strings)).astype(I16)
    zero = jnp.zeros(ids.shape, BF16)
    mixer = mixer_ref[...]
    code = columns_at(code_ref)
    size = jnp.abs(code)
    sign = sign_of(code)
    for base in range(0, code.shape[1], 16):
        halves = []
        for low in (base, base + 8):
            hot = jnp.concatenate(
                [
                    jnp.where(
                        jnp.broadcast_to(size[:, a : a + 1], ids.shape).astype(I16) == ids,
                        jnp.broadcast_to(sign[:, a : a + 1], ids.shape).astype(BF16),
                        zero,
                    )
                    for a in range(low, low + 8)
                ],
                0,
            )
            part = dot(mixer, hot)
            one_ref[pl.ds(low, 8), :] = part[wide:]
            halves.append(part[:wide].reshape(pairs, 8, strings))
        mixed_ref[:, pl.ds(base, 16), :] = jnp.concatenate(halves, 1).astype(BF16)


def hot_tile(code, ids):
    size = jnp.broadcast_to(jnp.abs(code), ids.shape).astype(I16)
    sign = jnp.broadcast_to(sign_of(code), ids.shape).astype(BF16)
    return jnp.where(size == ids, sign, jnp.zeros(ids.shape, BF16))


def row_ids(live_ref, first, rows, strings):
    return jnp.concatenate([live_ref[pl.ds(first, rows), :]] * (strings // 128), 1).astype(I16)


def hot_kernel(steps, place, live_ref, code_ref, mixed_ref, one_ref, hot_ref, block_ref, total_ref):
    pairs, strings = code_ref.shape
    rows, columns = block_ref.shape
    step = 0 if steps == 1 else pl.program_id(0)
    first = pl.multiple_of(place(), columns)
    ids = row_ids(live_ref, first, columns, strings)
    if steps > 1:

        @pl.when(step == 0)
        def _():
            total_ref[...] = jnp.zeros_like(total_ref)

    total = jnp.zeros((rows, columns), F32) if steps == 1 else total_ref[...]
    for q in range(pairs):
        hot = hot_tile(code_ref[q : q + 1, :], ids)
        hot_ref[pl.ds(q * columns, columns), :] = hot
        total = total + dot_nt(mixed_ref[q, :rows, :], hot)
    if steps > 1:
        total_ref[...] = total
    block_ref[...] = (one_ref[:rows, pl.ds(first, columns)] + 0.5 * total).astype(BF16)


def mixed_kernel(steps, groups, peers, place, mixed_ref, hot_ref, block_ref, *refs):
    arrived = refs[:groups]
    own_ref, amplitudes_ref = refs[groups : groups + 2]
    sent = refs[groups + 2 : groups + 1 + peers]
    line, total_ref = refs[groups + 1 + peers :]
    pairs, strings = mixed_ref.shape[0], mixed_ref.shape[2]
    rows, columns = own_ref.shape
    step = 0 if steps == 1 else pl.program_id(0)
    group, core, column = place()

    @pl.when(step == 0)
    def _():
        total_ref[...] = jnp.zeros_like(total_ref)
        for k in range(groups):
            first = (group ^ k) * 2
            at = pl.multiple_of((first + core) * rows, rows)
            amplitudes_ref[pl.ds(at, rows), :] = arrived[k][:rows]
            at = pl.multiple_of((first + 1 - core) * rows, rows)
            amplitudes_ref[pl.ds(at, rows), :] = arrived[k][rows:]

    amplitudes = amplitudes_ref[...]
    for q in range(pairs):
        part = dot(mixed_ref[q, :rows, :], amplitudes)
        line[:, pl.ds(q * columns, columns)] = part.astype(BF16)
    total_ref[...] += dot(line[...], hot_ref[...])

    @pl.when(step == steps - 1)
    def _():
        for k in range(peers):
            to = lax.rem(column + k, peers)
            part = total_ref[:, pl.ds(pl.multiple_of(to * columns, columns), columns)]
            if k == 0:
                own_ref[...] = part
            else:
                sent[k - 1][:rows] = part.astype(BF16)
                sent[k - 1][rows : 2 * rows] = arrived[0][:rows]
                sent[k - 1][2 * rows :] = block_ref[...]


def same_spin_kernel(steps, place, live_ref, code_ref, mixed_ref, one_ref, after_ref, *refs):
    pairs, both, strings = mixed_ref.shape
    side_refs, total_ref = refs[:-1], refs[-1]
    piece, columns = side_refs[0].shape
    half = piece * len(side_refs)
    step = 0 if steps == 1 else pl.program_id(0)
    at = pl.multiple_of(place() * half, half)
    tile = piece
    if steps > 1:

        @pl.when(step == 0)
        def _():
            total_ref[...] = jnp.zeros_like(total_ref)

    for first in range(0, half, tile):
        ids = row_ids(live_ref, at + first, tile, strings)
        total = jnp.zeros((tile, columns), F32) if steps == 1 else total_ref[pl.ds(first, tile), :]
        for q in range(pairs):
            total = total + dot_nt(hot_tile(code_ref[q : q + 1, :], ids), mixed_ref[q, both - columns :, :])
        if steps > 1:
            total_ref[pl.ds(first, tile), :] = total
        one = jnp.transpose(one_ref[both - columns :, pl.ds(at + first, tile)])
        side_refs[first // piece][...] = (one + 0.5 * total).astype(BF16)


def final_kernel(peers, place, alive_ref, own_ref, amplitudes_ref, message_ref, block_ref, *refs):
    out_ref, side_ref = refs[-2:]
    arrived, sides = refs[: peers - 1], refs[peers - 1 : -2]
    rows, columns = own_ref.shape
    piece = sides[0].shape[0]
    pieces = len(sides) // 2
    core, column = place()
    for i in range(pieces):
        side_ref[pl.ds(pl.multiple_of((core * pieces + i) * piece, piece), piece), :] = sides[i][...]
        at = pl.multiple_of(((1 - core) * pieces + i) * piece, piece)
        side_ref[pl.ds(at, piece), :] = sides[pieces + i][...]
    total = own_ref[...]
    left, right = [], []
    for k in range(peers):
        source = lax.rem(column + peers - k, peers)
        at = pl.multiple_of(source * columns, columns)
        if k == 0:
            left += [block_ref[...], message_ref[:rows]]
        else:
            left += [arrived[k - 1][2 * rows :], arrived[k - 1][rows : 2 * rows]]
            total = total + arrived[k - 1][:rows].astype(F32)
        right += [amplitudes_ref[pl.ds(at, columns), :], side_ref[pl.ds(at, columns), :]]
    total = total + dot(jnp.concatenate(left, 1), jnp.concatenate(right, 0))
    out_ref[...] = (total * alive_ref[...]).astype(BF16)


def per_device(sizes, amplitudes, code, counts, pair_irrep, integrals, one_body):
    rows, columns = amplitudes.shape
    pairs, strings = code.shape
    cap = strings // counts.shape[0]
    groups, peers = sizes[0] // 2, sizes[1]
    both = rows + columns
    resident = pairs * both * strings * 2 <= RESIDENT
    tile = both if resident else 128
    row_tiles = both // tile
    pair_tiles = 1 if resident else pairs // 4
    part = pairs // pair_tiles
    hbm = pl.BlockSpec(memory_space=pl.ANY)
    vmem = pl.BlockSpec(memory_space=pltpu.VMEM)

    def tiled(shape, dim):
        if resident:
            return vmem
        return pl.BlockSpec(shape, lambda i: tuple(i if d == dim else 0 for d in range(len(shape))))

    def shape_of(shape, dtype):
        return pltpu.VMEM(shape, dtype) if resident else jax.ShapeDtypeStruct(shape, dtype)

    def near(value):
        return pltpu.with_memory_space_constraint(value, pltpu.VMEM) if resident else value

    def far(value):
        return pltpu.with_memory_space_constraint(value, pltpu.HBM)

    def call(body, name, tiles, *args, flops=0, **keys):
        if tiles > 1:
            keys["grid"] = (tiles,)
        params = pltpu.CompilerParams(vmem_limit_bytes=NEAR_LIMIT if resident else VMEM_LIMIT)
        cost = pl.CostEstimate(flops=flops, bytes_accessed=0, transcendentals=0)
        return pl.pallas_call(body, name=name, compiler_params=params, cost_estimate=cost, **keys)(*args)

    def alpha():
        return lax.axis_index("aa")

    def beta():
        return lax.axis_index("ba")

    def over_alpha(value, mask):
        return lax.ppermute(value, "aa", [(i, i ^ mask) for i in range(sizes[0])])

    def over_beta(value, shift):
        return lax.ppermute(value, "ba", [(i, (i + shift) % peers) for i in range(peers)])

    def columns_at(code_ref):
        if resident:
            chip = code_ref[:, pl.ds(pl.multiple_of(alpha() // 2 * 2 * rows, 2 * rows), 2 * rows)]
            own = jnp.where(alpha() % 2 == 0, chip[:, :rows], chip[:, rows:])
            return jnp.concatenate([own, code_ref[:, pl.ds(pl.multiple_of(beta() * columns, columns), columns)]], 1)
        at = pl.program_id(0) * tile
        first = jnp.where(at < rows, alpha() * rows + at, beta() * columns + at - rows)
        return code_ref[:, pl.ds(pl.multiple_of(first, tile), tile)]

    sibling = over_alpha(amplitudes, 1)
    codes, live, mixer, alive, own_c = call(
        functools.partial(tables_kernel, cap, lambda: (alpha() * rows, beta() * columns)),
        "tables",
        1,
        far(counts),
        far(pair_irrep),
        far(code),
        far(integrals),
        far(one_body.reshape(1, pairs)),
        far(amplitudes),
        in_specs=[hbm] * 6,
        out_shape=(
            shape_of((pairs, strings), I32),
            shape_of((strings, 128), I32),
            shape_of((pairs * 8 + 8, pairs * 8), BF16),
            shape_of((rows, columns), F32),
            shape_of((rows, columns), BF16),
        ),
        out_specs=(vmem,) * 5,
        scratch_shapes=[
            pltpu.SMEM(counts.shape, I32),
            pltpu.SMEM(pair_irrep.shape, I32),
            pltpu.VMEM((pairs, pairs), BF16),
            pltpu.VMEM((1, pairs), BF16),
            pltpu.SemaphoreType.DMA((6,)),
        ],
    )
    message = call(
        join_kernel,
        "join",
        1,
        near(own_c),
        near(sibling),
        in_specs=[vmem] * 2,
        out_shape=shape_of((2 * rows, columns), BF16),
        out_specs=vmem,
    )
    messages = [message] + [over_alpha(message, 2 * k) for k in range(1, groups)]
    mixed, one = call(
        functools.partial(mix_kernel, columns_at),
        "mix",
        row_tiles,
        near(codes),
        near(live),
        near(mixer),
        near(message),
        flops=2 * both * pairs * pairs * 8 * strings,
        in_specs=[vmem] * 4,
        out_shape=(shape_of((pairs, both, strings), BF16), shape_of((both, strings), F32)),
        out_specs=(tiled((pairs, tile, strings), 1), tiled((tile, strings), 0)),
    )
    code_parts = near(codes) if resident else codes.reshape(pair_tiles, part, strings)
    code_spec = vmem if resident else pl.BlockSpec((None, part, strings), lambda i: (i, 0, 0))
    hot, block = call(
        functools.partial(hot_kernel, pair_tiles, lambda: beta() * columns),
        "hot",
        pair_tiles,
        near(live),
        code_parts,
        near(mixed),
        near(one),
        flops=2 * pairs * rows * columns * strings,
        in_specs=[vmem, code_spec, tiled((part, both, strings), 0), vmem],
        out_shape=(shape_of((pairs * columns, strings), BF16), shape_of((rows, columns), BF16)),
        out_specs=(tiled((part * columns, strings), 0), vmem),
        scratch_shapes=[pltpu.VMEM((rows, columns), F32)],
    )
    outs = call(
        functools.partial(mixed_kernel, pair_tiles, groups, peers, lambda: (alpha() // 2, alpha() % 2, beta())),
        "mixed",
        pair_tiles,
        near(mixed),
        near(hot),
        near(block),
        *[near(m) for m in messages],
        in_specs=[tiled((part, both, strings), 0), tiled((part * columns, strings), 0)] + [vmem] * (groups + 1),
        out_shape=(shape_of((rows, columns), F32), shape_of((strings, columns), BF16))
        + tuple(shape_of((3 * rows, columns), BF16) for _ in range(peers - 1)),
        out_specs=(vmem,) * (peers + 1),
        scratch_shapes=[pltpu.VMEM((rows, part * columns), BF16), pltpu.VMEM((rows, strings), F32)],
    )
    own, gathered = outs[:2]
    arrived = [over_beta(m, k + 1) for k, m in enumerate(outs[2:])]
    pieces = SIDE_PIECES
    sides = call(
        functools.partial(same_spin_kernel, pair_tiles, lambda: alpha() % 2),
        "same_spin",
        pair_tiles,
        near(live),
        code_parts,
        near(mixed),
        near(one),
        near(own),
        flops=2 * columns * pairs * strings * strings,
        in_specs=[vmem, code_spec, tiled((part, both, strings), 0)] + [vmem] * 2,
        out_shape=tuple(shape_of((strings // 2 // pieces, columns), BF16) for _ in range(pieces)),
        out_specs=(vmem,) * pieces,
        scratch_shapes=[pltpu.VMEM((strings // 2, columns), F32)],
    )
    sides = list(sides) + [over_alpha(side, 1) for side in sides]
    return call(
        functools.partial(final_kernel, peers, lambda: (alpha() % 2, beta())),
        "final",
        1,
        near(alive),
        near(own),
        near(gathered),
        near(message),
        near(block),
        *[near(m) for m in arrived],
        *[near(side) for side in sides],
        in_specs=[vmem] * (4 + peers + 2 * pieces),
        out_shape=jax.ShapeDtypeStruct((rows, columns), BF16),
        out_specs=vmem,
        scratch_shapes=[pltpu.VMEM((strings, columns), BF16)],
    )


def solution(mesh):
    placed = (P("aa", "ba"), P(), P(), P(), P(), P())
    sizes = (mesh.shape["aa"], mesh.shape["ba"])
    return jax.shard_map(
        functools.partial(per_device, sizes), mesh=mesh, in_specs=placed, out_specs=P("aa", "ba"), check_vma=False
    )
```

time: 25.1 us -> 22 us (0.88)
  waiting for transfers between devices: 9.63 us -> 0.88 us
  Pallas kernels: 6.22 us -> 9.74 us
  starting transfers between devices: 9.06 us -> 11.1 us
    ppermute x7 -> x9, waiting for transfers between devices: 9.63 us -> 0.88 us  [the longest x6 0.87 us: over_alpha(): return lax.ppermute(value, 'aa', [(i, i ^ mask) for i in range(sizes[0])])]
    pallas_call x4 -> x7, Pallas kernels: 6.22 us -> 9.74 us  [call(): pl.pallas_call(body, name=name, compiler_params=params, cost_estimate=cos...]
    ppermute x7 -> x9, starting transfers between devices: 9.06 us -> 11.1 us  [the longest x3 5.96 us: over_beta(): lax.ppermute(value, 'ba', [(i, (i + shift) % peers) for i in range(peers)])]
  transfers between devices with their start and end apart: 7 -> 9, of which waited for: 5 -> 2; matrix products, arithmetic and copies ran while one was open for 0% -> 0% of each run, Pallas kernels for 10% -> 34%
where the time goes in v3:
time: 22 us; the launch traced here: 21.8 us
  starting transfers between devices  11.1 us (50%)
  Pallas kernels  9.74 us (44%)
  waiting for transfers between devices  0.88 us (4%)
    pallas_call x7, Pallas kernels, call(): pl.pallas_call(body, name=name, compiler_params=params, cost_estimate=cos...  9.74 us
    ppermute x3, starting transfers between devices, over_beta(): lax.ppermute(value, 'ba', [(i, (i + shift) % peers) for i in range(peers)])  5.96 us
    ppermute x6, starting transfers between devices, over_alpha(): return lax.ppermute(value, 'aa', [(i, i ^ mask) for i in range(sizes[0])])  5.17 us
    ppermute x6, waiting for transfers between devices, over_alpha(): return lax.ppermute(value, 'aa', [(i, i ^ mask) for i in range(sizes[0])])  0.87 us
  transfers between devices with their start and end apart: 9, of which 2 were waited for; matrix products, arithmetic and copies ran while one was open for 0% of the time, Pallas kernels for 34%

profile of v3, /device:TPU:0, one launch (start us, length us, event | category | flops | bytes accessed | tf_op | source)
XLA Modules:
  0.0 21.8 jit_solution(4663087337415205064)
XLA Ops:
  0.0 0.5 %collective-permute-start = (bf16[64,128]{1,0:T(8,128)(2,1)}, bf16[64,128]{1,0:T(8,128)(2,1)S(1)}, u32[]{:S(2)}, u32[]{:S(2)}) collective-permute-start(bf16[64,128]{1,0:T(8,128)(2,1)} %amplitudes_hbm.1), channel_id=1, source_target_pairs={{0,4},{4,0},{8,12},{12,8},{16,20},{20,16},{24,28},{28,24},{1,5},{5... | collective-permute-start | bytes 49160 | tf_op jit(solution)/shard_map/ppermute | solution.py:288
  0.5 1.3 %tables.1 = (s32[32,512]{1,0:T(8,128)S(1)}, s32[512,128]{1,0:T(8,128)S(1)}, bf16[264,256]{1,0:T(8,128)(2,1)S(1)}, f32[64,128]{1,0:T(8,128)S(1)}, bf16[64,128]{1,0:T(8,128)(2,1)S(1)}) custom-call(s32[32]{0:T(128)} %counts_hbm.1, s32[32]{0:T(128)} %irrep_hbm.1, s32[32,512]{1,0:T(8,128)} %code_hbm.1, bf16[32,32]{1,0:T(8,128)(2,1)} %integrals_hbm.1, ...), custom_call_target="tpu_custom_call" | custom-call | tf_op jit(solution)/shard_map/tables/pallas_call | solution.py:279
  1.8 0.0 collective-permute-done.sibling_ref
  1.8 3.5 %collective-permute-start.3 = (bf16[128,128]{1,0:T(8,128)(2,1)S(1)}, bf16[128,128]{1,0:T(8,128)(2,1)S(1)}, u32[]{:S(2)}, u32[]{:S(2)}) collective-permute-start(bf16[128,128]{1,0:T(8,128)(2,1)S(1)} %join.1.after_ref.refs_0_.message_ref), channel_id=1, source_target_pairs={{0,24},{4,28},{8,16},{12,20},{16,8},{20,12},{24,0},{28,4},{1,25},{... | collective-permute-start | bytes 98312 | tf_op jit(solution)/shard_map/ppermute | solution.py:288
  5.3 0.5 %collective-permute-start.2 = (bf16[128,128]{1,0:T(8,128)(2,1)S(1)}, bf16[128,128]{1,0:T(8,128)(2,1)S(1)}, u32[]{:S(2)}, u32[]{:S(2)}) collective-permute-start(bf16[128,128]{1,0:T(8,128)(2,1)S(1)} %join.1.after_ref.refs_0_.message_ref), channel_id=1, source_target_pairs={{0,16},{4,20},{8,24},{12,28},{16,0},{20,4},{24,8},{28,12},{1,17},{... | collective-permute-start | bytes 98312 | tf_op jit(solution)/shard_map/ppermute | solution.py:288
  5.8 0.1 collective-permute-start.1
  6.0 2.2 %mix.1 = (bf16[32,192,512]{2,1,0:T(8,128)(2,1)S(1)}, f32[192,512]{1,0:T(8,128)S(1)}) custom-call(s32[32,512]{1,0:T(8,128)S(1)} %get-tuple-element.22.code_ref, s32[512,128]{1,0:T(8,128)S(1)} %get-tuple-element.23.live_ref, bf16[264,256]{1,0:T(8,128)(2,1)S(1)} %get-tuple-element.24.mixer_ref, bf16[128,128]{1,0:T(8,128)(2,1)S(1)} %join.1.after_ref.refs_0_.message_ref), custom_call_target="tpu_custom_call" | custom-call | flops 1610612736 | tf_op jit(solution)/shard_map/mix/pallas_call | solution.py:279
  8.2 1.6 %hot.1 = (bf16[4096,512]{1,0:T(8,128)(2,1)S(1)}, bf16[64,128]{1,0:T(8,128)(2,1)S(1)}) custom-call(s32[512,128]{1,0:T(8,128)S(1)} %get-tuple-element.23.live_ref, s32[32,512]{1,0:T(8,128)S(1)} %get-tuple-element.22.code_ref, bf16[32,192,512]{2,1,0:T(8,128)(2,1)S(1)} %get-tuple-element.26.mixed_ref, f32[192,512]{1,0:T(8,128)S(1)} %get-tuple-element.27.one_ref), custom_call_target="tpu_custom_call" | custom-call | flops 268435456 | tf_op jit(solution)/shard_map/hot/pallas_call | solution.py:279
  9.7 0.0 collective-permute-done.3.refs_3_
  9.8 0.0 collective-permute-done.2.refs_2_
  9.8 0.0 collective-permute-done.1.refs_1_
  9.8 1.5 %mixed.1 = (f32[64,128]{1,0:T(8,128)S(1)}, bf16[512,128]{1,0:T(8,128)(2,1)S(1)}, bf16[192,128]{1,0:T(8,128)(2,1)S(1)}, bf16[192,128]{1,0:T(8,128)(2,1)S(1)}, bf16[192,128]{1,0:T(8,128)(2,1)S(1)}) custom-call(bf16[32,192,512]{2,1,0:T(8,128)(2,1)S(1)} %get-tuple-element.26.mixed_ref, bf16[4096,512]{1,0:T(8,128)(2,1)S(1)} %get-tuple-element.28.hot_ref, ...), custom_call_target="tpu_custom_call" | custom-call | tf_op jit(solution)/shard_map/mixed/pallas_call | solution.py:279
  11.3 2.0 %collective-permute-start.4 = (bf16[192,128]{1,0:T(8,128)(2,1)S(1)}, bf16[192,128]{1,0:T(8,128)(2,1)S(1)}, u32[]{:S(2)}, u32[]{:S(2)}) collective-permute-start(bf16[192,128]{1,0:T(8,128)(2,1)S(1)} %get-tuple-element.32), channel_id=1, source_target_pairs={{0,1},{1,2},{2,3},{3,0},{4,5},{5,6},{6,7},{7,4},{8,9},{9,10},{10,1... | collective-permute-start | bytes 147464 | tf_op jit(solution)/shard_map/ppermute | solution.py:291
  13.3 2.6 %collective-permute-start.5 = (bf16[192,128]{1,0:T(8,128)(2,1)S(1)}, bf16[192,128]{1,0:T(8,128)(2,1)S(1)}, u32[]{:S(2)}, u32[]{:S(2)}) collective-permute-start(bf16[192,128]{1,0:T(8,128)(2,1)S(1)} %get-tuple-element.33), channel_id=1, source_target_pairs={{0,2},{1,3},{2,0},{3,1},{4,6},{5,7},{6,4},{7,5},{8,10},{9,11},{10,... | collective-permute-start | bytes 147464 | tf_op jit(solution)/shard_map/ppermute | solution.py:291
  15.9 1.3 %collective-permute-start.6 = (bf16[192,128]{1,0:T(8,128)(2,1)S(1)}, bf16[192,128]{1,0:T(8,128)(2,1)S(1)}, u32[]{:S(2)}, u32[]{:S(2)}) collective-permute-start(bf16[192,128]{1,0:T(8,128)(2,1)S(1)} %get-tuple-element.34), channel_id=1, source_target_pairs={{0,3},{1,0},{2,1},{3,2},{4,7},{5,4},{6,5},{7,6},{8,11},{9,8},{10,9... | collective-permute-start | bytes 147464 | tf_op jit(solution)/shard_map/ppermute | solution.py:291
  17.2 2.3 %same_spin.1 = (bf16[128,128]{1,0:T(8,128)(2,1)S(1)}, bf16[128,128]{1,0:T(8,128)(2,1)S(1)}) custom-call(s32[512,128]{1,0:T(8,128)S(1)} %get-tuple-element.23.live_ref, s32[32,512]{1,0:T(8,128)S(1)} %get-tuple-element.22.code_ref, bf16[32,192,512]{2,1,0:T(8,128)(2,1)S(1)} %get-tuple-element.26.mixed_ref, f32[192,512]{1,0:T(8,128)S(1)} %get-tuple-element.27.one_ref, ...), custom_call_target="tpu_custom_call" | custom-call | flops 2147483648 | tf_op jit(solution)/shard_map/same_spin/pallas_call | solution.py:279
  19.6 0.1 collective-permute-start.7
  19.7 0.5 %collective-permute-start.8 = (bf16[128,128]{1,0:T(8,128)(2,1)S(1)}, bf16[128,128]{1,0:T(8,128)(2,1)S(1)}, u32[]{:S(2)}, u32[]{:S(2)}) collective-permute-start(bf16[128,128]{1,0:T(8,128)(2,1)S(1)} %get-tuple-element.36.refs_4_), channel_id=1, source_target_pairs={{0,4},{4,0},{8,12},{12,8},{16,20},{20,16},{24,28},{28,24},{1,5},{5... | collective-permute-start | bytes 98312 | tf_op jit(solution)/shard_map/ppermute | solution.py:288
  20.2 0.7 %collective-permute-done.7.refs_5_ = bf16[128,128]{1,0:T(8,128)(2,1)S(1)} collective-permute-done((bf16[128,128]{1,0:T(8,128)(2,1)S(1)}, bf16[128,128]{1,0:T(8,128)(2,1)S(1)}, u32[]{:S(2)}, u32[]{:S(2)}) %collective-permute-start.7) | collective-permute-done | bytes 32800 | tf_op jit(solution)/shard_map/ppermute | solution.py:288
  20.9 0.2 collective-permute-done.8.refs_6_
  21.0 0.0 collective-permute-done.4.refs_0_
  21.0 0.0 collective-permute-done.5.refs_1_
  21.0 0.0 collective-permute-done.6.refs_2_
  21.0 0.8 %final.1 = bf16[64,128]{1,0:T(8,128)(2,1)} custom-call(f32[64,128]{1,0:T(8,128)S(1)} %get-tuple-element.21.alive_ref, f32[64,128]{1,0:T(8,128)S(1)} %get-tuple-element.30.after_ref.own_ref, bf16[512,128]{1,0:T(8,128)(2,1)S(1)} %get-tuple-element.31.amplitudes_ref, bf16[128,128]{1,0:T(8,128)(2,1)S(1)} %join.1.after_ref.refs_0_.message_ref, ...), custom_call_target="tpu_custom_call" | custom-call | tf_op jit(solution)/shard_map/final/pallas_call | solution.py:279
  (1 shorter events, 0.0 us)
Async XLA Ops:
  0.0 1.8 %collective-permute-start = (bf16[64,128]{1,0:T(8,128)(2,1)}, bf16[64,128]{1,0:T(8,128)(2,1)S(1)}, u32[]{:S(2)}, u32[]{:S(2)}) collective-permute-start(bf16[64,128]{1,0:T(8,128)(2,1)} %amplitudes_hbm.1), channel_id=1, source_target_pairs={{0,4},{4,0},{8,12},{12,8},{16,20},{20,16},{24,28},{28,24},{1,5},{5... | collective-permute-start | bytes 49160 | tf_op jit(solution)/shard_map/ppermute | solution.py:288
  1.8 7.9 %collective-permute-start.3 = (bf16[128,128]{1,0:T(8,128)(2,1)S(1)}, bf16[128,128]{1,0:T(8,128)(2,1)S(1)}, u32[]{:S(2)}, u32[]{:S(2)}) collective-permute-start(bf16[128,128]{1,0:T(8,128)(2,1)S(1)} %join.1.after_ref.refs_0_.message_ref), channel_id=1, source_target_pairs={{0,24},{4,28},{8,16},{12,20},{16,8},{20,12},{24,0},{28,4},{1,25},{... | collective-permute-start | bytes 98312 | tf_op jit(solution)/shard_map/ppermute | solution.py:288
  5.3 4.4 %collective-permute-start.2 = (bf16[128,128]{1,0:T(8,128)(2,1)S(1)}, bf16[128,128]{1,0:T(8,128)(2,1)S(1)}, u32[]{:S(2)}, u32[]{:S(2)}) collective-permute-start(bf16[128,128]{1,0:T(8,128)(2,1)S(1)} %join.1.after_ref.refs_0_.message_ref), channel_id=1, source_target_pairs={{0,16},{4,20},{8,24},{12,28},{16,0},{20,4},{24,8},{28,12},{1,17},{... | collective-permute-start | bytes 98312 | tf_op jit(solution)/shard_map/ppermute | solution.py:288
  5.8 3.9 %collective-permute-start.1 = (bf16[128,128]{1,0:T(8,128)(2,1)S(1)}, bf16[128,128]{1,0:T(8,128)(2,1)S(1)}, u32[]{:S(2)}, u32[]{:S(2)}) collective-permute-start(bf16[128,128]{1,0:T(8,128)(2,1)S(1)} %join.1.after_ref.refs_0_.message_ref), channel_id=1, source_target_pairs={{0,8},{4,12},{8,0},{12,4},{16,24},{20,28},{24,16},{28,20},{1,9},{5... | collective-permute-start | bytes 98312 | tf_op jit(solution)/shard_map/ppermute | solution.py:288
  11.3 9.7 %collective-permute-start.4 = (bf16[192,128]{1,0:T(8,128)(2,1)S(1)}, bf16[192,128]{1,0:T(8,128)(2,1)S(1)}, u32[]{:S(2)}, u32[]{:S(2)}) collective-permute-start(bf16[192,128]{1,0:T(8,128)(2,1)S(1)} %get-tuple-element.32), channel_id=1, source_target_pairs={{0,1},{1,2},{2,3},{3,0},{4,5},{5,6},{6,7},{7,4},{8,9},{9,10},{10,1... | collective-permute-start | bytes 147464 | tf_op jit(solution)/shard_map/ppermute | solution.py:291
  13.3 7.7 %collective-permute-start.5 = (bf16[192,128]{1,0:T(8,128)(2,1)S(1)}, bf16[192,128]{1,0:T(8,128)(2,1)S(1)}, u32[]{:S(2)}, u32[]{:S(2)}) collective-permute-start(bf16[192,128]{1,0:T(8,128)(2,1)S(1)} %get-tuple-element.33), channel_id=1, source_target_pairs={{0,2},{1,3},{2,0},{3,1},{4,6},{5,7},{6,4},{7,5},{8,10},{9,11},{10,... | collective-permute-start | bytes 147464 | tf_op jit(solution)/shard_map/ppermute | solution.py:291
  15.9 5.1 %collective-permute-start.6 = (bf16[192,128]{1,0:T(8,128)(2,1)S(1)}, bf16[192,128]{1,0:T(8,128)(2,1)S(1)}, u32[]{:S(2)}, u32[]{:S(2)}) collective-permute-start(bf16[192,128]{1,0:T(8,128)(2,1)S(1)} %get-tuple-element.34), channel_id=1, source_target_pairs={{0,3},{1,0},{2,1},{3,2},{4,7},{5,4},{6,5},{7,6},{8,11},{9,8},{10,9... | collective-permute-start | bytes 147464 | tf_op jit(solution)/shard_map/ppermute | solution.py:291
  19.6 1.3 %collective-permute-start.7 = (bf16[128,128]{1,0:T(8,128)(2,1)S(1)}, bf16[128,128]{1,0:T(8,128)(2,1)S(1)}, u32[]{:S(2)}, u32[]{:S(2)}) collective-permute-start(bf16[128,128]{1,0:T(8,128)(2,1)S(1)} %get-tuple-element.35.refs_3_), channel_id=1, source_target_pairs={{0,4},{4,0},{8,12},{12,8},{16,20},{20,16},{24,28},{28,24},{1,5},{5... | collective-permute-start | bytes 98312 | tf_op jit(solution)/shard_map/ppermute | solution.py:288
  19.7 1.4 %collective-permute-start.8 = (bf16[128,128]{1,0:T(8,128)(2,1)S(1)}, bf16[128,128]{1,0:T(8,128)(2,1)S(1)}, u32[]{:S(2)}, u32[]{:S(2)}) collective-permute-start(bf16[128,128]{1,0:T(8,128)(2,1)S(1)} %get-tuple-element.36.refs_4_), channel_id=1, source_target_pairs={{0,4},{4,0},{8,12},{12,8},{16,20},{20,16},{24,28},{28,24},{1,5},{5... | collective-permute-start | bytes 98312 | tf_op jit(solution)/shard_map/ppermute | solution.py:288

commit v4 on v3

--- a/solution.py
+++ b/solution.py
@@ -101,16 +101,17 @@
     code = columns_at(code_ref)
     size = jnp.abs(code)
     sign = sign_of(code)
+
+    def along(table, at, dtype):
+        tile = jnp.broadcast_to(table[:, at : at + 1], (pairs, 128)).astype(dtype)
+        return jnp.concatenate([tile] * (strings // 128), 1)
+
     for base in range(0, code.shape[1], 16):
         halves = []
         for low in (base, base + 8):
             hot = jnp.concatenate(
                 [
-                    jnp.where(
-                        jnp.broadcast_to(size[:, a : a + 1], ids.shape).astype(I16) == ids,
-                        jnp.broadcast_to(sign[:, a : a + 1], ids.shape).astype(BF16),
-                        zero,
-                    )
+                    jnp.where(along(size, a, I16) == ids, along(sign, a, BF16), zero)
                     for a in range(low, low + 8)
                 ],
                 0,
@@ -122,8 +123,11 @@
 
 
 def hot_tile(code, ids):
-    size = jnp.broadcast_to(jnp.abs(code), ids.shape).astype(I16)
-    sign = jnp.broadcast_to(sign_of(code), ids.shape).astype(BF16)
+    rows, strings = ids.shape
+    size = jnp.broadcast_to(jnp.abs(code), (16, strings)).astype(I16)
+    sign = jnp.broadcast_to(sign_of(code), (16, strings)).astype(BF16)
+    size = jnp.concatenate([size] * (rows // 16), 0)
+    sign = jnp.concatenate([sign] * (rows // 16), 0)
     return jnp.where(size == ids, sign, jnp.zeros(ids.shape, BF16))
 
 
@@ -143,20 +147,20 @@
         def _():
             total_ref[...] = jnp.zeros_like(total_ref)
 
-    total = jnp.zeros((rows, columns), F32) if steps == 1 else total_ref[...]
+    total = jnp.zeros((columns, rows), F32) if steps == 1 else total_ref[...]
     for q in range(pairs):
         hot = hot_tile(code_ref[q : q + 1, :], ids)
         hot_ref[pl.ds(q * columns, columns), :] = hot
-        total = total + dot_nt(mixed_ref[q, :rows, :], hot)
+        total = total + dot_nt(hot, mixed_ref[q, :rows, :])
     if steps > 1:
         total_ref[...] = total
-    block_ref[...] = (one_ref[:rows, pl.ds(first, columns)] + 0.5 * total).astype(BF16)
+    block_ref[...] = (one_ref[:rows, pl.ds(first, columns)] + 0.5 * jnp.transpose(total)).astype(BF16)
 
 
 def mixed_kernel(steps, groups, peers, place, mixed_ref, hot_ref, block_ref, *refs):
     arrived = refs[:groups]
     own_ref, amplitudes_ref = refs[groups : groups + 2]
-    sent = refs[groups + 2 : groups + 1 + peers]
+    sent = refs[groups + 2 : groups + 1 + peers][::-1]
     line, total_ref = refs[groups + 1 + peers :]
     pairs, strings = mixed_ref.shape[0], mixed_ref.shape[2]
     rows, columns = own_ref.shape
@@ -182,8 +186,7 @@
     @pl.when(step == steps - 1)
     def _():
         for k in range(peers):
-            to = lax.rem(column + k, peers)
-            part = total_ref[:, pl.ds(pl.multiple_of(to * columns, columns), columns)]
+            part = total_ref[:, pl.ds(pl.multiple_of((column ^ k) * columns, columns), columns)]
             if k == 0:
                 own_ref[...] = part
             else:
@@ -219,7 +222,7 @@
 
 def final_kernel(peers, place, alive_ref, own_ref, amplitudes_ref, message_ref, block_ref, *refs):
     out_ref, side_ref = refs[-2:]
-    arrived, sides = refs[: peers - 1], refs[peers - 1 : -2]
+    arrived, sides = refs[: peers - 1][::-1], refs[peers - 1 : -2]
     rows, columns = own_ref.shape
     piece = sides[0].shape[0]
     pieces = len(sides) // 2
@@ -231,8 +234,7 @@
     total = own_ref[...]
     left, right = [], []
     for k in range(peers):
-        source = lax.rem(column + peers - k, peers)
-        at = pl.multiple_of(source * columns, columns)
+        at = pl.multiple_of((column ^ k) * columns, columns)
         if k == 0:
             left += [block_ref[...], message_ref[:rows]]
         else:
@@ -287,8 +289,8 @@
     def over_alpha(value, mask):
         return lax.ppermute(value, "aa", [(i, i ^ mask) for i in range(sizes[0])])
 
-    def over_beta(value, shift):
-        return lax.ppermute(value, "ba", [(i, (i + shift) % peers) for i in range(peers)])
+    def over_beta(value, mask):
+        return lax.ppermute(value, "ba", [(i, i ^ mask) for i in range(peers)])
 
     def columns_at(code_ref):
         if resident:
@@ -365,7 +367,7 @@
         in_specs=[vmem, code_spec, tiled((part, both, strings), 0), vmem],
         out_shape=(shape_of((pairs * columns, strings), BF16), shape_of((rows, columns), BF16)),
         out_specs=(tiled((part * columns, strings), 0), vmem),
-        scratch_shapes=[pltpu.VMEM((rows, columns), F32)],
+        scratch_shapes=[pltpu.VMEM((columns, rows), F32)],
     )
     outs = call(
         functools.partial(mixed_kernel, pair_tiles, groups, peers, lambda: (alpha() // 2, alpha() % 2, beta())),
@@ -382,7 +384,7 @@
         scratch_shapes=[pltpu.VMEM((rows, part * columns), BF16), pltpu.VMEM((rows, strings), F32)],
     )
     own, gathered = outs[:2]
-    arrived = [over_beta(m, k + 1) for k, m in enumerate(outs[2:])]
+    arrived = [over_beta(m, k) for k, m in zip(range(peers - 1, 0, -1), outs[2:])]
     pieces = SIDE_PIECES
     sides = call(
         functools.partial(same_spin_kernel, pair_tiles, lambda: alpha() % 2),

time: 22 us -> 21 us (0.955)
  starting transfers between devices: 11.1 us -> 9.66 us
  waiting for transfers between devices: 0.88 us -> 1.7 us
  Pallas kernels: 9.74 us -> 9.43 us
    ppermute x3, starting transfers between devices: 5.96 us -> 4.49 us  [over_beta(): return lax.ppermute(value, 'ba', [(i, i ^ mask) for i in range(peers)])]
    ppermute x3, waiting for transfers between devices: 0.01 us -> 0.59 us  [over_beta(): return lax.ppermute(value, 'ba', [(i, i ^ mask) for i in range(peers)])]
    pallas_call x7, Pallas kernels: 9.74 us -> 9.43 us  [call(): pl.pallas_call(body, name=name, compiler_params=params, cost_estimate=cos...]
    ppermute x6, waiting for transfers between devices: 0.87 us -> 1.11 us  [over_alpha(): return lax.ppermute(value, 'aa', [(i, i ^ mask) for i in range(sizes[0])])]
  transfers between devices with their start and end apart: 9 -> 9, of which waited for: 2 -> 4; matrix products, arithmetic and copies ran while one was open for 0% -> 0% of each run, Pallas kernels for 34% -> 34%
where the time goes in v4:
time: 21 us; the launch traced here: 20.9 us
  starting transfers between devices  9.66 us (46%)
  Pallas kernels  9.43 us (45%)
  waiting for transfers between devices  1.7 us (8%)
    pallas_call x7, Pallas kernels, call(): pl.pallas_call(body, name=name, compiler_params=params, cost_estimate=cos...  9.43 us
    ppermute x6, starting transfers between devices, over_alpha(): return lax.ppermute(value, 'aa', [(i, i ^ mask) for i in range(sizes[0])])  5.17 us
    ppermute x3, starting transfers between devices, over_beta(): return lax.ppermute(value, 'ba', [(i, i ^ mask) for i in range(peers)])  4.49 us
    ppermute x6, waiting for transfers between devices, over_alpha(): return lax.ppermute(value, 'aa', [(i, i ^ mask) for i in range(sizes[0])])  1.11 us
    ppermute x3, waiting for transfers between devices, over_beta(): return lax.ppermute(value, 'ba', [(i, i ^ mask) for i in range(peers)])  0.59 us
  transfers between devices with their start and end apart: 9, of which 4 were waited for; matrix products, arithmetic and copies ran while one was open for 0% of the time, Pallas kernels for 34%

profile of v4, /device:TPU:0, one launch (start us, length us, event | category | flops | bytes accessed | tf_op | source)
XLA Modules:
  0.0 20.9 jit_solution(2500467714575809520)
XLA Ops:
  0.0 0.5 %collective-permute-start = (bf16[64,128]{1,0:T(8,128)(2,1)}, bf16[64,128]{1,0:T(8,128)(2,1)S(1)}, u32[]{:S(2)}, u32[]{:S(2)}) collective-permute-start(bf16[64,128]{1,0:T(8,128)(2,1)} %amplitudes_hbm.1), channel_id=1, source_target_pairs={{0,4},{4,0},{8,12},{12,8},{16,20},{20,16},{24,28},{28,24},{1,5},{5... | collective-permute-start | bytes 49160 | tf_op jit(solution)/shard_map/ppermute | solution.py:290
  0.5 1.3 %tables.1 = (s32[32,512]{1,0:T(8,128)S(1)}, s32[512,128]{1,0:T(8,128)S(1)}, bf16[264,256]{1,0:T(8,128)(2,1)S(1)}, f32[64,128]{1,0:T(8,128)S(1)}, bf16[64,128]{1,0:T(8,128)(2,1)S(1)}) custom-call(s32[32]{0:T(128)} %counts_hbm.1, s32[32]{0:T(128)} %irrep_hbm.1, s32[32,512]{1,0:T(8,128)} %code_hbm.1, bf16[32,32]{1,0:T(8,128)(2,1)} %integrals_hbm.1, ...), custom_call_target="tpu_custom_call" | custom-call | tf_op jit(solution)/shard_map/tables/pallas_call | solution.py:281
  1.8 0.0 collective-permute-done.sibling_ref
  1.8 3.5 %collective-permute-start.3 = (bf16[128,128]{1,0:T(8,128)(2,1)S(1)}, bf16[128,128]{1,0:T(8,128)(2,1)S(1)}, u32[]{:S(2)}, u32[]{:S(2)}) collective-permute-start(bf16[128,128]{1,0:T(8,128)(2,1)S(1)} %join.1.after_ref.refs_0_.message_ref), channel_id=1, source_target_pairs={{0,24},{4,28},{8,16},{12,20},{16,8},{20,12},{24,0},{28,4},{1,25},{... | collective-permute-start | bytes 98312 | tf_op jit(solution)/shard_map/ppermute | solution.py:290
  5.3 0.5 %collective-permute-start.2 = (bf16[128,128]{1,0:T(8,128)(2,1)S(1)}, bf16[128,128]{1,0:T(8,128)(2,1)S(1)}, u32[]{:S(2)}, u32[]{:S(2)}) collective-permute-start(bf16[128,128]{1,0:T(8,128)(2,1)S(1)} %join.1.after_ref.refs_0_.message_ref), channel_id=1, source_target_pairs={{0,16},{4,20},{8,24},{12,28},{16,0},{20,4},{24,8},{28,12},{1,17},{... | collective-permute-start | bytes 98312 | tf_op jit(solution)/shard_map/ppermute | solution.py:290
  5.8 0.1 collective-permute-start.1
  6.0 2.2 %mix.1 = (bf16[32,192,512]{2,1,0:T(8,128)(2,1)S(1)}, f32[192,512]{1,0:T(8,128)S(1)}) custom-call(s32[32,512]{1,0:T(8,128)S(1)} %get-tuple-element.22.code_ref, s32[512,128]{1,0:T(8,128)S(1)} %get-tuple-element.23.live_ref, bf16[264,256]{1,0:T(8,128)(2,1)S(1)} %get-tuple-element.24.mixer_ref, bf16[128,128]{1,0:T(8,128)(2,1)S(1)} %join.1.after_ref.refs_0_.message_ref), custom_call_target="tpu_custom_call" | custom-call | flops 1610612736 | tf_op jit(solution)/shard_map/mix/pallas_call | solution.py:281
  8.2 1.3 %hot.1 = (bf16[4096,512]{1,0:T(8,128)(2,1)S(1)}, bf16[64,128]{1,0:T(8,128)(2,1)S(1)}) custom-call(s32[512,128]{1,0:T(8,128)S(1)} %get-tuple-element.23.live_ref, s32[32,512]{1,0:T(8,128)S(1)} %get-tuple-element.22.code_ref, bf16[32,192,512]{2,1,0:T(8,128)(2,1)S(1)} %get-tuple-element.26.mixed_ref, f32[192,512]{1,0:T(8,128)S(1)} %get-tuple-element.27.one_ref), custom_call_target="tpu_custom_call" | custom-call | flops 268435456 | tf_op jit(solution)/shard_map/hot/pallas_call | solution.py:281
  9.5 0.0 collective-permute-done.3.refs_3_
  9.5 0.0 collective-permute-done.2.refs_2_
  9.5 0.2 %collective-permute-done.1.refs_1_ = bf16[128,128]{1,0:T(8,128)(2,1)S(1)} collective-permute-done((bf16[128,128]{1,0:T(8,128)(2,1)S(1)}, bf16[128,128]{1,0:T(8,128)(2,1)S(1)}, u32[]{:S(2)}, u32[]{:S(2)}) %collective-permute-start.1) | collective-permute-done | bytes 32800 | tf_op jit(solution)/shard_map/ppermute | solution.py:290
  9.7 1.5 %mixed.1 = (f32[64,128]{1,0:T(8,128)S(1)}, bf16[512,128]{1,0:T(8,128)(2,1)S(1)}, bf16[192,128]{1,0:T(8,128)(2,1)S(1)}, bf16[192,128]{1,0:T(8,128)(2,1)S(1)}, bf16[192,128]{1,0:T(8,128)(2,1)S(1)}) custom-call(bf16[32,192,512]{2,1,0:T(8,128)(2,1)S(1)} %get-tuple-element.26.mixed_ref, bf16[4096,512]{1,0:T(8,128)(2,1)S(1)} %get-tuple-element.28.hot_ref, ...), custom_call_target="tpu_custom_call" | custom-call | tf_op jit(solution)/shard_map/mixed/pallas_call | solution.py:281
  11.2 3.9 %collective-permute-start.4 = (bf16[192,128]{1,0:T(8,128)(2,1)S(1)}, bf16[192,128]{1,0:T(8,128)(2,1)S(1)}, u32[]{:S(2)}, u32[]{:S(2)}) collective-permute-start(bf16[192,128]{1,0:T(8,128)(2,1)S(1)} %get-tuple-element.32), channel_id=1, source_target_pairs={{0,3},{1,2},{2,1},{3,0},{4,7},{5,6},{6,5},{7,4},{8,11},{9,10},{10,... | collective-permute-start | bytes 147464 | tf_op jit(solution)/shard_map/ppermute | solution.py:293
  15.1 0.0 collective-permute-start.5
  15.1 0.6 %collective-permute-start.6 = (bf16[192,128]{1,0:T(8,128)(2,1)S(1)}, bf16[192,128]{1,0:T(8,128)(2,1)S(1)}, u32[]{:S(2)}, u32[]{:S(2)}) collective-permute-start(bf16[192,128]{1,0:T(8,128)(2,1)S(1)} %get-tuple-element.34), channel_id=1, source_target_pairs={{0,1},{1,0},{2,3},{3,2},{4,5},{5,4},{6,7},{7,6},{8,9},{9,8},{10,11... | collective-permute-start | bytes 147464 | tf_op jit(solution)/shard_map/ppermute | solution.py:293
  15.7 2.3 %same_spin.1 = (bf16[128,128]{1,0:T(8,128)(2,1)S(1)}, bf16[128,128]{1,0:T(8,128)(2,1)S(1)}) custom-call(s32[512,128]{1,0:T(8,128)S(1)} %get-tuple-element.23.live_ref, s32[32,512]{1,0:T(8,128)S(1)} %get-tuple-element.22.code_ref, bf16[32,192,512]{2,1,0:T(8,128)(2,1)S(1)} %get-tuple-element.26.mixed_ref, f32[192,512]{1,0:T(8,128)S(1)} %get-tuple-element.27.one_ref, ...), custom_call_target="tpu_custom_call" | custom-call | flops 2147483648 | tf_op jit(solution)/shard_map/same_spin/pallas_call | solution.py:281
  18.0 0.1 collective-permute-start.7
  18.1 0.5 %collective-permute-start.8 = (bf16[128,128]{1,0:T(8,128)(2,1)S(1)}, bf16[128,128]{1,0:T(8,128)(2,1)S(1)}, u32[]{:S(2)}, u32[]{:S(2)}) collective-permute-start(bf16[128,128]{1,0:T(8,128)(2,1)S(1)} %get-tuple-element.36.refs_4_), channel_id=1, source_target_pairs={{0,4},{4,0},{8,12},{12,8},{16,20},{20,16},{24,28},{28,24},{1,5},{5... | collective-permute-start | bytes 98312 | tf_op jit(solution)/shard_map/ppermute | solution.py:290
  18.6 0.7 %collective-permute-done.7.refs_5_ = bf16[128,128]{1,0:T(8,128)(2,1)S(1)} collective-permute-done((bf16[128,128]{1,0:T(8,128)(2,1)S(1)}, bf16[128,128]{1,0:T(8,128)(2,1)S(1)}, u32[]{:S(2)}, u32[]{:S(2)}) %collective-permute-start.7) | collective-permute-done | bytes 32800 | tf_op jit(solution)/shard_map/ppermute | solution.py:290
  19.3 0.2 collective-permute-done.8.refs_6_
  19.5 0.0 collective-permute-done.4.refs_0_
  19.5 0.6 %collective-permute-done.5.refs_1_ = bf16[192,128]{1,0:T(8,128)(2,1)S(1)} collective-permute-done((bf16[192,128]{1,0:T(8,128)(2,1)S(1)}, bf16[192,128]{1,0:T(8,128)(2,1)S(1)}, u32[]{:S(2)}, u32[]{:S(2)}) %collective-permute-start.5) | collective-permute-done | bytes 49184 | tf_op jit(solution)/shard_map/ppermute | solution.py:293
  20.1 0.0 collective-permute-done.6.refs_2_
  20.1 0.8 %final.1 = bf16[64,128]{1,0:T(8,128)(2,1)} custom-call(f32[64,128]{1,0:T(8,128)S(1)} %get-tuple-element.21.alive_ref, f32[64,128]{1,0:T(8,128)S(1)} %get-tuple-element.30.after_ref.own_ref, bf16[512,128]{1,0:T(8,128)(2,1)S(1)} %get-tuple-element.31.amplitudes_ref, bf16[128,128]{1,0:T(8,128)(2,1)S(1)} %join.1.after_ref.refs_0_.message_ref, ...), custom_call_target="tpu_custom_call" | custom-call | tf_op jit(solution)/shard_map/final/pallas_call | solution.py:281
  (1 shorter events, 0.0 us)
Async XLA Ops:
  0.0 1.8 %collective-permute-start = (bf16[64,128]{1,0:T(8,128)(2,1)}, bf16[64,128]{1,0:T(8,128)(2,1)S(1)}, u32[]{:S(2)}, u32[]{:S(2)}) collective-permute-start(bf16[64,128]{1,0:T(8,128)(2,1)} %amplitudes_hbm.1), channel_id=1, source_target_pairs={{0,4},{4,0},{8,12},{12,8},{16,20},{20,16},{24,28},{28,24},{1,5},{5... | collective-permute-start | bytes 49160 | tf_op jit(solution)/shard_map/ppermute | solution.py:290
  1.8 7.7 %collective-permute-start.3 = (bf16[128,128]{1,0:T(8,128)(2,1)S(1)}, bf16[128,128]{1,0:T(8,128)(2,1)S(1)}, u32[]{:S(2)}, u32[]{:S(2)}) collective-permute-start(bf16[128,128]{1,0:T(8,128)(2,1)S(1)} %join.1.after_ref.refs_0_.message_ref), channel_id=1, source_target_pairs={{0,24},{4,28},{8,16},{12,20},{16,8},{20,12},{24,0},{28,4},{1,25},{... | collective-permute-start | bytes 98312 | tf_op jit(solution)/shard_map/ppermute | solution.py:290
  5.3 4.2 %collective-permute-start.2 = (bf16[128,128]{1,0:T(8,128)(2,1)S(1)}, bf16[128,128]{1,0:T(8,128)(2,1)S(1)}, u32[]{:S(2)}, u32[]{:S(2)}) collective-permute-start(bf16[128,128]{1,0:T(8,128)(2,1)S(1)} %join.1.after_ref.refs_0_.message_ref), channel_id=1, source_target_pairs={{0,16},{4,20},{8,24},{12,28},{16,0},{20,4},{24,8},{28,12},{1,17},{... | collective-permute-start | bytes 98312 | tf_op jit(solution)/shard_map/ppermute | solution.py:290
  5.8 3.9 %collective-permute-start.1 = (bf16[128,128]{1,0:T(8,128)(2,1)S(1)}, bf16[128,128]{1,0:T(8,128)(2,1)S(1)}, u32[]{:S(2)}, u32[]{:S(2)}) collective-permute-start(bf16[128,128]{1,0:T(8,128)(2,1)S(1)} %join.1.after_ref.refs_0_.message_ref), channel_id=1, source_target_pairs={{0,8},{4,12},{8,0},{12,4},{16,24},{20,28},{24,16},{28,20},{1,9},{5... | collective-permute-start | bytes 98312 | tf_op jit(solution)/shard_map/ppermute | solution.py:290
  11.2 8.3 %collective-permute-start.4 = (bf16[192,128]{1,0:T(8,128)(2,1)S(1)}, bf16[192,128]{1,0:T(8,128)(2,1)S(1)}, u32[]{:S(2)}, u32[]{:S(2)}) collective-permute-start(bf16[192,128]{1,0:T(8,128)(2,1)S(1)} %get-tuple-element.32), channel_id=1, source_target_pairs={{0,3},{1,2},{2,1},{3,0},{4,7},{5,6},{6,5},{7,4},{8,11},{9,10},{10,... | collective-permute-start | bytes 147464 | tf_op jit(solution)/shard_map/ppermute | solution.py:293
  15.1 5.0 %collective-permute-start.5 = (bf16[192,128]{1,0:T(8,128)(2,1)S(1)}, bf16[192,128]{1,0:T(8,128)(2,1)S(1)}, u32[]{:S(2)}, u32[]{:S(2)}) collective-permute-start(bf16[192,128]{1,0:T(8,128)(2,1)S(1)} %get-tuple-element.33), channel_id=1, source_target_pairs={{0,2},{1,3},{2,0},{3,1},{4,6},{5,7},{6,4},{7,5},{8,10},{9,11},{10,... | collective-permute-start | bytes 147464 | tf_op jit(solution)/shard_map/ppermute | solution.py:293
  15.1 5.0 %collective-permute-start.6 = (bf16[192,128]{1,0:T(8,128)(2,1)S(1)}, bf16[192,128]{1,0:T(8,128)(2,1)S(1)}, u32[]{:S(2)}, u32[]{:S(2)}) collective-permute-start(bf16[192,128]{1,0:T(8,128)(2,1)S(1)} %get-tuple-element.34), channel_id=1, source_target_pairs={{0,1},{1,0},{2,3},{3,2},{4,5},{5,4},{6,7},{7,6},{8,9},{9,8},{10,11... | collective-permute-start | bytes 147464 | tf_op jit(solution)/shard_map/ppermute | solution.py:293
  18.0 1.3 %collective-permute-start.7 = (bf16[128,128]{1,0:T(8,128)(2,1)S(1)}, bf16[128,128]{1,0:T(8,128)(2,1)S(1)}, u32[]{:S(2)}, u32[]{:S(2)}) collective-permute-start(bf16[128,128]{1,0:T(8,128)(2,1)S(1)} %get-tuple-element.35.refs_3_), channel_id=1, source_target_pairs={{0,4},{4,0},{8,12},{12,8},{16,20},{20,16},{24,28},{28,24},{1,5},{5... | collective-permute-start | bytes 98312 | tf_op jit(solution)/shard_map/ppermute | solution.py:290
  18.1 1.4 %collective-permute-start.8 = (bf16[128,128]{1,0:T(8,128)(2,1)S(1)}, bf16[128,128]{1,0:T(8,128)(2,1)S(1)}, u32[]{:S(2)}, u32[]{:S(2)}) collective-permute-start(bf16[128,128]{1,0:T(8,128)(2,1)S(1)} %get-tuple-element.36.refs_4_), channel_id=1, source_target_pairs={{0,4},{4,0},{8,12},{12,8},{16,20},{20,16},{24,28},{28,24},{1,5},{5... | collective-permute-start | bytes 98312 | tf_op jit(solution)/shard_map/ppermute | solution.py:290

commit v5 on v4

--- a/solution.py
+++ b/solution.py
@@ -42,12 +42,17 @@
     return jnp.where(code > 0, 1.0, -1.0).astype(F32)
 
 
+def turned(at, column, columns):
+    return ((at // columns) ^ column) * columns + at % columns
+
+
 def tables_kernel(cap, place, counts_hbm, irrep_hbm, code_hbm, integrals_hbm, gains_hbm, amplitudes_hbm, *refs):
-    code_ref, live_ref, mixer_ref, alive_ref, amplitudes_ref = refs[:5]
-    counts_ref, irrep_ref, integrals_ref, gains_ref, sems = refs[5:]
+    code_ref, live_ref, lane_ref, mixer_ref, alive_ref, amplitudes_ref = refs[:6]
+    counts_ref, irrep_ref, integrals_ref, gains_ref, plain_ref, sems = refs[6:]
     pairs, strings = code_ref.shape
     rows, columns = amplitudes_ref.shape
-    first_a, first_b = place()
+    first_a, column = place()
+    first_b = column * columns
     copies = [
         pltpu.make_async_copy(source, target, sems.at[i])
         for i, (source, target) in enumerate(
@@ -56,7 +61,7 @@
                 (integrals_hbm, integrals_ref),
                 (gains_hbm, gains_ref),
                 (counts_hbm, counts_ref),
-                (code_hbm, code_ref),
+                (code_hbm, plain_ref),
                 (amplitudes_hbm, amplitudes_ref),
             )
         )
@@ -80,7 +85,14 @@
     mixer = dot(left, spread_p)
     same = iota(mixer.shape, 0) % 8 == iota(mixer.shape, 1) // pairs
     mixer_ref[...] = jnp.where(same, mixer, 0.0).astype(BF16)
-    live_ref[...] = live_ids(counts_ref, 0, live_ref.shape, 0, cap)
+    within = iota((cap, 128), 0)
+    for block in range(strings // cap):
+        at = block * cap
+        live_ref[pl.ds(at, cap), :] = jnp.where(within < counts_ref[block], within + (at + 1), -1)
+    for k in range(strings // columns):
+        at = pl.multiple_of((column ^ k) * columns, columns)
+        code_ref[:, k * columns : (k + 1) * columns] = plain_ref[:, pl.ds(at, columns)]
+        lane_ref[:, k * columns : (k + 1) * columns] = live_ids(counts_ref, at, (8, columns), 1, cap)
     live_a = live_ids(counts_ref, first_a, (rows, columns), 0, cap)
     live_b = live_ids(counts_ref, first_b, (1, columns), 1, cap)
     alive_ref[...] = jnp.where((live_a > 0) & (live_b > 0), 1.0, 0.0)
@@ -92,10 +104,10 @@
     message_ref[rows:] = sibling_ref[...]
 
 
-def mix_kernel(columns_at, code_ref, live_ref, mixer_ref, after_ref, mixed_ref, one_ref):
+def mix_kernel(columns_at, code_ref, lane_ref, mixer_ref, after_ref, mixed_ref, one_ref):
     pairs, strings = code_ref.shape
     wide = pairs * 8
-    ids = jnp.broadcast_to(jnp.transpose(live_ref[...])[:1], (pairs, strings)).astype(I16)
+    ids = jnp.broadcast_to(lane_ref[:1, :], (pairs, strings)).astype(I16)
     zero = jnp.zeros(ids.shape, BF16)
     mixer = mixer_ref[...]
     code = columns_at(code_ref)
@@ -139,7 +151,8 @@
     pairs, strings = code_ref.shape
     rows, columns = block_ref.shape
     step = 0 if steps == 1 else pl.program_id(0)
-    first = pl.multiple_of(place(), columns)
+    column = place()
+    first = pl.multiple_of(column * columns, columns)
     ids = row_ids(live_ref, first, columns, strings)
     if steps > 1:
 
@@ -154,7 +167,7 @@
         total = total + dot_nt(hot, mixed_ref[q, :rows, :])
     if steps > 1:
         total_ref[...] = total
-    block_ref[...] = (one_ref[:rows, pl.ds(first, columns)] + 0.5 * jnp.transpose(total)).astype(BF16)
+    block_ref[...] = (one_ref[:rows, :columns] + 0.5 * jnp.transpose(total)).astype(BF16)
 
 
 def mixed_kernel(steps, groups, peers, place, mixed_ref, hot_ref, block_ref, *refs):
@@ -163,46 +176,60 @@
     sent = refs[groups + 2 : groups + 1 + peers][::-1]
     line, total_ref = refs[groups + 1 + peers :]
     pairs, strings = mixed_ref.shape[0], mixed_ref.shape[2]
-    rows, columns = own_ref.shape
+    rows, columns = block_ref.shape
     step = 0 if steps == 1 else pl.program_id(0)
     group, core, column = place()
 
     @pl.when(step == 0)
     def _():
-        total_ref[...] = jnp.zeros_like(total_ref)
+        if steps > 1:
+            total_ref[...] = jnp.zeros_like(total_ref)
         for k in range(groups):
             first = (group ^ k) * 2
-            at = pl.multiple_of((first + core) * rows, rows)
+            at = pl.multiple_of(turned((first + core) * rows, column, columns), rows)
             amplitudes_ref[pl.ds(at, rows), :] = arrived[k][:rows]
-            at = pl.multiple_of((first + 1 - core) * rows, rows)
+            at = pl.multiple_of(turned((first + 1 - core) * rows, column, columns), rows)
             amplitudes_ref[pl.ds(at, rows), :] = arrived[k][rows:]
 
+    if steps == 1:
+        line = own_ref
     amplitudes = amplitudes_ref[...]
     for q in range(pairs):
         part = dot(mixed_ref[q, :rows, :], amplitudes)
         line[:, pl.ds(q * columns, columns)] = part.astype(BF16)
-    total_ref[...] += dot(line[...], hot_ref[...])
+    if steps == 1:
+        total = dot(line[...], hot_ref[:, columns:])
+    else:
+        total_ref[...] += dot(line[...], hot_ref[...])
 
     @pl.when(step == steps - 1)
     def _():
-        for k in range(peers):
-            part = total_ref[:, pl.ds(pl.multiple_of((column ^ k) * columns, columns), columns)]
-            if k == 0:
-                own_ref[...] = part
+        if steps > 1:
+            own_ref[...] = total_ref[:, :columns]
+        for k in range(1, peers):
+            if steps == 1:
+                part = total[:, (k - 1) * columns : k * columns]
             else:
-                sent[k - 1][:rows] = part.astype(BF16)
-                sent[k - 1][rows : 2 * rows] = arrived[0][:rows]
-                sent[k - 1][2 * rows :] = block_ref[...]
-
-
-def same_spin_kernel(steps, place, live_ref, code_ref, mixed_ref, one_ref, after_ref, *refs):
+                part = total_ref[:, pl.ds(k * columns, columns)]
+            sent[k - 1][:rows] = part.astype(BF16)
+            sent[k - 1][rows : 2 * rows] = arrived[0][:rows]
+            sent[k - 1][2 * rows :] = block_ref[...]
+
+
+def same_spin_kernel(steps, place, live_ref, code_ref, mixed_ref, one_ref, part_ref, hot_ref, *refs):
     pairs, both, strings = mixed_ref.shape
-    side_refs, total_ref = refs[:-1], refs[-1]
+    own_ref, side_refs, total_ref = refs[0], refs[1:-1], refs[-1]
     piece, columns = side_refs[0].shape
     half = piece * len(side_refs)
     step = 0 if steps == 1 else pl.program_id(0)
-    at = pl.multiple_of(place() * half, half)
+    core, column = place()
+    at = pl.multiple_of(core * half, half)
+    width = min(piece, columns)
     tile = piece
+    if steps == 1:
+        own_ref[...] = dot(part_ref[...], hot_ref[:, :columns])
+    else:
+        own_ref[...] = part_ref[...]
     if steps > 1:
 
         @pl.when(step == 0)
@@ -216,7 +243,11 @@
             total = total + dot_nt(hot_tile(code_ref[q : q + 1, :], ids), mixed_ref[q, both - columns :, :])
         if steps > 1:
             total_ref[pl.ds(first, tile), :] = total
-        one = jnp.transpose(one_ref[both - columns :, pl.ds(at + first, tile)])
+        blocks = [
+            one_ref[both - columns :, pl.ds(pl.multiple_of(turned(at + low, column, columns), width), width)]
+            for low in range(first, first + tile, width)
+        ]
+        one = jnp.transpose(jnp.concatenate(blocks, 1))
         side_refs[first // piece][...] = (one + 0.5 * total).astype(BF16)
 
 
@@ -240,7 +271,7 @@
         else:
             left += [arrived[k - 1][2 * rows :], arrived[k - 1][rows : 2 * rows]]
             total = total + arrived[k - 1][:rows].astype(F32)
-        right += [amplitudes_ref[pl.ds(at, columns), :], side_ref[pl.ds(at, columns), :]]
+        right += [amplitudes_ref[k * columns : (k + 1) * columns, :], side_ref[pl.ds(at, columns), :]]
     total = total + dot(jnp.concatenate(left, 1), jnp.concatenate(right, 0))
     out_ref[...] = (total * alive_ref[...]).astype(BF16)
 
@@ -294,16 +325,17 @@
 
     def columns_at(code_ref):
         if resident:
-            chip = code_ref[:, pl.ds(pl.multiple_of(alpha() // 2 * 2 * rows, 2 * rows), 2 * rows)]
+            at = turned(alpha() // 2 * 2 * rows, beta(), columns)
+            chip = code_ref[:, pl.ds(pl.multiple_of(at, 2 * rows), 2 * rows)]
             own = jnp.where(alpha() % 2 == 0, chip[:, :rows], chip[:, rows:])
-            return jnp.concatenate([own, code_ref[:, pl.ds(pl.multiple_of(beta() * columns, columns), columns)]], 1)
+            return jnp.concatenate([own, code_ref[:, :columns]], 1)
         at = pl.program_id(0) * tile
         first = jnp.where(at < rows, alpha() * rows + at, beta() * columns + at - rows)
-        return code_ref[:, pl.ds(pl.multiple_of(first, tile), tile)]
+        return code_ref[:, pl.ds(pl.multiple_of(turned(first, beta(), columns), tile), tile)]
 
     sibling = over_alpha(amplitudes, 1)
-    codes, live, mixer, alive, own_c = call(
-        functools.partial(tables_kernel, cap, lambda: (alpha() * rows, beta() * columns)),
+    codes, live, lane, mixer, alive, own_c = call(
+        functools.partial(tables_kernel, cap, lambda: (alpha() * rows, beta())),
         "tables",
         1,
         far(counts),
@@ -316,16 +348,18 @@
         out_shape=(
             shape_of((pairs, strings), I32),
             shape_of((strings, 128), I32),
+            shape_of((8, strings), I32),
             shape_of((pairs * 8 + 8, pairs * 8), BF16),
             shape_of((rows, columns), F32),
             shape_of((rows, columns), BF16),
         ),
-        out_specs=(vmem,) * 5,
+        out_specs=(vmem,) * 6,
         scratch_shapes=[
             pltpu.SMEM(counts.shape, I32),
             pltpu.SMEM(pair_irrep.shape, I32),
             pltpu.VMEM((pairs, pairs), BF16),
             pltpu.VMEM((1, pairs), BF16),
+            pltpu.VMEM((pairs, strings), I32),
             pltpu.SemaphoreType.DMA((6,)),
         ],
     )
@@ -345,7 +379,7 @@
         "mix",
         row_tiles,
         near(codes),
-        near(live),
+        near(lane),
         near(mixer),
         near(message),
         flops=2 * both * pairs * pairs * 8 * strings,
@@ -356,7 +390,7 @@
     code_parts = near(codes) if resident else codes.reshape(pair_tiles, part, strings)
     code_spec = vmem if resident else pl.BlockSpec((None, part, strings), lambda i: (i, 0, 0))
     hot, block = call(
-        functools.partial(hot_kernel, pair_tiles, lambda: beta() * columns),
+        functools.partial(hot_kernel, pair_tiles, beta),
         "hot",
         pair_tiles,
         near(live),
@@ -378,7 +412,10 @@
         near(block),
         *[near(m) for m in messages],
         in_specs=[tiled((part, both, strings), 0), tiled((part * columns, strings), 0)] + [vmem] * (groups + 1),
-        out_shape=(shape_of((rows, columns), F32), shape_of((strings, columns), BF16))
+        out_shape=(
+            shape_of((rows, pairs * columns), BF16) if resident else shape_of((rows, columns), F32),
+            shape_of((strings, columns), BF16),
+        )
         + tuple(shape_of((3 * rows, columns), BF16) for _ in range(peers - 1)),
         out_specs=(vmem,) * (peers + 1),
         scratch_shapes=[pltpu.VMEM((rows, part * columns), BF16), pltpu.VMEM((rows, strings), F32)],
@@ -386,8 +423,8 @@
     own, gathered = outs[:2]
     arrived = [over_beta(m, k) for k, m in zip(range(peers - 1, 0, -1), outs[2:])]
     pieces = SIDE_PIECES
-    sides = call(
-        functools.partial(same_spin_kernel, pair_tiles, lambda: alpha() % 2),
+    own, *sides = call(
+        functools.partial(same_spin_kernel, pair_tiles, lambda: (alpha() % 2, beta())),
         "same_spin",
         pair_tiles,
         near(live),
@@ -395,10 +432,12 @@
         near(mixed),
         near(one),
         near(own),
+        near(hot) if resident else hot[:16, :128],
         flops=2 * columns * pairs * strings * strings,
-        in_specs=[vmem, code_spec, tiled((part, both, strings), 0)] + [vmem] * 2,
-        out_shape=tuple(shape_of((strings // 2 // pieces, columns), BF16) for _ in range(pieces)),
-        out_specs=(vmem,) * pieces,
+        in_specs=[vmem, code_spec, tiled((part, both, strings), 0)] + [vmem] * 3,
+        out_shape=(shape_of((rows, columns), F32),)
+        + tuple(shape_of((strings // 2 // pieces, columns), BF16) for _ in range(pieces)),
+        out_specs=(vmem,) * (1 + pieces),
         scratch_shapes=[pltpu.VMEM((strings // 2, columns), F32)],
     )
     sides = list(sides) + [over_alpha(side, 1) for side in sides]

time: 21 us -> 20.7 us (0.986)
    ppermute x3, waiting for transfers between devices: 0.59 us -> 0.35 us  [over_beta(): return lax.ppermute(value, 'ba', [(i, i ^ mask) for i in range(peers)])]
  transfers between devices with their start and end apart: 9 -> 9, of which waited for: 4 -> 4; matrix products, arithmetic and copies ran while one was open for 0% -> 0% of each run, Pallas kernels for 34% -> 35%
where the time goes in v5:
time: 20.7 us; the launch traced here: 20.6 us
  starting transfers between devices  9.63 us (47%)
  Pallas kernels  9.29 us (45%)
  waiting for transfers between devices  1.55 us (7%)
    pallas_call x7, Pallas kernels, call(): pl.pallas_call(body, name=name, compiler_params=params, cost_estimate=cos...  9.29 us
    ppermute x6, starting transfers between devices, over_alpha(): return lax.ppermute(value, 'aa', [(i, i ^ mask) for i in range(sizes[0])])  5.17 us
    ppermute x3, starting transfers between devices, over_beta(): return lax.ppermute(value, 'ba', [(i, i ^ mask) for i in range(peers)])  4.45 us
    ppermute x6, waiting for transfers between devices, over_alpha(): return lax.ppermute(value, 'aa', [(i, i ^ mask) for i in range(sizes[0])])  1.2 us
  transfers between devices with their start and end apart: 9, of which 4 were waited for; matrix products, arithmetic and copies ran while one was open for 0% of the time, Pallas kernels for 35%

profile of v5, /device:TPU:0, one launch (start us, length us, event | category | flops | bytes accessed | tf_op | source)
XLA Modules:
  0.0 20.6 jit_solution(633133274082695938)
XLA Ops:
  0.0 0.5 %collective-permute-start = (bf16[64,128]{1,0:T(8,128)(2,1)}, bf16[64,128]{1,0:T(8,128)(2,1)S(1)}, u32[]{:S(2)}, u32[]{:S(2)}) collective-permute-start(bf16[64,128]{1,0:T(8,128)(2,1)} %amplitudes_hbm.1), channel_id=1, source_target_pairs={{0,4},{4,0},{8,12},{12,8},{16,20},{20,16},{24,28},{28,24},{1,5},{5... | collective-permute-start | bytes 49160 | tf_op jit(solution)/shard_map/ppermute | solution.py:321
  0.5 1.3 %tables.1 = (s32[32,512]{1,0:T(8,128)S(1)}, s32[512,128]{1,0:T(8,128)S(1)}, s32[8,512]{1,0:T(8,128)S(1)}, bf16[264,256]{1,0:T(8,128)(2,1)S(1)}, f32[64,128]{1,0:T(8,128)S(1)}, /*index=5*/bf16[64,128]{1,0:T(8,128)(2,1)S(1)}) custom-call(s32[32]{0:T(128)} %counts_hbm.1, s32[32]{0:T(128)} %irrep_hbm.1, s32[32,512]{1,0:T(8,128)} %code_hbm.1, ...), custom_call_target="tpu_custom_call" | custom-call | tf_op jit(solution)/shard_map/tables/pallas_call | solution.py:312
  1.8 0.0 collective-permute-done.sibling_ref
  1.8 3.5 %collective-permute-start.3 = (bf16[128,128]{1,0:T(8,128)(2,1)S(1)}, bf16[128,128]{1,0:T(8,128)(2,1)S(1)}, u32[]{:S(2)}, u32[]{:S(2)}) collective-permute-start(bf16[128,128]{1,0:T(8,128)(2,1)S(1)} %join.1.after_ref.refs_0_.message_ref), channel_id=1, source_target_pairs={{0,24},{4,28},{8,16},{12,20},{16,8},{20,12},{24,0},{28,4},{1,25},{... | collective-permute-start | bytes 98312 | tf_op jit(solution)/shard_map/ppermute | solution.py:321
  5.3 0.5 %collective-permute-start.2 = (bf16[128,128]{1,0:T(8,128)(2,1)S(1)}, bf16[128,128]{1,0:T(8,128)(2,1)S(1)}, u32[]{:S(2)}, u32[]{:S(2)}) collective-permute-start(bf16[128,128]{1,0:T(8,128)(2,1)S(1)} %join.1.after_ref.refs_0_.message_ref), channel_id=1, source_target_pairs={{0,16},{4,20},{8,24},{12,28},{16,0},{20,4},{24,8},{28,12},{1,17},{... | collective-permute-start | bytes 98312 | tf_op jit(solution)/shard_map/ppermute | solution.py:321
  5.8 0.1 collective-permute-start.1
  5.9 2.1 %mix.1 = (bf16[32,192,512]{2,1,0:T(8,128)(2,1)S(1)}, f32[192,512]{1,0:T(8,128)S(1)}) custom-call(s32[32,512]{1,0:T(8,128)S(1)} %get-tuple-element.25.code_ref, s32[8,512]{1,0:T(8,128)S(1)} %get-tuple-element.26.lane_ref, bf16[264,256]{1,0:T(8,128)(2,1)S(1)} %get-tuple-element.27.mixer_ref, bf16[128,128]{1,0:T(8,128)(2,1)S(1)} %join.1.after_ref.refs_0_.message_ref), custom_call_target="tpu_custom_call" | custom-call | flops 1610612736 | tf_op jit(solution)/shard_map/mix/pallas_call | solution.py:312
  8.1 1.3 %hot.1 = (bf16[4096,512]{1,0:T(8,128)(2,1)S(1)}, bf16[64,128]{1,0:T(8,128)(2,1)S(1)}) custom-call(s32[512,128]{1,0:T(8,128)S(1)} %get-tuple-element.24.live_ref, s32[32,512]{1,0:T(8,128)S(1)} %get-tuple-element.25.code_ref, bf16[32,192,512]{2,1,0:T(8,128)(2,1)S(1)} %get-tuple-element.29.mixed_ref, f32[192,512]{1,0:T(8,128)S(1)} %get-tuple-element.30.one_ref), custom_call_target="tpu_custom_call" | custom-call | flops 268435456 | tf_op jit(solution)/shard_map/hot/pallas_call | solution.py:312
  9.4 0.0 collective-permute-done.3.refs_3_
  9.4 0.0 collective-permute-done.2.refs_2_
  9.4 0.3 %collective-permute-done.1.refs_1_ = bf16[128,128]{1,0:T(8,128)(2,1)S(1)} collective-permute-done((bf16[128,128]{1,0:T(8,128)(2,1)S(1)}, bf16[128,128]{1,0:T(8,128)(2,1)S(1)}, u32[]{:S(2)}, u32[]{:S(2)}) %collective-permute-start.1) | collective-permute-done | bytes 32800 | tf_op jit(solution)/shard_map/ppermute | solution.py:321
  9.7 1.3 %mixed.1 = (bf16[64,4096]{1,0:T(8,128)(2,1)S(1)}, bf16[512,128]{1,0:T(8,128)(2,1)S(1)}, bf16[192,128]{1,0:T(8,128)(2,1)S(1)}, bf16[192,128]{1,0:T(8,128)(2,1)S(1)}, bf16[192,128]{1,0:T(8,128)(2,1)S(1)}) custom-call(bf16[32,192,512]{2,1,0:T(8,128)(2,1)S(1)} %get-tuple-element.29.mixed_ref, bf16[4096,512]{1,0:T(8,128)(2,1)S(1)} %get-tuple-element.31.hot_ref, ...), custom_call_target="tpu_custom_call" | custom-call | tf_op jit(solution)/shard_map/mixed/pallas_call | solution.py:312
  11.0 3.8 %collective-permute-start.4 = (bf16[192,128]{1,0:T(8,128)(2,1)S(1)}, bf16[192,128]{1,0:T(8,128)(2,1)S(1)}, u32[]{:S(2)}, u32[]{:S(2)}) collective-permute-start(bf16[192,128]{1,0:T(8,128)(2,1)S(1)} %get-tuple-element.36), channel_id=1, source_target_pairs={{0,3},{1,2},{2,1},{3,0},{4,7},{5,6},{6,5},{7,4},{8,11},{9,10},{10,... | collective-permute-start | bytes 147464 | tf_op jit(solution)/shard_map/ppermute | solution.py:324
  14.8 0.0 collective-permute-start.5
  14.8 0.7 %collective-permute-start.6 = (bf16[192,128]{1,0:T(8,128)(2,1)S(1)}, bf16[192,128]{1,0:T(8,128)(2,1)S(1)}, u32[]{:S(2)}, u32[]{:S(2)}) collective-permute-start(bf16[192,128]{1,0:T(8,128)(2,1)S(1)} %get-tuple-element.38), channel_id=1, source_target_pairs={{0,1},{1,0},{2,3},{3,2},{4,5},{5,4},{6,7},{7,6},{8,9},{9,8},{10,11... | collective-permute-start | bytes 147464 | tf_op jit(solution)/shard_map/ppermute | solution.py:324
  15.4 2.5 %same_spin.1 = (f32[64,128]{1,0:T(8,128)S(1)}, bf16[128,128]{1,0:T(8,128)(2,1)S(1)}, bf16[128,128]{1,0:T(8,128)(2,1)S(1)}) custom-call(s32[512,128]{1,0:T(8,128)S(1)} %get-tuple-element.24.live_ref, s32[32,512]{1,0:T(8,128)S(1)} %get-tuple-element.25.code_ref, bf16[32,192,512]{2,1,0:T(8,128)(2,1)S(1)} %get-tuple-element.29.mixed_ref, ...), custom_call_target="tpu_custom_call" | custom-call | flops 2147483648 | tf_op jit(solution)/shard_map/same_spin/pallas_call | solution.py:312
  18.0 0.1 collective-permute-start.7
  18.0 0.5 %collective-permute-start.8 = (bf16[128,128]{1,0:T(8,128)(2,1)S(1)}, bf16[128,128]{1,0:T(8,128)(2,1)S(1)}, u32[]{:S(2)}, u32[]{:S(2)}) collective-permute-start(bf16[128,128]{1,0:T(8,128)(2,1)S(1)} %get-tuple-element.40.refs_4_), channel_id=1, source_target_pairs={{0,4},{4,0},{8,12},{12,8},{16,20},{20,16},{24,28},{28,24},{1,5},{5... | collective-permute-start | bytes 98312 | tf_op jit(solution)/shard_map/ppermute | solution.py:321
  18.5 0.7 %collective-permute-done.7.refs_5_ = bf16[128,128]{1,0:T(8,128)(2,1)S(1)} collective-permute-done((bf16[128,128]{1,0:T(8,128)(2,1)S(1)}, bf16[128,128]{1,0:T(8,128)(2,1)S(1)}, u32[]{:S(2)}, u32[]{:S(2)}) %collective-permute-start.7) | collective-permute-done | bytes 32800 | tf_op jit(solution)/shard_map/ppermute | solution.py:321
  19.2 0.2 collective-permute-done.8.refs_6_
  19.4 0.0 collective-permute-done.4.refs_0_
  19.4 0.3 %collective-permute-done.5.refs_1_ = bf16[192,128]{1,0:T(8,128)(2,1)S(1)} collective-permute-done((bf16[192,128]{1,0:T(8,128)(2,1)S(1)}, bf16[192,128]{1,0:T(8,128)(2,1)S(1)}, u32[]{:S(2)}, u32[]{:S(2)}) %collective-permute-start.5) | collective-permute-done | bytes 49184 | tf_op jit(solution)/shard_map/ppermute | solution.py:324
  19.7 0.0 collective-permute-done.6.refs_2_
  19.7 0.8 %final.1 = bf16[64,128]{1,0:T(8,128)(2,1)} custom-call(f32[64,128]{1,0:T(8,128)S(1)} %get-tuple-element.23.alive_ref, f32[64,128]{1,0:T(8,128)S(1)} %get-tuple-element.34.own_ref, bf16[512,128]{1,0:T(8,128)(2,1)S(1)} %get-tuple-element.35.amplitudes_ref, bf16[128,128]{1,0:T(8,128)(2,1)S(1)} %join.1.after_ref.refs_0_.message_ref, ...), custom_call_target="tpu_custom_call" | custom-call | tf_op jit(solution)/shard_map/final/pallas_call | solution.py:312
  (1 shorter events, 0.0 us)
Async XLA Ops:
  0.0 1.8 %collective-permute-start = (bf16[64,128]{1,0:T(8,128)(2,1)}, bf16[64,128]{1,0:T(8,128)(2,1)S(1)}, u32[]{:S(2)}, u32[]{:S(2)}) collective-permute-start(bf16[64,128]{1,0:T(8,128)(2,1)} %amplitudes_hbm.1), channel_id=1, source_target_pairs={{0,4},{4,0},{8,12},{12,8},{16,20},{20,16},{24,28},{28,24},{1,5},{5... | collective-permute-start | bytes 49160 | tf_op jit(solution)/shard_map/ppermute | solution.py:321
  1.8 7.6 %collective-permute-start.3 = (bf16[128,128]{1,0:T(8,128)(2,1)S(1)}, bf16[128,128]{1,0:T(8,128)(2,1)S(1)}, u32[]{:S(2)}, u32[]{:S(2)}) collective-permute-start(bf16[128,128]{1,0:T(8,128)(2,1)S(1)} %join.1.after_ref.refs_0_.message_ref), channel_id=1, source_target_pairs={{0,24},{4,28},{8,16},{12,20},{16,8},{20,12},{24,0},{28,4},{1,25},{... | collective-permute-start | bytes 98312 | tf_op jit(solution)/shard_map/ppermute | solution.py:321
  5.3 4.1 %collective-permute-start.2 = (bf16[128,128]{1,0:T(8,128)(2,1)S(1)}, bf16[128,128]{1,0:T(8,128)(2,1)S(1)}, u32[]{:S(2)}, u32[]{:S(2)}) collective-permute-start(bf16[128,128]{1,0:T(8,128)(2,1)S(1)} %join.1.after_ref.refs_0_.message_ref), channel_id=1, source_target_pairs={{0,16},{4,20},{8,24},{12,28},{16,0},{20,4},{24,8},{28,12},{1,17},{... | collective-permute-start | bytes 98312 | tf_op jit(solution)/shard_map/ppermute | solution.py:321
  5.8 3.9 %collective-permute-start.1 = (bf16[128,128]{1,0:T(8,128)(2,1)S(1)}, bf16[128,128]{1,0:T(8,128)(2,1)S(1)}, u32[]{:S(2)}, u32[]{:S(2)}) collective-permute-start(bf16[128,128]{1,0:T(8,128)(2,1)S(1)} %join.1.after_ref.refs_0_.message_ref), channel_id=1, source_target_pairs={{0,8},{4,12},{8,0},{12,4},{16,24},{20,28},{24,16},{28,20},{1,9},{5... | collective-permute-start | bytes 98312 | tf_op jit(solution)/shard_map/ppermute | solution.py:321
  11.0 8.4 %collective-permute-start.4 = (bf16[192,128]{1,0:T(8,128)(2,1)S(1)}, bf16[192,128]{1,0:T(8,128)(2,1)S(1)}, u32[]{:S(2)}, u32[]{:S(2)}) collective-permute-start(bf16[192,128]{1,0:T(8,128)(2,1)S(1)} %get-tuple-element.36), channel_id=1, source_target_pairs={{0,3},{1,2},{2,1},{3,0},{4,7},{5,6},{6,5},{7,4},{8,11},{9,10},{10,... | collective-permute-start | bytes 147464 | tf_op jit(solution)/shard_map/ppermute | solution.py:324
  14.8 5.0 %collective-permute-start.5 = (bf16[192,128]{1,0:T(8,128)(2,1)S(1)}, bf16[192,128]{1,0:T(8,128)(2,1)S(1)}, u32[]{:S(2)}, u32[]{:S(2)}) collective-permute-start(bf16[192,128]{1,0:T(8,128)(2,1)S(1)} %get-tuple-element.37), channel_id=1, source_target_pairs={{0,2},{1,3},{2,0},{3,1},{4,6},{5,7},{6,4},{7,5},{8,10},{9,11},{10,... | collective-permute-start | bytes 147464 | tf_op jit(solution)/shard_map/ppermute | solution.py:324
  14.8 5.0 %collective-permute-start.6 = (bf16[192,128]{1,0:T(8,128)(2,1)S(1)}, bf16[192,128]{1,0:T(8,128)(2,1)S(1)}, u32[]{:S(2)}, u32[]{:S(2)}) collective-permute-start(bf16[192,128]{1,0:T(8,128)(2,1)S(1)} %get-tuple-element.38), channel_id=1, source_target_pairs={{0,1},{1,0},{2,3},{3,2},{4,5},{5,4},{6,7},{7,6},{8,9},{9,8},{10,11... | collective-permute-start | bytes 147464 | tf_op jit(solution)/shard_map/ppermute | solution.py:324
  18.0 1.3 %collective-permute-start.7 = (bf16[128,128]{1,0:T(8,128)(2,1)S(1)}, bf16[128,128]{1,0:T(8,128)(2,1)S(1)}, u32[]{:S(2)}, u32[]{:S(2)}) collective-permute-start(bf16[128,128]{1,0:T(8,128)(2,1)S(1)} %get-tuple-element.39.refs_3_), channel_id=1, source_target_pairs={{0,4},{4,0},{8,12},{12,8},{16,20},{20,16},{24,28},{28,24},{1,5},{5... | collective-permute-start | bytes 98312 | tf_op jit(solution)/shard_map/ppermute | solution.py:321
  18.0 1.4 %collective-permute-start.8 = (bf16[128,128]{1,0:T(8,128)(2,1)S(1)}, bf16[128,128]{1,0:T(8,128)(2,1)S(1)}, u32[]{:S(2)}, u32[]{:S(2)}) collective-permute-start(bf16[128,128]{1,0:T(8,128)(2,1)S(1)} %get-tuple-element.40.refs_4_), channel_id=1, source_target_pairs={{0,4},{4,0},{8,12},{12,8},{16,20},{20,16},{24,28},{28,24},{1,5},{5... | collective-permute-start | bytes 98312 | tf_op jit(solution)/shard_map/ppermute | solution.py:321

commit v6 on v5

--- a/solution.py
+++ b/solution.py
@@ -40,6 +40,10 @@
 
 def sign_of(code):
     return jnp.where(code > 0, 1.0, -1.0).astype(F32)
+
+
+def by_start(peers):
+    return (*range(2, peers), 1)
 
 
 def turned(at, column, columns):
@@ -173,7 +177,7 @@
 def mixed_kernel(steps, groups, peers, place, mixed_ref, hot_ref, block_ref, *refs):
     arrived = refs[:groups]
     own_ref, amplitudes_ref = refs[groups : groups + 2]
-    sent = refs[groups + 2 : groups + 1 + peers][::-1]
+    sent = [refs[groups + 2 + by_start(peers).index(k)] for k in range(1, peers)]
     line, total_ref = refs[groups + 1 + peers :]
     pairs, strings = mixed_ref.shape[0], mixed_ref.shape[2]
     rows, columns = block_ref.shape
@@ -194,9 +198,10 @@
     if steps == 1:
         line = own_ref
     amplitudes = amplitudes_ref[...]
-    for q in range(pairs):
-        part = dot(mixed_ref[q, :rows, :], amplitudes)
-        line[:, pl.ds(q * columns, columns)] = part.astype(BF16)
+    for low in range(0, pairs, 4):
+        part = dot(mixed_ref[low : low + 4, :rows, :].reshape(4 * rows, strings), amplitudes).astype(BF16)
+        for q in range(4):
+            line[:, pl.ds((low + q) * columns, columns)] = part[q * rows : (q + 1) * rows]
     if steps == 1:
         total = dot(line[...], hot_ref[:, columns:])
     else:
@@ -253,7 +258,7 @@
 
 def final_kernel(peers, place, alive_ref, own_ref, amplitudes_ref, message_ref, block_ref, *refs):
     out_ref, side_ref = refs[-2:]
-    arrived, sides = refs[: peers - 1][::-1], refs[peers - 1 : -2]
+    arrived, sides = [refs[by_start(peers).index(k)] for k in range(1, peers)], refs[peers - 1 : -2]
     rows, columns = own_ref.shape
     piece = sides[0].shape[0]
     pieces = len(sides) // 2
@@ -421,7 +426,7 @@
         scratch_shapes=[pltpu.VMEM((rows, part * columns), BF16), pltpu.VMEM((rows, strings), F32)],
     )
     own, gathered = outs[:2]
-    arrived = [over_beta(m, k) for k, m in zip(range(peers - 1, 0, -1), outs[2:])]
+    arrived = [over_beta(m, k) for k, m in zip(by_start(peers), outs[2:])]
     pieces = SIDE_PIECES
     own, *sides = call(
         functools.partial(same_spin_kernel, pair_tiles, lambda: (alpha() % 2, beta())),

time: 20.7 us -> 20.6 us (level)
  no operation moved by 1% of the time
where the time goes in v6:
time: 20.6 us; the launch traced here: 20.5 us
  starting transfers between devices  9.5 us (46%)
  Pallas kernels  9.28 us (45%)
  waiting for transfers between devices  1.63 us (8%)
    pallas_call x7, Pallas kernels, call(): pl.pallas_call(body, name=name, compiler_params=params, cost_estimate=cos...  9.28 us
    ppermute x6, starting transfers between devices, over_alpha(): return lax.ppermute(value, 'aa', [(i, i ^ mask) for i in range(sizes[0])])  5.17 us
    ppermute x3, starting transfers between devices, over_beta(): return lax.ppermute(value, 'ba', [(i, i ^ mask) for i in range(peers)])  4.33 us
    ppermute x6, waiting for transfers between devices, over_alpha(): return lax.ppermute(value, 'aa', [(i, i ^ mask) for i in range(sizes[0])])  1.2 us
    ppermute x3, waiting for transfers between devices, over_beta(): return lax.ppermute(value, 'ba', [(i, i ^ mask) for i in range(peers)])  0.43 us
  transfers between devices with their start and end apart: 9, of which 4 were waited for; matrix products, arithmetic and copies ran while one was open for 0% of the time, Pallas kernels for 35%

profile of v6, /device:TPU:0, one launch (start us, length us, event | category | flops | bytes accessed | tf_op | source)
XLA Modules:
  0.0 20.5 jit_solution(1310857331971231472)
XLA Ops:
  0.0 0.5 %collective-permute-start = (bf16[64,128]{1,0:T(8,128)(2,1)}, bf16[64,128]{1,0:T(8,128)(2,1)S(1)}, u32[]{:S(2)}, u32[]{:S(2)}) collective-permute-start(bf16[64,128]{1,0:T(8,128)(2,1)} %amplitudes_hbm.1), channel_id=1, source_target_pairs={{0,4},{4,0},{8,12},{12,8},{16,20},{20,16},{24,28},{28,24},{1,5},{5... | collective-permute-start | bytes 49160 | tf_op jit(solution)/shard_map/ppermute | solution.py:326
  0.5 1.3 %tables.1 = (s32[32,512]{1,0:T(8,128)S(1)}, s32[512,128]{1,0:T(8,128)S(1)}, s32[8,512]{1,0:T(8,128)S(1)}, bf16[264,256]{1,0:T(8,128)(2,1)S(1)}, f32[64,128]{1,0:T(8,128)S(1)}, /*index=5*/bf16[64,128]{1,0:T(8,128)(2,1)S(1)}) custom-call(s32[32]{0:T(128)} %counts_hbm.1, s32[32]{0:T(128)} %irrep_hbm.1, s32[32,512]{1,0:T(8,128)} %code_hbm.1, ...), custom_call_target="tpu_custom_call" | custom-call | tf_op jit(solution)/shard_map/tables/pallas_call | solution.py:317
  1.8 0.0 collective-permute-done.sibling_ref
  1.8 3.5 %collective-permute-start.3 = (bf16[128,128]{1,0:T(8,128)(2,1)S(1)}, bf16[128,128]{1,0:T(8,128)(2,1)S(1)}, u32[]{:S(2)}, u32[]{:S(2)}) collective-permute-start(bf16[128,128]{1,0:T(8,128)(2,1)S(1)} %join.1.after_ref.refs_0_.message_ref), channel_id=1, source_target_pairs={{0,24},{4,28},{8,16},{12,20},{16,8},{20,12},{24,0},{28,4},{1,25},{... | collective-permute-start | bytes 98312 | tf_op jit(solution)/shard_map/ppermute | solution.py:326
  5.3 0.5 %collective-permute-start.2 = (bf16[128,128]{1,0:T(8,128)(2,1)S(1)}, bf16[128,128]{1,0:T(8,128)(2,1)S(1)}, u32[]{:S(2)}, u32[]{:S(2)}) collective-permute-start(bf16[128,128]{1,0:T(8,128)(2,1)S(1)} %join.1.after_ref.refs_0_.message_ref), channel_id=1, source_target_pairs={{0,16},{4,20},{8,24},{12,28},{16,0},{20,4},{24,8},{28,12},{1,17},{... | collective-permute-start | bytes 98312 | tf_op jit(solution)/shard_map/ppermute | solution.py:326
  5.8 0.1 collective-permute-start.1
  5.9 2.1 %mix.1 = (bf16[32,192,512]{2,1,0:T(8,128)(2,1)S(1)}, f32[192,512]{1,0:T(8,128)S(1)}) custom-call(s32[32,512]{1,0:T(8,128)S(1)} %get-tuple-element.25.code_ref, s32[8,512]{1,0:T(8,128)S(1)} %get-tuple-element.26.lane_ref, bf16[264,256]{1,0:T(8,128)(2,1)S(1)} %get-tuple-element.27.mixer_ref, bf16[128,128]{1,0:T(8,128)(2,1)S(1)} %join.1.after_ref.refs_0_.message_ref), custom_call_target="tpu_custom_call" | custom-call | flops 1610612736 | tf_op jit(solution)/shard_map/mix/pallas_call | solution.py:317
  8.1 1.3 %hot.1 = (bf16[4096,512]{1,0:T(8,128)(2,1)S(1)}, bf16[64,128]{1,0:T(8,128)(2,1)S(1)}) custom-call(s32[512,128]{1,0:T(8,128)S(1)} %get-tuple-element.24.live_ref, s32[32,512]{1,0:T(8,128)S(1)} %get-tuple-element.25.code_ref, bf16[32,192,512]{2,1,0:T(8,128)(2,1)S(1)} %get-tuple-element.29.mixed_ref, f32[192,512]{1,0:T(8,128)S(1)} %get-tuple-element.30.one_ref), custom_call_target="tpu_custom_call" | custom-call | flops 268435456 | tf_op jit(solution)/shard_map/hot/pallas_call | solution.py:317
  9.4 0.0 collective-permute-done.3.refs_3_
  9.4 0.0 collective-permute-done.2.refs_2_
  9.4 0.3 %collective-permute-done.1.refs_1_ = bf16[128,128]{1,0:T(8,128)(2,1)S(1)} collective-permute-done((bf16[128,128]{1,0:T(8,128)(2,1)S(1)}, bf16[128,128]{1,0:T(8,128)(2,1)S(1)}, u32[]{:S(2)}, u32[]{:S(2)}) %collective-permute-start.1) | collective-permute-done | bytes 32800 | tf_op jit(solution)/shard_map/ppermute | solution.py:326
  9.7 1.2 %mixed.1 = (bf16[64,4096]{1,0:T(8,128)(2,1)S(1)}, bf16[512,128]{1,0:T(8,128)(2,1)S(1)}, bf16[192,128]{1,0:T(8,128)(2,1)S(1)}, bf16[192,128]{1,0:T(8,128)(2,1)S(1)}, bf16[192,128]{1,0:T(8,128)(2,1)S(1)}) custom-call(bf16[32,192,512]{2,1,0:T(8,128)(2,1)S(1)} %get-tuple-element.29.mixed_ref, bf16[4096,512]{1,0:T(8,128)(2,1)S(1)} %get-tuple-element.31.hot_ref, ...), custom_call_target="tpu_custom_call" | custom-call | tf_op jit(solution)/shard_map/mixed/pallas_call | solution.py:317
  11.0 2.7 %collective-permute-start.4 = (bf16[192,128]{1,0:T(8,128)(2,1)S(1)}, bf16[192,128]{1,0:T(8,128)(2,1)S(1)}, u32[]{:S(2)}, u32[]{:S(2)}) collective-permute-start(bf16[192,128]{1,0:T(8,128)(2,1)S(1)} %get-tuple-element.36), channel_id=1, source_target_pairs={{0,2},{1,3},{2,0},{3,1},{4,6},{5,7},{6,4},{7,5},{8,10},{9,11},{10,... | collective-permute-start | bytes 147464 | tf_op jit(solution)/shard_map/ppermute | solution.py:329
  13.7 1.3 %collective-permute-start.5 = (bf16[192,128]{1,0:T(8,128)(2,1)S(1)}, bf16[192,128]{1,0:T(8,128)(2,1)S(1)}, u32[]{:S(2)}, u32[]{:S(2)}) collective-permute-start(bf16[192,128]{1,0:T(8,128)(2,1)S(1)} %get-tuple-element.37), channel_id=1, source_target_pairs={{0,3},{1,2},{2,1},{3,0},{4,7},{5,6},{6,5},{7,4},{8,11},{9,10},{10,... | collective-permute-start | bytes 147464 | tf_op jit(solution)/shard_map/ppermute | solution.py:329
  15.1 0.2 %collective-permute-start.6 = (bf16[192,128]{1,0:T(8,128)(2,1)S(1)}, bf16[192,128]{1,0:T(8,128)(2,1)S(1)}, u32[]{:S(2)}, u32[]{:S(2)}) collective-permute-start(bf16[192,128]{1,0:T(8,128)(2,1)S(1)} %get-tuple-element.38), channel_id=1, source_target_pairs={{0,1},{1,0},{2,3},{3,2},{4,5},{5,4},{6,7},{7,6},{8,9},{9,8},{10,11... | collective-permute-start | bytes 147464 | tf_op jit(solution)/shard_map/ppermute | solution.py:329
  15.3 2.5 %same_spin.1 = (f32[64,128]{1,0:T(8,128)S(1)}, bf16[128,128]{1,0:T(8,128)(2,1)S(1)}, bf16[128,128]{1,0:T(8,128)(2,1)S(1)}) custom-call(s32[512,128]{1,0:T(8,128)S(1)} %get-tuple-element.24.live_ref, s32[32,512]{1,0:T(8,128)S(1)} %get-tuple-element.25.code_ref, bf16[32,192,512]{2,1,0:T(8,128)(2,1)S(1)} %get-tuple-element.29.mixed_ref, ...), custom_call_target="tpu_custom_call" | custom-call | flops 2147483648 | tf_op jit(solution)/shard_map/same_spin/pallas_call | solution.py:317
  17.8 0.1 collective-permute-start.7
  17.9 0.5 %collective-permute-start.8 = (bf16[128,128]{1,0:T(8,128)(2,1)S(1)}, bf16[128,128]{1,0:T(8,128)(2,1)S(1)}, u32[]{:S(2)}, u32[]{:S(2)}) collective-permute-start(bf16[128,128]{1,0:T(8,128)(2,1)S(1)} %get-tuple-element.40.refs_4_), channel_id=1, source_target_pairs={{0,4},{4,0},{8,12},{12,8},{16,20},{20,16},{24,28},{28,24},{1,5},{5... | collective-permute-start | bytes 98312 | tf_op jit(solution)/shard_map/ppermute | solution.py:326
  18.4 0.7 %collective-permute-done.7.refs_5_ = bf16[128,128]{1,0:T(8,128)(2,1)S(1)} collective-permute-done((bf16[128,128]{1,0:T(8,128)(2,1)S(1)}, bf16[128,128]{1,0:T(8,128)(2,1)S(1)}, u32[]{:S(2)}, u32[]{:S(2)}) %collective-permute-start.7) | collective-permute-done | bytes 32800 | tf_op jit(solution)/shard_map/ppermute | solution.py:326
  19.1 0.2 collective-permute-done.8.refs_6_
  19.3 0.0 collective-permute-done.4.refs_0_
  19.3 0.4 %collective-permute-done.5.refs_1_ = bf16[192,128]{1,0:T(8,128)(2,1)S(1)} collective-permute-done((bf16[192,128]{1,0:T(8,128)(2,1)S(1)}, bf16[192,128]{1,0:T(8,128)(2,1)S(1)}, u32[]{:S(2)}, u32[]{:S(2)}) %collective-permute-start.5) | collective-permute-done | bytes 49184 | tf_op jit(solution)/shard_map/ppermute | solution.py:329
  19.7 0.0 collective-permute-done.6.refs_2_
  19.7 0.8 %final.1 = bf16[64,128]{1,0:T(8,128)(2,1)} custom-call(f32[64,128]{1,0:T(8,128)S(1)} %get-tuple-element.23.alive_ref, f32[64,128]{1,0:T(8,128)S(1)} %get-tuple-element.34.own_ref, bf16[512,128]{1,0:T(8,128)(2,1)S(1)} %get-tuple-element.35.amplitudes_ref, bf16[128,128]{1,0:T(8,128)(2,1)S(1)} %join.1.after_ref.refs_0_.message_ref, ...), custom_call_target="tpu_custom_call" | custom-call | tf_op jit(solution)/shard_map/final/pallas_call | solution.py:317
  (1 shorter events, 0.0 us)
Async XLA Ops:
  0.0 1.8 %collective-permute-start = (bf16[64,128]{1,0:T(8,128)(2,1)}, bf16[64,128]{1,0:T(8,128)(2,1)S(1)}, u32[]{:S(2)}, u32[]{:S(2)}) collective-permute-start(bf16[64,128]{1,0:T(8,128)(2,1)} %amplitudes_hbm.1), channel_id=1, source_target_pairs={{0,4},{4,0},{8,12},{12,8},{16,20},{20,16},{24,28},{28,24},{1,5},{5... | collective-permute-start | bytes 49160 | tf_op jit(solution)/shard_map/ppermute | solution.py:326
  1.8 7.6 %collective-permute-start.3 = (bf16[128,128]{1,0:T(8,128)(2,1)S(1)}, bf16[128,128]{1,0:T(8,128)(2,1)S(1)}, u32[]{:S(2)}, u32[]{:S(2)}) collective-permute-start(bf16[128,128]{1,0:T(8,128)(2,1)S(1)} %join.1.after_ref.refs_0_.message_ref), channel_id=1, source_target_pairs={{0,24},{4,28},{8,16},{12,20},{16,8},{20,12},{24,0},{28,4},{1,25},{... | collective-permute-start | bytes 98312 | tf_op jit(solution)/shard_map/ppermute | solution.py:326
  5.3 4.1 %collective-permute-start.2 = (bf16[128,128]{1,0:T(8,128)(2,1)S(1)}, bf16[128,128]{1,0:T(8,128)(2,1)S(1)}, u32[]{:S(2)}, u32[]{:S(2)}) collective-permute-start(bf16[128,128]{1,0:T(8,128)(2,1)S(1)} %join.1.after_ref.refs_0_.message_ref), channel_id=1, source_target_pairs={{0,16},{4,20},{8,24},{12,28},{16,0},{20,4},{24,8},{28,12},{1,17},{... | collective-permute-start | bytes 98312 | tf_op jit(solution)/shard_map/ppermute | solution.py:326
  5.8 3.9 %collective-permute-start.1 = (bf16[128,128]{1,0:T(8,128)(2,1)S(1)}, bf16[128,128]{1,0:T(8,128)(2,1)S(1)}, u32[]{:S(2)}, u32[]{:S(2)}) collective-permute-start(bf16[128,128]{1,0:T(8,128)(2,1)S(1)} %join.1.after_ref.refs_0_.message_ref), channel_id=1, source_target_pairs={{0,8},{4,12},{8,0},{12,4},{16,24},{20,28},{24,16},{28,20},{1,9},{5... | collective-permute-start | bytes 98312 | tf_op jit(solution)/shard_map/ppermute | solution.py:326
  11.0 8.3 %collective-permute-start.4 = (bf16[192,128]{1,0:T(8,128)(2,1)S(1)}, bf16[192,128]{1,0:T(8,128)(2,1)S(1)}, u32[]{:S(2)}, u32[]{:S(2)}) collective-permute-start(bf16[192,128]{1,0:T(8,128)(2,1)S(1)} %get-tuple-element.36), channel_id=1, source_target_pairs={{0,2},{1,3},{2,0},{3,1},{4,6},{5,7},{6,4},{7,5},{8,10},{9,11},{10,... | collective-permute-start | bytes 147464 | tf_op jit(solution)/shard_map/ppermute | solution.py:329
  13.7 6.0 %collective-permute-start.5 = (bf16[192,128]{1,0:T(8,128)(2,1)S(1)}, bf16[192,128]{1,0:T(8,128)(2,1)S(1)}, u32[]{:S(2)}, u32[]{:S(2)}) collective-permute-start(bf16[192,128]{1,0:T(8,128)(2,1)S(1)} %get-tuple-element.37), channel_id=1, source_target_pairs={{0,3},{1,2},{2,1},{3,0},{4,7},{5,6},{6,5},{7,4},{8,11},{9,10},{10,... | collective-permute-start | bytes 147464 | tf_op jit(solution)/shard_map/ppermute | solution.py:329
  15.1 4.6 %collective-permute-start.6 = (bf16[192,128]{1,0:T(8,128)(2,1)S(1)}, bf16[192,128]{1,0:T(8,128)(2,1)S(1)}, u32[]{:S(2)}, u32[]{:S(2)}) collective-permute-start(bf16[192,128]{1,0:T(8,128)(2,1)S(1)} %get-tuple-element.38), channel_id=1, source_target_pairs={{0,1},{1,0},{2,3},{3,2},{4,5},{5,4},{6,7},{7,6},{8,9},{9,8},{10,11... | collective-permute-start | bytes 147464 | tf_op jit(solution)/shard_map/ppermute | solution.py:329
  17.8 1.3 %collective-permute-start.7 = (bf16[128,128]{1,0:T(8,128)(2,1)S(1)}, bf16[128,128]{1,0:T(8,128)(2,1)S(1)}, u32[]{:S(2)}, u32[]{:S(2)}) collective-permute-start(bf16[128,128]{1,0:T(8,128)(2,1)S(1)} %get-tuple-element.39.refs_3_), channel_id=1, source_target_pairs={{0,4},{4,0},{8,12},{12,8},{16,20},{20,16},{24,28},{28,24},{1,5},{5... | collective-permute-start | bytes 98312 | tf_op jit(solution)/shard_map/ppermute | solution.py:326
  17.9 1.4 %collective-permute-start.8 = (bf16[128,128]{1,0:T(8,128)(2,1)S(1)}, bf16[128,128]{1,0:T(8,128)(2,1)S(1)}, u32[]{:S(2)}, u32[]{:S(2)}) collective-permute-start(bf16[128,128]{1,0:T(8,128)(2,1)S(1)} %get-tuple-element.40.refs_4_), channel_id=1, source_target_pairs={{0,4},{4,0},{8,12},{12,8},{16,20},{20,16},{24,28},{28,24},{1,5},{5... | collective-permute-start | bytes 98312 | tf_op jit(solution)/shard_map/ppermute | solution.py:326

commit v7 on v6

--- a/solution.py
+++ b/solution.py
@@ -40,6 +40,10 @@
 
 def sign_of(code):
     return jnp.where(code > 0, 1.0, -1.0).astype(F32)
+
+
+def by_chip(groups):
+    return (0, 2, 1, *range(3, groups)) if groups > 2 else tuple(range(groups))
 
 
 def by_start(peers):
@@ -175,7 +179,7 @@
 
 
 def mixed_kernel(steps, groups, peers, place, mixed_ref, hot_ref, block_ref, *refs):
-    arrived = refs[:groups]
+    arrived = [refs[by_chip(groups).index(k)] for k in range(groups)]
     own_ref, amplitudes_ref = refs[groups : groups + 2]
     sent = [refs[groups + 2 + by_start(peers).index(k)] for k in range(1, peers)]
     line, total_ref = refs[groups + 1 + peers :]
@@ -415,7 +419,7 @@
         near(mixed),
         near(hot),
         near(block),
-        *[near(m) for m in messages],
+        *[near(messages[k]) for k in by_chip(groups)],
         in_specs=[tiled((part, both, strings), 0), tiled((part * columns, strings), 0)] + [vmem] * (groups + 1),
         out_shape=(
             shape_of((rows, pairs * columns), BF16) if resident else shape_of((rows, columns), F32),

time: 20.6 us -> 20.6 us (level)
  no operation moved by 1% of the time
where the time goes in v7:
time: 20.6 us; the launch traced here: 20.5 us
  starting transfers between devices  9.46 us (46%)
  Pallas kernels  9.28 us (45%)
  waiting for transfers between devices  1.66 us (8%)
    pallas_call x7, Pallas kernels, call(): pl.pallas_call(body, name=name, compiler_params=params, cost_estimate=cos...  9.28 us
    ppermute x6, starting transfers between devices, over_alpha(): return lax.ppermute(value, 'aa', [(i, i ^ mask) for i in range(sizes[0])])  5.17 us
    ppermute x3, starting transfers between devices, over_beta(): return lax.ppermute(value, 'ba', [(i, i ^ mask) for i in range(peers)])  4.29 us
    ppermute x6, waiting for transfers between devices, over_alpha(): return lax.ppermute(value, 'aa', [(i, i ^ mask) for i in range(sizes[0])])  1.23 us
    ppermute x3, waiting for transfers between devices, over_beta(): return lax.ppermute(value, 'ba', [(i, i ^ mask) for i in range(peers)])  0.43 us
  transfers between devices with their start and end apart: 9, of which 4 were waited for; matrix products, arithmetic and copies ran while one was open for 0% of the time, Pallas kernels for 35%

profile of v7, /device:TPU:0, one launch (start us, length us, event | category | flops | bytes accessed | tf_op | source)
XLA Modules:
  0.0 20.5 jit_solution(17630611249918704739)
XLA Ops:
  0.0 0.5 %collective-permute-start = (bf16[64,128]{1,0:T(8,128)(2,1)}, bf16[64,128]{1,0:T(8,128)(2,1)S(1)}, u32[]{:S(2)}, u32[]{:S(2)}) collective-permute-start(bf16[64,128]{1,0:T(8,128)(2,1)} %amplitudes_hbm.1), channel_id=1, source_target_pairs={{0,4},{4,0},{8,12},{12,8},{16,20},{20,16},{24,28},{28,24},{1,5},{5... | collective-permute-start | bytes 49160 | tf_op jit(solution)/shard_map/ppermute | solution.py:330
  0.5 1.3 %tables.1 = (s32[32,512]{1,0:T(8,128)S(1)}, s32[512,128]{1,0:T(8,128)S(1)}, s32[8,512]{1,0:T(8,128)S(1)}, bf16[264,256]{1,0:T(8,128)(2,1)S(1)}, f32[64,128]{1,0:T(8,128)S(1)}, /*index=5*/bf16[64,128]{1,0:T(8,128)(2,1)S(1)}) custom-call(s32[32]{0:T(128)} %counts_hbm.1, s32[32]{0:T(128)} %irrep_hbm.1, s32[32,512]{1,0:T(8,128)} %code_hbm.1, ...), custom_call_target="tpu_custom_call" | custom-call | tf_op jit(solution)/shard_map/tables/pallas_call | solution.py:321
  1.8 0.0 collective-permute-done.sibling_ref
  1.8 3.5 %collective-permute-start.3 = (bf16[128,128]{1,0:T(8,128)(2,1)S(1)}, bf16[128,128]{1,0:T(8,128)(2,1)S(1)}, u32[]{:S(2)}, u32[]{:S(2)}) collective-permute-start(bf16[128,128]{1,0:T(8,128)(2,1)S(1)} %join.1.after_ref.refs_0_.message_ref), channel_id=1, source_target_pairs={{0,24},{4,28},{8,16},{12,20},{16,8},{20,12},{24,0},{28,4},{1,25},{... | collective-permute-start | bytes 98312 | tf_op jit(solution)/shard_map/ppermute | solution.py:330
  5.3 0.5 %collective-permute-start.2 = (bf16[128,128]{1,0:T(8,128)(2,1)S(1)}, bf16[128,128]{1,0:T(8,128)(2,1)S(1)}, u32[]{:S(2)}, u32[]{:S(2)}) collective-permute-start(bf16[128,128]{1,0:T(8,128)(2,1)S(1)} %join.1.after_ref.refs_0_.message_ref), channel_id=1, source_target_pairs={{0,8},{4,12},{8,0},{12,4},{16,24},{20,28},{24,16},{28,20},{1,9},{5... | collective-permute-start | bytes 98312 | tf_op jit(solution)/shard_map/ppermute | solution.py:330
  5.8 0.1 collective-permute-start.1
  5.9 2.1 %mix.1 = (bf16[32,192,512]{2,1,0:T(8,128)(2,1)S(1)}, f32[192,512]{1,0:T(8,128)S(1)}) custom-call(s32[32,512]{1,0:T(8,128)S(1)} %get-tuple-element.25.code_ref, s32[8,512]{1,0:T(8,128)S(1)} %get-tuple-element.26.lane_ref, bf16[264,256]{1,0:T(8,128)(2,1)S(1)} %get-tuple-element.27.mixer_ref, bf16[128,128]{1,0:T(8,128)(2,1)S(1)} %join.1.after_ref.refs_0_.message_ref), custom_call_target="tpu_custom_call" | custom-call | flops 1610612736 | tf_op jit(solution)/shard_map/mix/pallas_call | solution.py:321
  8.1 1.3 %hot.1 = (bf16[4096,512]{1,0:T(8,128)(2,1)S(1)}, bf16[64,128]{1,0:T(8,128)(2,1)S(1)}) custom-call(s32[512,128]{1,0:T(8,128)S(1)} %get-tuple-element.24.live_ref, s32[32,512]{1,0:T(8,128)S(1)} %get-tuple-element.25.code_ref, bf16[32,192,512]{2,1,0:T(8,128)(2,1)S(1)} %get-tuple-element.29.mixed_ref, f32[192,512]{1,0:T(8,128)S(1)} %get-tuple-element.30.one_ref), custom_call_target="tpu_custom_call" | custom-call | flops 268435456 | tf_op jit(solution)/shard_map/hot/pallas_call | solution.py:321
  9.4 0.0 collective-permute-done.3.refs_3_
  9.4 0.0 collective-permute-done.2.refs_2_
  9.4 0.4 %collective-permute-done.1.refs_1_ = bf16[128,128]{1,0:T(8,128)(2,1)S(1)} collective-permute-done((bf16[128,128]{1,0:T(8,128)(2,1)S(1)}, bf16[128,128]{1,0:T(8,128)(2,1)S(1)}, u32[]{:S(2)}, u32[]{:S(2)}) %collective-permute-start.1) | collective-permute-done | bytes 32800 | tf_op jit(solution)/shard_map/ppermute | solution.py:330
  9.7 1.3 %mixed.1 = (bf16[64,4096]{1,0:T(8,128)(2,1)S(1)}, bf16[512,128]{1,0:T(8,128)(2,1)S(1)}, bf16[192,128]{1,0:T(8,128)(2,1)S(1)}, bf16[192,128]{1,0:T(8,128)(2,1)S(1)}, bf16[192,128]{1,0:T(8,128)(2,1)S(1)}) custom-call(bf16[32,192,512]{2,1,0:T(8,128)(2,1)S(1)} %get-tuple-element.29.mixed_ref, bf16[4096,512]{1,0:T(8,128)(2,1)S(1)} %get-tuple-element.31.hot_ref, ...), custom_call_target="tpu_custom_call" | custom-call | tf_op jit(solution)/shard_map/mixed/pallas_call | solution.py:321
  11.0 2.7 %collective-permute-start.4 = (bf16[192,128]{1,0:T(8,128)(2,1)S(1)}, bf16[192,128]{1,0:T(8,128)(2,1)S(1)}, u32[]{:S(2)}, u32[]{:S(2)}) collective-permute-start(bf16[192,128]{1,0:T(8,128)(2,1)S(1)} %get-tuple-element.36), channel_id=1, source_target_pairs={{0,2},{1,3},{2,0},{3,1},{4,6},{5,7},{6,4},{7,5},{8,10},{9,11},{10,... | collective-permute-start | bytes 147464 | tf_op jit(solution)/shard_map/ppermute | solution.py:333
  13.7 1.3 %collective-permute-start.5 = (bf16[192,128]{1,0:T(8,128)(2,1)S(1)}, bf16[192,128]{1,0:T(8,128)(2,1)S(1)}, u32[]{:S(2)}, u32[]{:S(2)}) collective-permute-start(bf16[192,128]{1,0:T(8,128)(2,1)S(1)} %get-tuple-element.37), channel_id=1, source_target_pairs={{0,3},{1,2},{2,1},{3,0},{4,7},{5,6},{6,5},{7,4},{8,11},{9,10},{10,... | collective-permute-start | bytes 147464 | tf_op jit(solution)/shard_map/ppermute | solution.py:333
  15.1 0.2 %collective-permute-start.6 = (bf16[192,128]{1,0:T(8,128)(2,1)S(1)}, bf16[192,128]{1,0:T(8,128)(2,1)S(1)}, u32[]{:S(2)}, u32[]{:S(2)}) collective-permute-start(bf16[192,128]{1,0:T(8,128)(2,1)S(1)} %get-tuple-element.38), channel_id=1, source_target_pairs={{0,1},{1,0},{2,3},{3,2},{4,5},{5,4},{6,7},{7,6},{8,9},{9,8},{10,11... | collective-permute-start | bytes 147464 | tf_op jit(solution)/shard_map/ppermute | solution.py:333
  15.3 2.5 %same_spin.1 = (f32[64,128]{1,0:T(8,128)S(1)}, bf16[128,128]{1,0:T(8,128)(2,1)S(1)}, bf16[128,128]{1,0:T(8,128)(2,1)S(1)}) custom-call(s32[512,128]{1,0:T(8,128)S(1)} %get-tuple-element.24.live_ref, s32[32,512]{1,0:T(8,128)S(1)} %get-tuple-element.25.code_ref, bf16[32,192,512]{2,1,0:T(8,128)(2,1)S(1)} %get-tuple-element.29.mixed_ref, ...), custom_call_target="tpu_custom_call" | custom-call | flops 2147483648 | tf_op jit(solution)/shard_map/same_spin/pallas_call | solution.py:321
  17.8 0.1 collective-permute-start.7
  17.9 0.5 %collective-permute-start.8 = (bf16[128,128]{1,0:T(8,128)(2,1)S(1)}, bf16[128,128]{1,0:T(8,128)(2,1)S(1)}, u32[]{:S(2)}, u32[]{:S(2)}) collective-permute-start(bf16[128,128]{1,0:T(8,128)(2,1)S(1)} %get-tuple-element.40.refs_4_), channel_id=1, source_target_pairs={{0,4},{4,0},{8,12},{12,8},{16,20},{20,16},{24,28},{28,24},{1,5},{5... | collective-permute-start | bytes 98312 | tf_op jit(solution)/shard_map/ppermute | solution.py:330
  18.4 0.7 %collective-permute-done.7.refs_5_ = bf16[128,128]{1,0:T(8,128)(2,1)S(1)} collective-permute-done((bf16[128,128]{1,0:T(8,128)(2,1)S(1)}, bf16[128,128]{1,0:T(8,128)(2,1)S(1)}, u32[]{:S(2)}, u32[]{:S(2)}) %collective-permute-start.7) | collective-permute-done | bytes 32800 | tf_op jit(solution)/shard_map/ppermute | solution.py:330
  19.1 0.2 collective-permute-done.8.refs_6_
  19.3 0.0 collective-permute-done.4.refs_0_
  19.3 0.4 %collective-permute-done.5.refs_1_ = bf16[192,128]{1,0:T(8,128)(2,1)S(1)} collective-permute-done((bf16[192,128]{1,0:T(8,128)(2,1)S(1)}, bf16[192,128]{1,0:T(8,128)(2,1)S(1)}, u32[]{:S(2)}, u32[]{:S(2)}) %collective-permute-start.5) | collective-permute-done | bytes 49184 | tf_op jit(solution)/shard_map/ppermute | solution.py:333
  19.7 0.0 collective-permute-done.6.refs_2_
  19.7 0.8 %final.1 = bf16[64,128]{1,0:T(8,128)(2,1)} custom-call(f32[64,128]{1,0:T(8,128)S(1)} %get-tuple-element.23.alive_ref, f32[64,128]{1,0:T(8,128)S(1)} %get-tuple-element.34.own_ref, bf16[512,128]{1,0:T(8,128)(2,1)S(1)} %get-tuple-element.35.amplitudes_ref, bf16[128,128]{1,0:T(8,128)(2,1)S(1)} %join.1.after_ref.refs_0_.message_ref, ...), custom_call_target="tpu_custom_call" | custom-call | tf_op jit(solution)/shard_map/final/pallas_call | solution.py:321
  (1 shorter events, 0.0 us)
Async XLA Ops:
  0.0 1.8 %collective-permute-start = (bf16[64,128]{1,0:T(8,128)(2,1)}, bf16[64,128]{1,0:T(8,128)(2,1)S(1)}, u32[]{:S(2)}, u32[]{:S(2)}) collective-permute-start(bf16[64,128]{1,0:T(8,128)(2,1)} %amplitudes_hbm.1), channel_id=1, source_target_pairs={{0,4},{4,0},{8,12},{12,8},{16,20},{20,16},{24,28},{28,24},{1,5},{5... | collective-permute-start | bytes 49160 | tf_op jit(solution)/shard_map/ppermute | solution.py:330
  1.8 7.6 %collective-permute-start.3 = (bf16[128,128]{1,0:T(8,128)(2,1)S(1)}, bf16[128,128]{1,0:T(8,128)(2,1)S(1)}, u32[]{:S(2)}, u32[]{:S(2)}) collective-permute-start(bf16[128,128]{1,0:T(8,128)(2,1)S(1)} %join.1.after_ref.refs_0_.message_ref), channel_id=1, source_target_pairs={{0,24},{4,28},{8,16},{12,20},{16,8},{20,12},{24,0},{28,4},{1,25},{... | collective-permute-start | bytes 98312 | tf_op jit(solution)/shard_map/ppermute | solution.py:330
  5.3 4.1 %collective-permute-start.2 = (bf16[128,128]{1,0:T(8,128)(2,1)S(1)}, bf16[128,128]{1,0:T(8,128)(2,1)S(1)}, u32[]{:S(2)}, u32[]{:S(2)}) collective-permute-start(bf16[128,128]{1,0:T(8,128)(2,1)S(1)} %join.1.after_ref.refs_0_.message_ref), channel_id=1, source_target_pairs={{0,8},{4,12},{8,0},{12,4},{16,24},{20,28},{24,16},{28,20},{1,9},{5... | collective-permute-start | bytes 98312 | tf_op jit(solution)/shard_map/ppermute | solution.py:330
  5.8 3.9 %collective-permute-start.1 = (bf16[128,128]{1,0:T(8,128)(2,1)S(1)}, bf16[128,128]{1,0:T(8,128)(2,1)S(1)}, u32[]{:S(2)}, u32[]{:S(2)}) collective-permute-start(bf16[128,128]{1,0:T(8,128)(2,1)S(1)} %join.1.after_ref.refs_0_.message_ref), channel_id=1, source_target_pairs={{0,16},{4,20},{8,24},{12,28},{16,0},{20,4},{24,8},{28,12},{1,17},{... | collective-permute-start | bytes 98312 | tf_op jit(solution)/shard_map/ppermute | solution.py:330
  11.0 8.2 %collective-permute-start.4 = (bf16[192,128]{1,0:T(8,128)(2,1)S(1)}, bf16[192,128]{1,0:T(8,128)(2,1)S(1)}, u32[]{:S(2)}, u32[]{:S(2)}) collective-permute-start(bf16[192,128]{1,0:T(8,128)(2,1)S(1)} %get-tuple-element.36), channel_id=1, source_target_pairs={{0,2},{1,3},{2,0},{3,1},{4,6},{5,7},{6,4},{7,5},{8,10},{9,11},{10,... | collective-permute-start | bytes 147464 | tf_op jit(solution)/shard_map/ppermute | solution.py:333
  13.7 6.0 %collective-permute-start.5 = (bf16[192,128]{1,0:T(8,128)(2,1)S(1)}, bf16[192,128]{1,0:T(8,128)(2,1)S(1)}, u32[]{:S(2)}, u32[]{:S(2)}) collective-permute-start(bf16[192,128]{1,0:T(8,128)(2,1)S(1)} %get-tuple-element.37), channel_id=1, source_target_pairs={{0,3},{1,2},{2,1},{3,0},{4,7},{5,6},{6,5},{7,4},{8,11},{9,10},{10,... | collective-permute-start | bytes 147464 | tf_op jit(solution)/shard_map/ppermute | solution.py:333
  15.1 4.6 %collective-permute-start.6 = (bf16[192,128]{1,0:T(8,128)(2,1)S(1)}, bf16[192,128]{1,0:T(8,128)(2,1)S(1)}, u32[]{:S(2)}, u32[]{:S(2)}) collective-permute-start(bf16[192,128]{1,0:T(8,128)(2,1)S(1)} %get-tuple-element.38), channel_id=1, source_target_pairs={{0,1},{1,0},{2,3},{3,2},{4,5},{5,4},{6,7},{7,6},{8,9},{9,8},{10,11... | collective-permute-start | bytes 147464 | tf_op jit(solution)/shard_map/ppermute | solution.py:333
  17.8 1.3 %collective-permute-start.7 = (bf16[128,128]{1,0:T(8,128)(2,1)S(1)}, bf16[128,128]{1,0:T(8,128)(2,1)S(1)}, u32[]{:S(2)}, u32[]{:S(2)}) collective-permute-start(bf16[128,128]{1,0:T(8,128)(2,1)S(1)} %get-tuple-element.39.refs_3_), channel_id=1, source_target_pairs={{0,4},{4,0},{8,12},{12,8},{16,20},{20,16},{24,28},{28,24},{1,5},{5... | collective-permute-start | bytes 98312 | tf_op jit(solution)/shard_map/ppermute | solution.py:330
  17.9 1.4 %collective-permute-start.8 = (bf16[128,128]{1,0:T(8,128)(2,1)S(1)}, bf16[128,128]{1,0:T(8,128)(2,1)S(1)}, u32[]{:S(2)}, u32[]{:S(2)}) collective-permute-start(bf16[128,128]{1,0:T(8,128)(2,1)S(1)} %get-tuple-element.40.refs_4_), channel_id=1, source_target_pairs={{0,4},{4,0},{8,12},{12,8},{16,20},{20,16},{24,28},{28,24},{1,5},{5... | collective-permute-start | bytes 98312 | tf_op jit(solution)/shard_map/ppermute | solution.py:330
